TPU v7x, 256 devices: a whole 4x4x8 slice. The times are simulated.
256 devices in a mesh: bin: 16 (over y_lo, z), sky: 16 (over x, y_hi, core).
Axes of the slice: x: 4, y: 4 (y_hi: 2, y_lo: 2; y = y_hi * 2 + y_lo), z: 8, core: 2. Of those that a mesh axis runs over, the one named last changes fastest.
Arguments:
- lensing_maps: bfloat16 [16, 128, 8192], P('bin', 'sky')
- filter_taps: float32 [5, 17], replicated, may hold values from -1.5 to 1.5
- survey_mask: int32 [16, 64], P('sky'), may hold values 0 or 1
- bin_pairs: int32 [136, 2], replicated, may hold values from 0 to 15, as said below
- target_corr: float32 [136, 5, 4], replicated, may hold values from -3 to 3
- pair_weight: float32 [136, 5, 4], replicated, may hold values from 0.3 to 3
Outputs:
- corr_table: float32 [136, 5, 4], replicated
- map_gradient: float32 [16, 128, 8192], P('bin', 'sky')
Inputs may be any that keep to these rules, and one draw needn't show every extreme that they name: `bin_pairs`: every unordered pair of the 16 bins, a bin with itself included, is listed exactly once; the order of the list and of the two bins in a row vary.
All inputs are finite; a program needn't handle non-finite values. No bound on the sum of `survey_mask` on one device may be relied on, other than what follows from the above.
Results may differ from a plain program's by a relative error of at most 0.0015.
Values may be sent and summed in bfloat16 or wider, within the bound.
No kernel may reach another device: no remote copies, remote signals or barrier semaphores. Data moves between devices by JAX's collectives and lax.ppermute only.
A program may use at most 64 MiB of HBM per device.

v0:
```python
import jax
import jax.numpy as jnp
from jax import lax
from jax.sharding import PartitionSpec as P

HIGH = lax.Precision.HIGHEST


def with_halo(block, sides, width):
    for axis, dim in sides:
        count = lax.axis_size(axis)
        forward = [(i, i + 1) for i in range(count - 1)]
        backward = [(target, source) for source, target in forward]
        low = lax.ppermute(
            lax.slice_in_dim(block, block.shape[dim] - width, None, axis=dim), axis, forward
        )
        high = lax.ppermute(lax.slice_in_dim(block, 0, width, axis=dim), axis, backward)
        block = jnp.concatenate([low, block, high], axis=dim)
    return block


def shifted(value, axis, steps):
    count = lax.axis_size(axis)
    pairs = [(source, (source + steps) % count) for source in range(count)]
    return lax.ppermute(value, axis, pairs)


def expand_mask(survey_mask):
    values = survey_mask.astype(jnp.float32)
    tiles_x, tiles_y = values.shape
    return jnp.broadcast_to(values[:, None, :, None], (tiles_x, 8, tiles_y, 128)).reshape(
        tiles_x * 8, tiles_y * 128
    )


def smooth(haloed, filter_taps, row_count):
    tap_count = filter_taps.shape[1]
    half_width = (tap_count - 1) // 2
    widened = haloed.astype(jnp.float32)
    across = filter_taps[:, 0, None, None] * widened[None, 0:row_count]
    for a in range(1, tap_count):
        across = across + filter_taps[:, a, None, None] * widened[None, a : a + row_count]
    padded = jnp.pad(across, ((0, 0), (0, 0), (half_width, half_width)))
    col_count = widened.shape[1]
    result = filter_taps[:, 0, None, None] * padded[:, :, 0:col_count]
    for c in range(1, tap_count):
        result = result + filter_taps[:, c, None, None] * padded[:, :, c : c + col_count]
    return result.astype(jnp.bfloat16)


def lagged(left_maps, right_maps, pixmask, lag_count):
    col_count = left_maps.shape[2]
    columns = []
    for offset in range(lag_count):
        joint_mask = pixmask[:, : col_count - offset] * pixmask[:, offset:]
        product = (
            left_maps[:, :, : col_count - offset].astype(jnp.float32)
            * right_maps[:, :, offset:].astype(jnp.float32)
            * joint_mask[None]
        )
        columns.append(jnp.sum(product, axis=(1, 2)))
    return jnp.stack(columns, axis=1)


def adjoint_lags(partner, ahead_w, behind_w, pixmask):
    col_count = partner.shape[2]
    widened = partner.astype(jnp.float32)
    totals = jnp.zeros(partner.shape, jnp.float32)
    for offset in range(ahead_w.shape[1]):
        joint_mask = pixmask[:, : col_count - offset] * pixmask[:, offset:]
        front = jnp.pad(joint_mask[None] * widened[:, :, offset:], ((0, 0), (0, 0), (0, offset)))
        back = jnp.pad(
            joint_mask[None] * widened[:, :, : col_count - offset], ((0, 0), (0, 0), (offset, 0))
        )
        totals = (
            totals + ahead_w[:, offset, None, None] * front + behind_w[:, offset, None, None] * back
        )
    return totals


def adjoint_cols(grads, filter_taps):
    tap_count = filter_taps.shape[1]
    half_width = (tap_count - 1) // 2
    col_count = grads.shape[2]
    padded = jnp.pad(grads, ((0, 0), (0, 0), (half_width, half_width)))
    result = filter_taps[:, tap_count - 1, None, None] * padded[:, :, 0:col_count]
    for c in range(1, tap_count):
        result = (
            result + filter_taps[:, tap_count - 1 - c, None, None] * padded[:, :, c : c + col_count]
        )
    return result


def adjoint_rows(widened, filter_taps, row_count):
    tap_count = filter_taps.shape[1]
    result = filter_taps[:, tap_count - 1, None, None] * widened[:, 0:row_count]
    for a in range(1, tap_count):
        result = (
            result + filter_taps[:, tap_count - 1 - a, None, None] * widened[:, a : a + row_count]
        )
    return jnp.sum(result, axis=0)


def put_block(row_hot, col_hot, values):
    return row_hot[:, None, None, None] * col_hot[None, :, None, None] * values[None, None]


def take_block(table, row_hot, col_hot):
    return jnp.einsum("i,j,ijsl->sl", row_hot, col_hot, table, precision=HIGH)


def per_device(lensing_maps, filter_taps, survey_mask, bin_pairs, target_corr, pair_weight):
    tap_count = filter_taps.shape[1]
    half_width = (tap_count - 1) // 2
    my_strip = lensing_maps[0]
    row_count, col_count = my_strip.shape
    bin_count = lax.axis_size("bin")
    sky_count = lax.axis_size("sky")
    my_bin = lax.axis_index("bin")
    lag_count = pair_weight.shape[2]
    inverse_area = 1.0 / (row_count * sky_count * col_count)
    pixmask = expand_mask(survey_mask)
    haloed = with_halo(my_strip, (("sky", 0),), half_width)
    own_maps = smooth(haloed, filter_taps, row_count)

    def forward_move(carried):
        moved = shifted(carried, "bin", 1)
        return moved

    indices = jnp.arange(bin_count, dtype=jnp.int32)
    mine_hot = (indices == my_bin).astype(jnp.float32)

    def bin_hot(k):
        return (indices == (my_bin - k) % bin_count).astype(jnp.float32)

    visit_count = bin_count - 1
    stored_init = jnp.zeros((visit_count,) + own_maps.shape, own_maps.dtype)

    def keep_visitor(stored, carried, k):
        stored = lax.dynamic_update_index_in_dim(stored, carried, k - 1, 0)
        return stored

    initial = put_block(
        mine_hot, mine_hot, lagged(own_maps, own_maps, pixmask, lag_count) * inverse_area
    )

    def advance(k, state_all):
        carried, tables, stored = state_all
        carried = forward_move(carried)
        stored = keep_visitor(stored, carried, k)
        tables = tables + put_block(
            mine_hot, bin_hot(k), lagged(own_maps, carried, pixmask, lag_count) * inverse_area
        )
        return (carried, tables, stored)

    _, tables, stored = lax.fori_loop(1, bin_count, advance, (own_maps, initial, stored_init))
    pair_table = lax.psum(tables, ("bin", "sky"))
    left_hot = (bin_pairs[:, 0:1] == indices[None, :]).astype(jnp.float32)
    right_hot = (bin_pairs[:, 1:2] == indices[None, :]).astype(jnp.float32)
    corr_table = jnp.einsum("pi,pj,ijsl->psl", left_hot, right_hot, pair_table, precision=HIGH)
    pair_grad = pair_weight * (corr_table - target_corr)
    table_grad = jnp.einsum("pi,pj,psl->ijsl", left_hot, right_hot, pair_grad, precision=HIGH)
    own_block = take_block(table_grad, mine_hot, mine_hot)
    start_grad = adjoint_lags(own_maps, own_block, own_block, pixmask)

    def partner_term(visitor, k):
        other_hot = bin_hot(k)
        return adjoint_lags(
            visitor,
            take_block(table_grad, mine_hot, other_hot),
            take_block(table_grad, other_hot, mine_hot),
            pixmask,
        )

    def reread(k, totals):
        visitor = lax.dynamic_index_in_dim(stored, k - 1, 0, keepdims=False)
        return totals + partner_term(visitor, k)

    totals = lax.fori_loop(1, visit_count + 1, reread, start_grad)
    col_pass = adjoint_cols(totals, filter_taps)
    widened = with_halo(col_pass, (("sky", 1),), half_width)
    map_grad = adjoint_rows(widened, filter_taps, row_count)
    return (corr_table, map_grad[None])


def solution(mesh):
    placed = (P("bin", "sky", None), P(), P("sky", None), P(), P(), P())
    return jax.shard_map(
        per_device,
        mesh=mesh,
        in_specs=placed,
        out_specs=(P(), P("bin", "sky", None)),
        check_vma=False,
    )
```

profile of v0, /device:TPU:16, one launch (start us, length us, event | category | flops | bytes accessed | tf_op | source)
XLA Modules:
  0.0 566.7 jit_solution(2589536851537405955)
XLA Ops:
  0.6 1.9 collective-permute-start.1
  2.6 5.1 collective-permute-start.2
  9.6 1.8 slice_reduce_fusion.16
  12.9 1.8 multiply_add_fusion.4
  14.8 5.9 %fusion.112 = (f32[5,8,8192]{2,1,0:T(8,128)S(1)}, bf16[5,8,8192]{2,1,0:T(8,128)(2,1)S(1)}) fusion(f32[5]{0:T(128)S(1)} %get-tuple-element.778, f32[5]{0:T(128)S(1)} %get-tuple-element.779, f32[5]{0:T(128)S(1)} %get-tuple-element.764, f32[5]{0:T(128)S(1)} %get-tuple-element.765, f32[5]{0:T(128)S(1)} %get-tuple-element.766, f32[5]{0:T(128)S(1)} %get-tuple-element.767, ...), kind=kLoop, calls=%fused_computation.221 | loop fusion | flops 11468800 | bytes 3277140 | tf_op jit(solution)/shard_map/convert_element_type | solution.py:57
  21.6 1.7 slice_multiply_fusion.11
  23.3 2.2 slice_multiply_fusion.9
  25.4 2.1 slice_multiply_fusion.7
  28.0 294.2 %while.42 = (s32[]{:T(128)}, bf16[5,8,8192]{2,1,0:T(8,128)(2,1)}, f32[16,16,5,4]{1,3,2,0:T(4,128)S(1)}, bf16[15,5,8,8192]{3,2,1,0:T(8,128)(2,1)}, s32[]{:T(128)}...) while((s32[]{:T(128)}, bf16[5,8,8192]{2,1,0:T(8,128)(2,1)}, ...), condition=%wide.region_9.10_spmd.clone.clone, body=%wide.region_4.9_spmd.clone.clone.sunk | while | flops 6563034 | bytes 10659906 | solution.py:156
  28.0 2.0 collective-permute-start
  30.1 18.8 %collective-permute-done = bf16[5,8,8192]{2,1,0:T(8,128)(2,1)S(1)} collective-permute-done((bf16[5,8,8192]{2,1,0:T(8,128)(2,1)}, bf16[5,8,8192]{2,1,0:T(8,128)(2,1)S(1)}, u32[]{:S(2)}, u32[]{:S(2)}) %collective-permute-start) | collective-permute-done | bytes 655392 | tf_op jit(solution)/shard_map/while/body/eval_jaxpr/ppermute | solution.py:25
  52.7 19.5 %collective-permute-done = bf16[5,8,8192]{2,1,0:T(8,128)(2,1)S(1)} collective-permute-done((bf16[5,8,8192]{2,1,0:T(8,128)(2,1)}, bf16[5,8,8192]{2,1,0:T(8,128)(2,1)S(1)}, u32[]{:S(2)}, u32[]{:S(2)}) %collective-permute-start) | collective-permute-done | bytes 655392 | tf_op jit(solution)/shard_map/while/body/eval_jaxpr/ppermute | solution.py:25
  76.0 19.0 %collective-permute-done = bf16[5,8,8192]{2,1,0:T(8,128)(2,1)S(1)} collective-permute-done((bf16[5,8,8192]{2,1,0:T(8,128)(2,1)}, bf16[5,8,8192]{2,1,0:T(8,128)(2,1)S(1)}, u32[]{:S(2)}, u32[]{:S(2)}) %collective-permute-start) | collective-permute-done | bytes 655392 | tf_op jit(solution)/shard_map/while/body/eval_jaxpr/ppermute | solution.py:25
  98.7 18.2 %collective-permute-done = bf16[5,8,8192]{2,1,0:T(8,128)(2,1)S(1)} collective-permute-done((bf16[5,8,8192]{2,1,0:T(8,128)(2,1)}, bf16[5,8,8192]{2,1,0:T(8,128)(2,1)S(1)}, u32[]{:S(2)}, u32[]{:S(2)}) %collective-permute-start) | collective-permute-done | bytes 655392 | tf_op jit(solution)/shard_map/while/body/eval_jaxpr/ppermute | solution.py:25
  120.7 17.3 %collective-permute-done = bf16[5,8,8192]{2,1,0:T(8,128)(2,1)S(1)} collective-permute-done((bf16[5,8,8192]{2,1,0:T(8,128)(2,1)}, bf16[5,8,8192]{2,1,0:T(8,128)(2,1)S(1)}, u32[]{:S(2)}, u32[]{:S(2)}) %collective-permute-start) | collective-permute-done | bytes 655392 | tf_op jit(solution)/shard_map/while/body/eval_jaxpr/ppermute | solution.py:25
  141.7 16.3 %collective-permute-done = bf16[5,8,8192]{2,1,0:T(8,128)(2,1)S(1)} collective-permute-done((bf16[5,8,8192]{2,1,0:T(8,128)(2,1)}, bf16[5,8,8192]{2,1,0:T(8,128)(2,1)S(1)}, u32[]{:S(2)}, u32[]{:S(2)}) %collective-permute-start) | collective-permute-done | bytes 655392 | tf_op jit(solution)/shard_map/while/body/eval_jaxpr/ppermute | solution.py:25
  161.8 15.4 %collective-permute-done = bf16[5,8,8192]{2,1,0:T(8,128)(2,1)S(1)} collective-permute-done((bf16[5,8,8192]{2,1,0:T(8,128)(2,1)}, bf16[5,8,8192]{2,1,0:T(8,128)(2,1)S(1)}, u32[]{:S(2)}, u32[]{:S(2)}) %collective-permute-start) | collective-permute-done | bytes 655392 | tf_op jit(solution)/shard_map/while/body/eval_jaxpr/ppermute | solution.py:25
  180.9 14.5 %collective-permute-done = bf16[5,8,8192]{2,1,0:T(8,128)(2,1)S(1)} collective-permute-done((bf16[5,8,8192]{2,1,0:T(8,128)(2,1)}, bf16[5,8,8192]{2,1,0:T(8,128)(2,1)S(1)}, u32[]{:S(2)}, u32[]{:S(2)}) %collective-permute-start) | collective-permute-done | bytes 655392 | tf_op jit(solution)/shard_map/while/body/eval_jaxpr/ppermute | solution.py:25
  199.2 13.6 %collective-permute-done = bf16[5,8,8192]{2,1,0:T(8,128)(2,1)S(1)} collective-permute-done((bf16[5,8,8192]{2,1,0:T(8,128)(2,1)}, bf16[5,8,8192]{2,1,0:T(8,128)(2,1)S(1)}, u32[]{:S(2)}, u32[]{:S(2)}) %collective-permute-start) | collective-permute-done | bytes 655392 | tf_op jit(solution)/shard_map/while/body/eval_jaxpr/ppermute | solution.py:25
  216.5 12.8 %collective-permute-done = bf16[5,8,8192]{2,1,0:T(8,128)(2,1)S(1)} collective-permute-done((bf16[5,8,8192]{2,1,0:T(8,128)(2,1)}, bf16[5,8,8192]{2,1,0:T(8,128)(2,1)S(1)}, u32[]{:S(2)}, u32[]{:S(2)}) %collective-permute-start) | collective-permute-done | bytes 655392 | tf_op jit(solution)/shard_map/while/body/eval_jaxpr/ppermute | solution.py:25
  233.1 12.8 %collective-permute-done = bf16[5,8,8192]{2,1,0:T(8,128)(2,1)S(1)} collective-permute-done((bf16[5,8,8192]{2,1,0:T(8,128)(2,1)}, bf16[5,8,8192]{2,1,0:T(8,128)(2,1)S(1)}, u32[]{:S(2)}, u32[]{:S(2)}) %collective-permute-start) | collective-permute-done | bytes 655392 | tf_op jit(solution)/shard_map/while/body/eval_jaxpr/ppermute | solution.py:25
  249.6 13.9 %collective-permute-done = bf16[5,8,8192]{2,1,0:T(8,128)(2,1)S(1)} collective-permute-done((bf16[5,8,8192]{2,1,0:T(8,128)(2,1)}, bf16[5,8,8192]{2,1,0:T(8,128)(2,1)S(1)}, u32[]{:S(2)}, u32[]{:S(2)}) %collective-permute-start) | collective-permute-done | bytes 655392 | tf_op jit(solution)/shard_map/while/body/eval_jaxpr/ppermute | solution.py:25
  267.2 14.9 %collective-permute-done = bf16[5,8,8192]{2,1,0:T(8,128)(2,1)S(1)} collective-permute-done((bf16[5,8,8192]{2,1,0:T(8,128)(2,1)}, bf16[5,8,8192]{2,1,0:T(8,128)(2,1)S(1)}, u32[]{:S(2)}, u32[]{:S(2)}) %collective-permute-start) | collective-permute-done | bytes 655392 | tf_op jit(solution)/shard_map/while/body/eval_jaxpr/ppermute | solution.py:25
  285.9 16.0 %collective-permute-done = bf16[5,8,8192]{2,1,0:T(8,128)(2,1)S(1)} collective-permute-done((bf16[5,8,8192]{2,1,0:T(8,128)(2,1)}, bf16[5,8,8192]{2,1,0:T(8,128)(2,1)S(1)}, u32[]{:S(2)}, u32[]{:S(2)}) %collective-permute-start) | collective-permute-done | bytes 655392 | tf_op jit(solution)/shard_map/while/body/eval_jaxpr/ppermute | solution.py:25
  305.7 12.8 %collective-permute-done = bf16[5,8,8192]{2,1,0:T(8,128)(2,1)S(1)} collective-permute-done((bf16[5,8,8192]{2,1,0:T(8,128)(2,1)}, bf16[5,8,8192]{2,1,0:T(8,128)(2,1)S(1)}, u32[]{:S(2)}, u32[]{:S(2)}) %collective-permute-start) | collective-permute-done | bytes 655392 | tf_op jit(solution)/shard_map/while/body/eval_jaxpr/ppermute | solution.py:25
  322.2 74.1 %psum.7 = f32[16,16,5,4]{1,2,0,3:T(8,128)S(1)} all-reduce(f32[16,16,5,4]{1,2,0,3:T(8,128)S(1)} %copy.10), channel_id=1, replica_groups=mesh['bin'=16,'sky'=16] {'bin','sky'}, use_global_device_ids=true, to_apply=%region_10.11 | all-reduce | flops 5120 | bytes 40960 | tf_op jit(solution)/shard_map/psum | solution.py:157
  398.4 1.8 fusion.116
  400.2 4.0 fusion.78
  404.4 116.3 %while.43 = (s32[]{:T(128)}, f32[5,8,8192]{2,1,0:T(8,128)S(1)}, s32[]{:T(128)}, f32[16,16,5,4]{1,3,2,0:T(4,128)S(1)}, bf16[15,5,8,8192]{3,2,1,0:T(8,128)(2,1)}, ...) while((s32[]{:T(128)}, f32[5,8,8192]{2,1,0:T(8,128)S(1)}, ...), condition=%wide.region_12.13_spmd.clone.clone, body=%wide.region_11.12_spmd.clone.clone.sunk | while | flops 7608159 | bytes 29140764 | solution.py:179
  404.9 2.0 convolution_bitcast_fusion.4
  409.7 2.4 fusion.129
  412.6 2.0 convolution_bitcast_fusion.4
  417.5 2.4 fusion.129
  420.4 2.0 convolution_bitcast_fusion.4
  425.3 2.4 fusion.129
  428.1 2.0 convolution_bitcast_fusion.4
  433.0 2.4 fusion.129
  435.9 2.0 convolution_bitcast_fusion.4
  440.8 2.4 fusion.129
  443.7 2.0 convolution_bitcast_fusion.4
  448.5 2.4 fusion.129
  451.4 2.0 convolution_bitcast_fusion.4
  456.3 2.4 fusion.129
  459.2 2.0 convolution_bitcast_fusion.4
  464.0 2.4 fusion.129
  466.9 2.0 convolution_bitcast_fusion.4
  471.8 2.4 fusion.129
  474.7 2.0 convolution_bitcast_fusion.4
  479.5 2.4 fusion.129
  482.4 2.0 convolution_bitcast_fusion.4
  487.3 2.4 fusion.129
  490.2 2.0 convolution_bitcast_fusion.4
  495.1 2.4 fusion.129
  497.9 2.0 convolution_bitcast_fusion.4
  502.8 2.4 fusion.129
  505.7 2.0 convolution_bitcast_fusion.4
  510.6 2.4 fusion.129
  513.5 2.0 convolution_bitcast_fusion.4
  518.3 2.4 fusion.129
  521.0 5.9 %multiply_add_fusion.3 = f32[5,8,8192]{2,1,0:T(8,128)S(1)} fusion(f32[5,8,8192]{2,1,0:T(8,128)S(1)} %get-tuple-element.629, f32[5]{0:T(128)S(1)} %copy-done.40, f32[5]{0:T(128)S(1)} %copy-done.43, f32[5]{0:T(128)S(1)} %get-tuple-element.764, f32[5]{0:T(128)S(1)} %get-tuple-element.765, f32[5]{0:T(128)S(1)} %get-tuple-element.766, f32[5]{0:T(128)S(1)} %copy-done.7, ...), kind=kLoop, calls=%fused_computation.127 | loop fusion | flops 10813440 | bytes 2621780 | tf_op jit(solution)/shard_map/add | solution.py:89
  526.9 1.9 collective-permute-start.3
  528.9 5.4 collective-permute-start.4
  534.9 26.5 %collective-permute-done.3 = f32[5,8,8192]{2,1,0:T(8,128)S(1)} collective-permute-done((f32[5,8,8192]{2,1,0:T(8,128)S(1)}, f32[5,8,8192]{2,1,0:T(8,128)S(1)}, u32[]{:S(2)}, u32[]{:S(2)}) %collective-permute-start.3) | collective-permute-done | bytes 1310752 | tf_op jit(solution)/shard_map/ppermute | solution.py:14
  561.5 5.2 fusion.36
  (565 shorter events, 113.3 us)
Async XLA Ops:
  0.6 10.9 %collective-permute-start.1 = (bf16[8,8192]{1,0:T(8,128)(2,1)}, bf16[8,8192]{1,0:T(8,128)(2,1)S(1)}, u32[]{:S(2)}, u32[]{:S(2)}) collective-permute-start(bf16[8,8192]{1,0:T(8,128)(2,1)} %bitcast.117), channel_id=1, source_target_pairs={{0,1},{1,2},{2,3},{3,4},{4,5},{5,6},{6,7},{7,8},{8,9},{9,10},{10,1... | collective-permute-start | bytes 393224 | tf_op jit(solution)/shard_map/ppermute | solution.py:14
  2.6 9.0 %collective-permute-start.2 = (bf16[8,8192]{1,0:T(8,128)(2,1)}, bf16[8,8192]{1,0:T(8,128)(2,1)S(1)}, u32[]{:S(2)}, u32[]{:S(2)}) collective-permute-start(bf16[8,8192]{1,0:T(8,128)(2,1)} %bitcast.118), channel_id=1, source_target_pairs={{1,0},{2,1},{3,2},{4,3},{5,4},{6,5},{7,6},{8,7},{9,8},{10,9},{11,1... | collective-permute-start | bytes 393224 | tf_op jit(solution)/shard_map/ppermute | solution.py:17
  28.0 20.9 %collective-permute-start = (bf16[5,8,8192]{2,1,0:T(8,128)(2,1)}, bf16[5,8,8192]{2,1,0:T(8,128)(2,1)S(1)}, u32[]{:S(2)}, u32[]{:S(2)}) collective-permute-start(bf16[5,8,8192]{2,1,0:T(8,128)(2,1)} %get-tuple-element.1039), channel_id=1, source_target_pairs={{0,16},{16,32},{32,48},{48,64},{64,80},{80,96},{96,112},{112,128},... | collective-permute-start | bytes 1966088 | tf_op jit(solution)/shard_map/while/body/eval_jaxpr/ppermute | solution.py:25
  52.6 19.6 %collective-permute-start = (bf16[5,8,8192]{2,1,0:T(8,128)(2,1)}, bf16[5,8,8192]{2,1,0:T(8,128)(2,1)S(1)}, u32[]{:S(2)}, u32[]{:S(2)}) collective-permute-start(bf16[5,8,8192]{2,1,0:T(8,128)(2,1)} %get-tuple-element.1039), channel_id=1, source_target_pairs={{0,16},{16,32},{32,48},{48,64},{64,80},{80,96},{96,112},{112,128},... | collective-permute-start | bytes 1966088 | tf_op jit(solution)/shard_map/while/body/eval_jaxpr/ppermute | solution.py:25
  75.9 19.1 %collective-permute-start = (bf16[5,8,8192]{2,1,0:T(8,128)(2,1)}, bf16[5,8,8192]{2,1,0:T(8,128)(2,1)S(1)}, u32[]{:S(2)}, u32[]{:S(2)}) collective-permute-start(bf16[5,8,8192]{2,1,0:T(8,128)(2,1)} %get-tuple-element.1039), channel_id=1, source_target_pairs={{0,16},{16,32},{32,48},{48,64},{64,80},{80,96},{96,112},{112,128},... | collective-permute-start | bytes 1966088 | tf_op jit(solution)/shard_map/while/body/eval_jaxpr/ppermute | solution.py:25
  98.6 18.3 %collective-permute-start = (bf16[5,8,8192]{2,1,0:T(8,128)(2,1)}, bf16[5,8,8192]{2,1,0:T(8,128)(2,1)S(1)}, u32[]{:S(2)}, u32[]{:S(2)}) collective-permute-start(bf16[5,8,8192]{2,1,0:T(8,128)(2,1)} %get-tuple-element.1039), channel_id=1, source_target_pairs={{0,16},{16,32},{32,48},{48,64},{64,80},{80,96},{96,112},{112,128},... | collective-permute-start | bytes 1966088 | tf_op jit(solution)/shard_map/while/body/eval_jaxpr/ppermute | solution.py:25
  120.6 17.3 %collective-permute-start = (bf16[5,8,8192]{2,1,0:T(8,128)(2,1)}, bf16[5,8,8192]{2,1,0:T(8,128)(2,1)S(1)}, u32[]{:S(2)}, u32[]{:S(2)}) collective-permute-start(bf16[5,8,8192]{2,1,0:T(8,128)(2,1)} %get-tuple-element.1039), channel_id=1, source_target_pairs={{0,16},{16,32},{32,48},{48,64},{64,80},{80,96},{96,112},{112,128},... | collective-permute-start | bytes 1966088 | tf_op jit(solution)/shard_map/while/body/eval_jaxpr/ppermute | solution.py:25
  141.6 16.4 %collective-permute-start = (bf16[5,8,8192]{2,1,0:T(8,128)(2,1)}, bf16[5,8,8192]{2,1,0:T(8,128)(2,1)S(1)}, u32[]{:S(2)}, u32[]{:S(2)}) collective-permute-start(bf16[5,8,8192]{2,1,0:T(8,128)(2,1)} %get-tuple-element.1039), channel_id=1, source_target_pairs={{0,16},{16,32},{32,48},{48,64},{64,80},{80,96},{96,112},{112,128},... | collective-permute-start | bytes 1966088 | tf_op jit(solution)/shard_map/while/body/eval_jaxpr/ppermute | solution.py:25
  161.7 15.5 %collective-permute-start = (bf16[5,8,8192]{2,1,0:T(8,128)(2,1)}, bf16[5,8,8192]{2,1,0:T(8,128)(2,1)S(1)}, u32[]{:S(2)}, u32[]{:S(2)}) collective-permute-start(bf16[5,8,8192]{2,1,0:T(8,128)(2,1)} %get-tuple-element.1039), channel_id=1, source_target_pairs={{0,16},{16,32},{32,48},{48,64},{64,80},{80,96},{96,112},{112,128},... | collective-permute-start | bytes 1966088 | tf_op jit(solution)/shard_map/while/body/eval_jaxpr/ppermute | solution.py:25
  180.8 14.6 %collective-permute-start = (bf16[5,8,8192]{2,1,0:T(8,128)(2,1)}, bf16[5,8,8192]{2,1,0:T(8,128)(2,1)S(1)}, u32[]{:S(2)}, u32[]{:S(2)}) collective-permute-start(bf16[5,8,8192]{2,1,0:T(8,128)(2,1)} %get-tuple-element.1039), channel_id=1, source_target_pairs={{0,16},{16,32},{32,48},{48,64},{64,80},{80,96},{96,112},{112,128},... | collective-permute-start | bytes 1966088 | tf_op jit(solution)/shard_map/while/body/eval_jaxpr/ppermute | solution.py:25
  199.1 13.7 %collective-permute-start = (bf16[5,8,8192]{2,1,0:T(8,128)(2,1)}, bf16[5,8,8192]{2,1,0:T(8,128)(2,1)S(1)}, u32[]{:S(2)}, u32[]{:S(2)}) collective-permute-start(bf16[5,8,8192]{2,1,0:T(8,128)(2,1)} %get-tuple-element.1039), channel_id=1, source_target_pairs={{0,16},{16,32},{32,48},{48,64},{64,80},{80,96},{96,112},{112,128},... | collective-permute-start | bytes 1966088 | tf_op jit(solution)/shard_map/while/body/eval_jaxpr/ppermute | solution.py:25
  216.4 12.9 %collective-permute-start = (bf16[5,8,8192]{2,1,0:T(8,128)(2,1)}, bf16[5,8,8192]{2,1,0:T(8,128)(2,1)S(1)}, u32[]{:S(2)}, u32[]{:S(2)}) collective-permute-start(bf16[5,8,8192]{2,1,0:T(8,128)(2,1)} %get-tuple-element.1039), channel_id=1, source_target_pairs={{0,16},{16,32},{32,48},{48,64},{64,80},{80,96},{96,112},{112,128},... | collective-permute-start | bytes 1966088 | tf_op jit(solution)/shard_map/while/body/eval_jaxpr/ppermute | solution.py:25
  233.0 12.9 %collective-permute-start = (bf16[5,8,8192]{2,1,0:T(8,128)(2,1)}, bf16[5,8,8192]{2,1,0:T(8,128)(2,1)S(1)}, u32[]{:S(2)}, u32[]{:S(2)}) collective-permute-start(bf16[5,8,8192]{2,1,0:T(8,128)(2,1)} %get-tuple-element.1039), channel_id=1, source_target_pairs={{0,16},{16,32},{32,48},{48,64},{64,80},{80,96},{96,112},{112,128},... | collective-permute-start | bytes 1966088 | tf_op jit(solution)/shard_map/while/body/eval_jaxpr/ppermute | solution.py:25
  249.5 13.9 %collective-permute-start = (bf16[5,8,8192]{2,1,0:T(8,128)(2,1)}, bf16[5,8,8192]{2,1,0:T(8,128)(2,1)S(1)}, u32[]{:S(2)}, u32[]{:S(2)}) collective-permute-start(bf16[5,8,8192]{2,1,0:T(8,128)(2,1)} %get-tuple-element.1039), channel_id=1, source_target_pairs={{0,16},{16,32},{32,48},{48,64},{64,80},{80,96},{96,112},{112,128},... | collective-permute-start | bytes 1966088 | tf_op jit(solution)/shard_map/while/body/eval_jaxpr/ppermute | solution.py:25
  267.1 15.0 %collective-permute-start = (bf16[5,8,8192]{2,1,0:T(8,128)(2,1)}, bf16[5,8,8192]{2,1,0:T(8,128)(2,1)S(1)}, u32[]{:S(2)}, u32[]{:S(2)}) collective-permute-start(bf16[5,8,8192]{2,1,0:T(8,128)(2,1)} %get-tuple-element.1039), channel_id=1, source_target_pairs={{0,16},{16,32},{32,48},{48,64},{64,80},{80,96},{96,112},{112,128},... | collective-permute-start | bytes 1966088 | tf_op jit(solution)/shard_map/while/body/eval_jaxpr/ppermute | solution.py:25
  285.8 16.1 %collective-permute-start = (bf16[5,8,8192]{2,1,0:T(8,128)(2,1)}, bf16[5,8,8192]{2,1,0:T(8,128)(2,1)S(1)}, u32[]{:S(2)}, u32[]{:S(2)}) collective-permute-start(bf16[5,8,8192]{2,1,0:T(8,128)(2,1)} %get-tuple-element.1039), channel_id=1, source_target_pairs={{0,16},{16,32},{32,48},{48,64},{64,80},{80,96},{96,112},{112,128},... | collective-permute-start | bytes 1966088 | tf_op jit(solution)/shard_map/while/body/eval_jaxpr/ppermute | solution.py:25
  305.6 12.9 %collective-permute-start = (bf16[5,8,8192]{2,1,0:T(8,128)(2,1)}, bf16[5,8,8192]{2,1,0:T(8,128)(2,1)S(1)}, u32[]{:S(2)}, u32[]{:S(2)}) collective-permute-start(bf16[5,8,8192]{2,1,0:T(8,128)(2,1)} %get-tuple-element.1039), channel_id=1, source_target_pairs={{0,16},{16,32},{32,48},{48,64},{64,80},{80,96},{96,112},{112,128},... | collective-permute-start | bytes 1966088 | tf_op jit(solution)/shard_map/while/body/eval_jaxpr/ppermute | solution.py:25
  322.2 76.2 %copy-start = (f32[8189]{0:T(1024)}, f32[8189]{0:T(1024)S(1)}, u32[]{:S(2)}) copy-start(f32[8189]{0:T(1024)S(1)} %get-tuple-element.1112) | copy-start | bytes 98272
  322.2 74.8 %copy-start.4 = (f32[136,5,4]{0,2,1:T(4,128)S(1)}, f32[136,5,4]{0,2,1:T(4,128)}, u32[]{:S(2)}) copy-start(f32[136,5,4]{0,2,1:T(4,128)} %param.15) | copy-start | bytes 32644
  322.2 74.8 %copy-start.5 = (f32[136,5,4]{0,2,1:T(4,128)S(1)}, f32[136,5,4]{0,2,1:T(4,128)}, u32[]{:S(2)}) copy-start(f32[136,5,4]{0,2,1:T(4,128)} %param.14) | copy-start | bytes 32644
  404.3 116.5 %copy-start.7 = (f32[5]{0:T(128)S(1)}, f32[5]{0:T(128)}, u32[]{:S(2)}) copy-start(f32[5]{0:T(128)} %copy-done.6) | copy-start | bytes 64
  404.3 116.5 %copy-start.10 = (f32[5]{0:T(128)S(1)}, f32[5]{0:T(128)}, u32[]{:S(2)}) copy-start(f32[5]{0:T(128)} %copy-done.9) | copy-start | bytes 64
  404.3 116.5 %copy-start.13 = (f32[5]{0:T(128)S(1)}, f32[5]{0:T(128)}, u32[]{:S(2)}) copy-start(f32[5]{0:T(128)} %copy-done.12) | copy-start | bytes 64
  404.3 116.5 %copy-start.16 = (f32[5]{0:T(128)S(1)}, f32[5]{0:T(128)}, u32[]{:S(2)}) copy-start(f32[5]{0:T(128)} %copy-done.15) | copy-start | bytes 64
  404.3 116.5 %copy-start.19 = (f32[5]{0:T(128)S(1)}, f32[5]{0:T(128)}, u32[]{:S(2)}) copy-start(f32[5]{0:T(128)} %copy-done.18) | copy-start | bytes 64
  404.3 116.5 %copy-start.22 = (f32[5]{0:T(128)S(1)}, f32[5]{0:T(128)}, u32[]{:S(2)}) copy-start(f32[5]{0:T(128)} %copy-done.21) | copy-start | bytes 64
  404.3 116.5 %copy-start.25 = (f32[5]{0:T(128)S(1)}, f32[5]{0:T(128)}, u32[]{:S(2)}) copy-start(f32[5]{0:T(128)} %copy-done.24) | copy-start | bytes 64
  404.3 116.5 %copy-start.28 = (f32[5]{0:T(128)S(1)}, f32[5]{0:T(128)}, u32[]{:S(2)}) copy-start(f32[5]{0:T(128)} %copy-done.27) | copy-start | bytes 64
  404.3 116.5 %copy-start.31 = (f32[5]{0:T(128)S(1)}, f32[5]{0:T(128)}, u32[]{:S(2)}) copy-start(f32[5]{0:T(128)} %copy-done.30) | copy-start | bytes 64
  404.3 116.5 %copy-start.34 = (f32[5]{0:T(128)S(1)}, f32[5]{0:T(128)}, u32[]{:S(2)}) copy-start(f32[5]{0:T(128)} %copy-done.33) | copy-start | bytes 64
  404.4 116.5 %copy-start.37 = (f32[5]{0:T(128)S(1)}, f32[5]{0:T(128)}, u32[]{:S(2)}) copy-start(f32[5]{0:T(128)} %copy-done.36) | copy-start | bytes 64
  404.4 116.5 %copy-start.40 = (f32[5]{0:T(128)S(1)}, f32[5]{0:T(128)}, u32[]{:S(2)}) copy-start(f32[5]{0:T(128)} %copy-done.39) | copy-start | bytes 64
  404.4 116.5 %copy-start.43 = (f32[5]{0:T(128)S(1)}, f32[5]{0:T(128)}, u32[]{:S(2)}) copy-start(f32[5]{0:T(128)} %copy-done.42) | copy-start | bytes 64
  404.4 4.1 copy-start.1
  412.2 4.1 copy-start.1
  419.9 4.1 copy-start.1
  427.7 4.1 copy-start.1
  435.4 4.1 copy-start.1
  443.2 4.1 copy-start.1
  450.9 4.1 copy-start.1
  458.7 4.1 copy-start.1
  466.4 4.1 copy-start.1
  474.2 4.1 copy-start.1
  481.9 4.1 copy-start.1
  489.7 4.1 copy-start.1
  497.5 4.1 copy-start.1
  505.2 4.1 copy-start.1
  513.0 4.1 copy-start.1
  520.8 13.4 %copy-start.3 = (f32[136,5,4]{0,1,2:T(8,128)S(1)}, f32[136,5,4]{0,1,2:T(8,128)}, u32[]{:S(2)}) copy-start(f32[136,5,4]{0,1,2:T(8,128)} %copy-done.2) | copy-start | bytes 32644
  520.9 40.6 %copy-start.8 = (f32[5]{0:T(128)S(1)}, f32[5]{0:T(128)}, u32[]{:S(2)}) copy-start(f32[5]{0:T(128)} %copy-done.6) | copy-start | bytes 64
  520.9 40.6 %copy-start.11 = (f32[5]{0:T(128)S(1)}, f32[5]{0:T(128)}, u32[]{:S(2)}) copy-start(f32[5]{0:T(128)} %copy-done.9) | copy-start | bytes 64
  520.9 40.5 %copy-start.14 = (f32[5]{0:T(128)S(1)}, f32[5]{0:T(128)}, u32[]{:S(2)}) copy-start(f32[5]{0:T(128)} %copy-done.12) | copy-start | bytes 64
  520.9 40.5 %copy-start.17 = (f32[5]{0:T(128)S(1)}, f32[5]{0:T(128)}, u32[]{:S(2)}) copy-start(f32[5]{0:T(128)} %copy-done.15) | copy-start | bytes 64
  520.9 40.5 %copy-start.20 = (f32[5]{0:T(128)S(1)}, f32[5]{0:T(128)}, u32[]{:S(2)}) copy-start(f32[5]{0:T(128)} %copy-done.18) | copy-start | bytes 64
  520.9 40.5 %copy-start.23 = (f32[5]{0:T(128)S(1)}, f32[5]{0:T(128)}, u32[]{:S(2)}) copy-start(f32[5]{0:T(128)} %copy-done.21) | copy-start | bytes 64
  520.9 40.5 %copy-start.26 = (f32[5]{0:T(128)S(1)}, f32[5]{0:T(128)}, u32[]{:S(2)}) copy-start(f32[5]{0:T(128)} %copy-done.24) | copy-start | bytes 64
  520.9 40.5 %copy-start.29 = (f32[5]{0:T(128)S(1)}, f32[5]{0:T(128)}, u32[]{:S(2)}) copy-start(f32[5]{0:T(128)} %copy-done.27) | copy-start | bytes 64
  520.9 40.5 %copy-start.32 = (f32[5]{0:T(128)S(1)}, f32[5]{0:T(128)}, u32[]{:S(2)}) copy-start(f32[5]{0:T(128)} %copy-done.30) | copy-start | bytes 64
  521.0 40.5 %copy-start.35 = (f32[5]{0:T(128)S(1)}, f32[5]{0:T(128)}, u32[]{:S(2)}) copy-start(f32[5]{0:T(128)} %copy-done.33) | copy-start | bytes 64
  521.0 40.5 %copy-start.38 = (f32[5]{0:T(128)S(1)}, f32[5]{0:T(128)}, u32[]{:S(2)}) copy-start(f32[5]{0:T(128)} %copy-done.36) | copy-start | bytes 64
  521.0 40.5 %copy-start.41 = (f32[5]{0:T(128)S(1)}, f32[5]{0:T(128)}, u32[]{:S(2)}) copy-start(f32[5]{0:T(128)} %copy-done.39) | copy-start | bytes 64
  521.0 40.5 %copy-start.44 = (f32[5]{0:T(128)S(1)}, f32[5]{0:T(128)}, u32[]{:S(2)}) copy-start(f32[5]{0:T(128)} %copy-done.42) | copy-start | bytes 64
  526.9 34.5 %collective-permute-start.3 = (f32[5,8,8192]{2,1,0:T(8,128)S(1)}, f32[5,8,8192]{2,1,0:T(8,128)S(1)}, u32[]{:S(2)}, u32[]{:S(2)}) collective-permute-start(f32[5,8,8192]{2,1,0:T(8,128)S(1)} %multiply_add_fusion.3), channel_id=1, source_target_pairs={{0,1},{1,2},{2,3},{3,4},{4,5},{5,6},{6,7},{7,8},{8,9},{9,10},{10,1... | collective-permute-start | bytes 3932168 | tf_op jit(solution)/shard_map/ppermute | solution.py:14
  528.9 32.5 %collective-permute-start.4 = (f32[5,8,8192]{2,1,0:T(8,128)S(1)}, f32[5,8,8192]{2,1,0:T(8,128)S(1)}, u32[]{:S(2)}, u32[]{:S(2)}) collective-permute-start(f32[5,8,8192]{2,1,0:T(8,128)S(1)} %multiply_add_fusion.3), channel_id=1, source_target_pairs={{1,0},{2,1},{3,2},{4,3},{5,4},{6,5},{7,6},{8,7},{9,8},{10,9},{11,1... | collective-permute-start | bytes 3932168 | tf_op jit(solution)/shard_map/ppermute | solution.py:17
  (14 other events, 45.4 us)
where the time goes:
time: 570 us; the launch traced here: 567 us
  waiting for transfers between devices  262 us (46%)
  other arithmetic  135 us (24%)
  blocking collectives  74.1 us (13%)
  local copies, waits for them, and re-layouts  42.4 us (7%)
  matrix products  33.2 us (6%)
  starting transfers between devices  16.4 us (3%)
    ppermute x15, waiting for transfers between devices, shifted(): return lax.ppermute(value, axis, pairs)  236 us
    psum x1, blocking collectives, per_device(): pair_table = lax.psum(tables, ('bin', 'sky'))  74.1 us
    add x15, other arithmetic, reread(): return totals + partner_term(visitor, k)  35.8 us
    dot_general x16, matrix products, take_block(): return jnp.einsum('i,j,ijsl->sl', row_hot, col_hot, table, precision=HIGH)  31.5 us
    ppermute x2, waiting for transfers between devices, with_halo(): lax.ppermute(lax.slice_in_dim(block, block.shape[dim] - width, None, axis...  26.5 us
    reduce_sum x61, other arithmetic, lagged(): columns.append(jnp.sum(product, axis=(1, 2)))  25.1 us
    mul x48, other arithmetic, adjoint_lags(): joint_mask[None] * widened[:, :, offset:]  24.7 us
    while x120, local copies, waits for them, and re-layouts  19.9 us
  transfers between devices with their start and end apart: 19, of which 16 were waited for; matrix products, arithmetic and copies ran while one was open for 1% of the time, Pallas kernels for 0%

commit v1 on v0

v1 whole, which is shorter than its diff:
```python
import jax
import jax.numpy as jnp
from jax import lax
from jax.experimental import pallas as pl
from jax.experimental.pallas import tpu as pltpu
from jax.sharding import PartitionSpec as P

F32 = jnp.float32
BF16 = jnp.bfloat16
HIGH = lax.Precision.HIGHEST

BINS = 16
SCALES = 5
TAPS = 17
LAGS = 4
ROWS = 8
OWN = 512
LANE = 128
EDGE = 64
WIN = OWN + 2 * EDGE
RAW = OWN + 4 * EDGE
XB = ROWS * BINS


def full(shape):
    return pl.BlockSpec(shape, lambda *_: (0,) * len(shape))


def per_scale(shape):
    return pl.BlockSpec((1,) + shape, lambda s: (s,) + (0,) * len(shape))


SMEM = pl.BlockSpec(memory_space=pltpu.SMEM)


def split2(v):
    hi = v.astype(BF16)
    return hi, (v - hi.astype(F32)).astype(BF16)


def iota(shape, dim):
    return lax.broadcasted_iota(jnp.int32, shape, dim)


def windows_kernel(x_ref, out_ref):
    x = x_ref[...].astype(F32)
    count = x.shape[1] // OWN
    blank = jnp.zeros((ROWS, LANE), F32)

    def window(b):
        parts = []
        if b == 0:
            parts.append(blank)
        low = max(b * OWN - LANE, 0)
        high = min((b + 1) * OWN + LANE, x.shape[1])
        parts.append(x[:, low:high])
        if b == count - 1:
            parts.append(blank)
        return jnp.concatenate(parts, axis=1) if len(parts) > 1 else parts[0]

    for p in range(count // 2):
        pair = jnp.concatenate([window(2 * p), window(2 * p + 1)], axis=0)
        out_ref[2 * ROWS * p : 2 * ROWS * (p + 1), :] = pair.astype(BF16)


def matrices_kernel(taps_ref, r_ref, w_ref, wa_ref, ra_ref):
    q = iota((XB, 3 * XB), 0)
    n = iota((XB, 3 * XB), 1)
    row_tap = jnp.where(q % BINS == (n % XB) // ROWS, n % ROWS - q // BINS + ROWS * (n // XB), -1)
    n = iota((2 * LANE, LANE), 0)
    o = iota((2 * LANE, LANE), 1)
    col_tap = n - o - 56
    col_adj_tap = o + 72 - n
    q = iota((3 * XB, XB), 0)
    n = iota((3 * XB, XB), 1)
    row_adj_tap = jnp.where(
        (q % XB) // ROWS == n % BINS, q % ROWS - n // BINS + ROWS * (q // XB), -1
    )

    def spread(index, s):
        value = jnp.zeros(index.shape, F32)
        for a in range(TAPS):
            value = jnp.where(index == a, taps_ref[s, a], value)
        return split2(value)

    def one(s, carry):
        hi, lo = spread(row_tap, s)
        r_ref[s, 0:XB, :] = hi
        r_ref[s, XB : 2 * XB, :] = lo
        hi, lo = spread(col_tap, s)
        w_ref[s, :, 0:LANE] = hi
        w_ref[s, :, LANE : 2 * LANE] = lo
        hi, lo = spread(col_adj_tap, s)
        wa_ref[s, :, 0:LANE] = hi
        wa_ref[s, :, LANE : 2 * LANE] = lo
        hi, lo = spread(row_adj_tap, s)
        at = pl.ds(pl.multiple_of(s * XB, XB), XB)
        ra_ref[0, :, at] = hi
        ra_ref[1, :, at] = lo
        return carry

    lax.fori_loop(0, SCALES, one, 0)


def window_mask(mask_ref):
    b = lax.axis_index("bin")
    tiles = mask_ref.shape[1]
    lane = iota((1, LANE), 1)

    def tile(t):
        value = mask_ref[0, jnp.clip(t, 0, tiles - 1)]
        return jnp.where((t >= 0) & (t < tiles), value, 0)

    first = b * (OWN // LANE)
    parts = [
        jnp.where(lane < EDGE, tile(first + f - 1), tile(first + f)) for f in range(WIN // LANE)
    ]
    return jnp.concatenate(parts, axis=1)


def banded(v, w, tiles):
    parts = split2(v)
    stacked = jnp.concatenate(
        [p[:, LANE * f : LANE * (f + 2)] for p in parts for f in range(tiles)], axis=0
    )
    d = jnp.dot(stacked, w, preferred_element_type=F32)
    d = d[:, :LANE] + d[:, LANE:]
    return [d[XB * f : XB * (f + 1)] + d[XB * (tiles + f) : XB * (tiles + f + 1)] for f in range(tiles)]


def forward_kernel(mask_ref, up_ref, own_ref, down_ref, r_ref, w_ref, g_ref, table_ref, raw_ref):
    s = pl.program_id(0)

    @pl.when(s == 0)
    def _():
        raw_ref[0:XB, :] = up_ref[...]
        raw_ref[XB : 2 * XB, :] = own_ref[...]
        raw_ref[2 * XB : 3 * XB, :] = down_ref[...]

    d = jnp.dot(r_ref[0], raw_ref[...], preferred_element_type=F32)
    row_pass = d[:XB] + d[XB:]
    tiles = banded(row_pass, w_ref[0], WIN // LANE)
    mask = window_mask(mask_ref)
    filtered = jnp.concatenate(tiles, axis=1).astype(BF16).astype(F32)
    g = jnp.where(mask != 0, filtered, 0.0)
    for l in range(LAGS):
        for side in range(2):
            steps = (WIN - l) % WIN if side == 0 else l
            moved = pltpu.roll(g, steps, 1) if steps else g
            at = (side * LAGS + l) * BINS
            g_ref[0, :, at : at + BINS, :] = moved.astype(BF16).reshape(ROWS, BINS, WIN)
    lane = iota((XB, WIN), 1)
    left = jnp.where((lane >= EDGE) & (lane < EDGE + OWN), g, 0.0).astype(BF16)
    right = g_ref[0, :, 0 : LAGS * BINS, :].reshape(ROWS * LAGS * BINS, WIN)
    cross = lax.dot_general(left, right, (((1,), (1,)), ((), ())), preferred_element_type=F32)
    width = LAGS * BINS
    lane = iota((BINS, ROWS * width), 1)
    total = jnp.zeros((BINS, ROWS * width), F32)
    for x in range(ROWS):
        total = total + jnp.where(lane // width == x, cross[BINS * x : BINS * (x + 1)], 0.0)
    total = sum(total[:, LANE * i : LANE * (i + 1)] for i in range(ROWS * width // LANE))
    total = total[:, :width] + total[:, width:]
    for i in range(SCALES):

        @pl.when(s == i)
        def _():
            table_ref[:, width * i : width * (i + 1)] = total


def backward_kernel(
    inverse_area,
    mask_ref, table_ref, pairs_ref, target_ref, weight_ref, g_ref, wa_ref, ra_ref,
    corr_ref, up_ref, own_ref, down_ref, a_ref, hi_ref, lo_ref,
):
    s = pl.program_id(0)
    width = LAGS * BINS
    total = SCALES * width

    @pl.when(s == 0)
    def _():
        count = pairs_ref.shape[0]
        first = pairs_ref[:, 0:1]
        second = pairs_ref[:, 1:2]
        bins = iota((count, BINS), 1)
        left = (first == bins).astype(F32)
        right = (second == bins).astype(F32)
        bins = iota((count, total), 1) % BINS
        left_wide = (first == bins).astype(F32)
        right_wide = (second == bins).astype(F32)
        entries = SCALES * LAGS
        expand = (iota((entries, total), 1) // BINS == iota((entries, total), 0)).astype(F32)

        def dot(a, b, dims):
            return lax.dot_general(a, b, (dims, ((), ())), precision=HIGH, preferred_element_type=F32)

        table = table_ref[...] * inverse_area
        chosen = dot(left, table, ((1,), (0,))) * right_wide
        corr = dot(chosen, expand, ((1,), (1,)))
        corr_ref[...] = corr
        grad = weight_ref[...] * (corr - target_ref[...])
        grad_wide = dot(grad, expand, ((1,), (0,)))
        ahead = dot(left, grad_wide * right_wide, ((0,), (0,)))
        behind = dot(right, grad_wide * left_wide, ((0,), (0,)))
        for i in range(SCALES):
            at = slice(width * i, width * (i + 1))
            both = jnp.concatenate([ahead[:, at], behind[:, at]], axis=1)
            hi, lo = split2(both)
            a_ref[i, 0:BINS, :] = hi
            a_ref[i, BINS : 2 * BINS, :] = lo

    mix = a_ref[s]
    mask = window_mask(mask_ref)
    rows = []
    for x in range(ROWS):
        d = jnp.dot(mix, g_ref[0, x], preferred_element_type=F32)
        rows.append(jnp.where(mask != 0, d[:BINS] + d[BINS:], 0.0))
    tiles = banded(jnp.concatenate(rows, axis=0), wa_ref[0], OWN // LANE)
    at = pl.ds(pl.multiple_of(s * XB, XB), XB)
    for c, tile in enumerate(tiles):
        hi, lo = split2(tile)
        hi_ref[at, LANE * c : LANE * (c + 1)] = hi
        lo_ref[at, LANE * c : LANE * (c + 1)] = lo

    @pl.when(s == SCALES - 1)
    def _():
        out = (
            jnp.dot(ra_ref[0], hi_ref[...], preferred_element_type=F32)
            + jnp.dot(ra_ref[0], lo_ref[...], preferred_element_type=F32)
            + jnp.dot(ra_ref[1], hi_ref[...], preferred_element_type=F32)
        )
        up_ref[...] = out[0:XB]
        own_ref[...] = out[XB : 2 * XB]
        down_ref[...] = out[2 * XB : 3 * XB]


def struct(shape, dtype):
    return jax.ShapeDtypeStruct(shape, dtype)


LIMIT = pltpu.CompilerParams(vmem_limit_bytes=48 * 1024 * 1024)


def total_over(value, axis):
    count = lax.axis_size(axis)
    copies = jnp.broadcast_to(value[None], (count,) + value.shape)
    return jnp.sum(lax.all_to_all(copies, axis, 0, 0, tiled=True), axis=0)


def per_device(lensing_maps, filter_taps, survey_mask, bin_pairs, target_corr, pair_weight):
    strip = lensing_maps[0]
    rows, cols = strip.shape
    sky = lax.axis_size("sky")
    pairs = bin_pairs.shape[0]
    inverse_area = 1.0 / (rows * sky * cols)
    down_perm = [(i, i + 1) for i in range(sky - 1)]
    up_perm = [(i + 1, i) for i in range(sky - 1)]

    windows = pl.pallas_call(
        windows_kernel,
        out_shape=struct((XB, RAW), BF16),
        name="windows",
    )(strip)
    own = lax.all_to_all(windows, "bin", 0, 0, tiled=True)
    r, w, wa, ra = pl.pallas_call(
        matrices_kernel,
        in_specs=[SMEM],
        out_shape=(
            struct((SCALES, 2 * XB, 3 * XB), BF16),
            struct((SCALES, 2 * LANE, 2 * LANE), BF16),
            struct((SCALES, 2 * LANE, 2 * LANE), BF16),
            struct((2, 3 * XB, SCALES * XB), BF16),
        ),
        compiler_params=LIMIT,
        cost_estimate=pl.CostEstimate(flops=20_000_000, bytes_accessed=4_000_000, transcendentals=0),
        name="matrices",
    )(filter_taps)
    above = lax.ppermute(own, "sky", down_perm)
    below = lax.ppermute(own, "sky", up_perm)
    width = LAGS * BINS
    g, partial = pl.pallas_call(
        forward_kernel,
        grid=(SCALES,),
        in_specs=[
            SMEM,
            full((XB, RAW)),
            full((XB, RAW)),
            full((XB, RAW)),
            per_scale((2 * XB, 3 * XB)),
            per_scale((2 * LANE, 2 * LANE)),
        ],
        out_specs=[per_scale((ROWS, 2 * width, WIN)), full((BINS, SCALES * width))],
        out_shape=(
            struct((SCALES, ROWS, 2 * width, WIN), BF16),
            struct((BINS, SCALES * width), F32),
        ),
        scratch_shapes=[pltpu.VMEM((3 * XB, RAW), BF16)],
        compiler_params=LIMIT,
        name="forward",
    )(survey_mask, above, own, below, r, w)
    table = total_over(total_over(partial, "sky"), "bin")
    corr, up, mid, down = pl.pallas_call(
        lambda *refs: backward_kernel(inverse_area, *refs),
        grid=(SCALES,),
        in_specs=[
            SMEM,
            full((BINS, SCALES * width)),
            full((pairs, 2)),
            full((pairs, SCALES * LAGS)),
            full((pairs, SCALES * LAGS)),
            per_scale((ROWS, 2 * width, WIN)),
            per_scale((2 * LANE, 2 * LANE)),
            full((2, 3 * XB, SCALES * XB)),
        ],
        out_specs=[full((pairs, SCALES * LAGS))] + [full((XB, OWN))] * 3,
        out_shape=(struct((pairs, SCALES * LAGS), F32),) + (struct((XB, OWN), F32),) * 3,
        scratch_shapes=[
            pltpu.VMEM((SCALES, 2 * BINS, 2 * width), BF16),
            pltpu.VMEM((SCALES * XB, OWN), BF16),
            pltpu.VMEM((SCALES * XB, OWN), BF16),
        ],
        compiler_params=LIMIT,
        name="backward",
    )(
        survey_mask,
        table,
        bin_pairs,
        target_corr.reshape(pairs, SCALES * LAGS),
        pair_weight.reshape(pairs, SCALES * LAGS),
        g,
        wa,
        ra,
    )
    from_below = lax.ppermute(up, "sky", up_perm)
    from_above = lax.ppermute(down, "sky", down_perm)
    tile_grad = mid + from_below + from_above
    back = lax.all_to_all(tile_grad, "bin", 0, 0, tiled=True)
    map_grad = jnp.transpose(back.reshape(BINS, rows, OWN), (1, 0, 2)).reshape(1, rows, cols)
    return (corr.reshape(target_corr.shape), map_grad)


def solution(mesh):
    placed = (P("bin", "sky", None), P(), P("sky", None), P(), P(), P())
    return jax.shard_map(
        per_device,
        mesh=mesh,
        in_specs=placed,
        out_specs=(P(), P("bin", "sky", None)),
        check_vma=False,
    )
```

time: 570 us -> 115 us (0.20)
  waiting for transfers between devices: 262 us -> 26.3 us
  other arithmetic: 135 us -> 0.83 us
  blocking collectives: 74.1 us -> 33.5 us
  local copies, waits for them, and re-layouts: 42.4 us -> 6.05 us
  matrix products: 33.2 us -> 0 us
  Pallas kernels: 0 us -> 23.2 us
  starting transfers between devices: 16.4 us -> 22.3 us
    ppermute x19 -> x4, waiting for transfers between devices: 262 us -> 6.79 us  [the longest x1 5.33 us: per_device(): from_above = lax.ppermute(down, 'sky', down_perm)]
    psum x1 -> x0, blocking collectives: 74.1 us -> none  [per_device(): pair_table = lax.psum(tables, ('bin', 'sky'))]
    add x33 -> x0, other arithmetic: 49.8 us -> none  [the longest x15 35.8 us: reread(): return totals + partner_term(visitor, k)]
    all_to_all x0 -> x2, blocking collectives: none -> 33.5 us  [the longest x1 18.3 us: per_device(): own = lax.all_to_all(windows, 'bin', 0, 0, tiled=True)]
    dot_general x18 -> x0, matrix products: 33.2 us -> none  [the longest x16 31.5 us: take_block(): return jnp.einsum('i,j,ijsl->sl', row_hot, col_hot, table, precision=HIGH)]
    reduce_sum x62 -> x2, other arithmetic: 30.3 us -> 0.07 us  [total_over(): return jnp.sum(lax.all_to_all(copies, axis, 0, 0, tiled=True), axis=0)]
    mul x101 -> x0, other arithmetic: 26.6 us -> none  [the longest x48 24.7 us: adjoint_lags(): joint_mask[None] * widened[:, :, offset:]]
    convert_element_type x63 -> x0, other arithmetic: 25 us -> none  [the longest x15 17.9 us: adjoint_lags(): widened = partner.astype(jnp.float32)]
  transfers between devices with their start and end apart: 19 -> 6, of which waited for: 16 -> 4; matrix products, arithmetic and copies ran while one was open for 1% -> 3% of each run, Pallas kernels for 0% -> 4%
where the time goes in v1:
time: 115 us; the launch traced here: 113 us
  blocking collectives  33.5 us (29%)
  waiting for transfers between devices  26.3 us (23%)
  Pallas kernels  23.2 us (20%)
  starting transfers between devices  22.3 us (19%)
  local copies, waits for them, and re-layouts  6.05 us (5%)
    all_to_all x1, blocking collectives, per_device(): own = lax.all_to_all(windows, 'bin', 0, 0, tiled=True)  18.3 us
    all_to_all x1, blocking collectives, total_over(): return jnp.sum(lax.all_to_all(copies, axis, 0, 0, tiled=True), axis=0)  15.1 us
    all_to_all x1, waiting for transfers between devices, total_over(): return jnp.sum(lax.all_to_all(copies, axis, 0, 0, tiled=True), axis=0)  11 us
    pallas_call x1, Pallas kernels, per_device(): pl.pallas_call(lambda *refs: backward_kernel(inverse_area, *refs), grid=(...  8.68 us
    pallas_call x1, Pallas kernels, per_device(): pl.pallas_call(forward_kernel, grid=(SCALES,), in_specs=[SMEM, full((XB,...  8.58 us
    all_to_all x1, waiting for transfers between devices, per_device(): back = lax.all_to_all(tile_grad, 'bin', 0, 0, tiled=True)  8.5 us
    all_to_all x1, starting transfers between devices, per_device(): back = lax.all_to_all(tile_grad, 'bin', 0, 0, tiled=True)  6.11 us
    ppermute x1, waiting for transfers between devices, per_device(): from_above = lax.ppermute(down, 'sky', down_perm)  5.33 us
  transfers between devices with their start and end apart: 6, of which 4 were waited for; matrix products, arithmetic and copies ran while one was open for 3% of the time, Pallas kernels for 4%

profile of v1, /device:TPU:16, one launch (start us, length us, event | category | flops | bytes accessed | tf_op | source)
XLA Modules:
  0.0 112.8 jit_solution(12912105205193021868)
XLA Ops:
  0.6 0.0 copy-start.1
  0.6 1.6 %windows.1 = bf16[128,768]{1,0:T(8,128)(2,1)} custom-call(bf16[8,8192]{1,0:T(8,128)(2,1)} %bitcast.19), custom_call_target="tpu_custom_call" | custom-call | tf_op jit(solution)/shard_map/windows/pallas_call | solution.py:258
  2.2 18.3 %all_to_all.30 = bf16[16,8,768]{2,1,0:T(8,128)(2,1)S(1)} all-to-all(bf16[16,8,768]{2,1,0:T(8,128)(2,1)} %bitcast.18), channel_id=1, replica_groups=mesh['bin'=16,'sky'=16] {'bin'}, dimensions={0} | all-to-all | bytes 393216 | tf_op jit(solution)/shard_map/all_to_all | solution.py:263
  20.6 1.9 %collective-permute-start = (bf16[128,768]{1,0:T(8,128)(2,1)S(1)}, bf16[128,768]{1,0:T(8,128)(2,1)S(1)}, u32[]{:S(2)}, u32[]{:S(2)}) collective-permute-start(bf16[128,768]{1,0:T(8,128)(2,1)S(1)} %bitcast.14), channel_id=1, source_target_pairs={{0,1},{1,2},{2,3},{3,4},{4,5},{5,6},{6,7},{7,8},{8,9},{9,10},{10,1... | collective-permute-start | bytes 589832 | tf_op jit(solution)/shard_map/ppermute | solution.py:277
  22.5 5.1 %collective-permute-start.1 = (bf16[128,768]{1,0:T(8,128)(2,1)S(1)}, bf16[128,768]{1,0:T(8,128)(2,1)S(1)}, u32[]{:S(2)}, u32[]{:S(2)}) collective-permute-start(bf16[128,768]{1,0:T(8,128)(2,1)S(1)} %bitcast.15), channel_id=1, source_target_pairs={{1,0},{2,1},{3,2},{4,3},{5,4},{6,5},{7,6},{8,7},{9,8},{10,9},{11,1... | collective-permute-start | bytes 589832 | tf_op jit(solution)/shard_map/ppermute | solution.py:278
  27.7 0.0 copy-start.2
  27.7 0.7 copy-done.2
  28.4 4.3 %matrices.1 = (bf16[5,256,384]{2,1,0:T(8,128)(2,1)S(1)}, bf16[5,256,256]{2,1,0:T(8,128)(2,1)S(1)}, bf16[5,256,256]{2,1,0:T(8,128)(2,1)S(1)}, bf16[2,384,640]{2,1,0:T(8,128)(2,1)S(1)}) custom-call(f32[5,17]{1,0:T(8,128)S(1)} %copy-done.2), custom_call_target="tpu_custom_call" | custom-call | flops 20000000 | bytes 4000000 | tf_op jit(solution)/shard_map/matrices/pallas_call | solution.py:264
  32.7 0.0 collective-permute-done.up_ref
  32.7 0.0 collective-permute-done.1.down_ref
  32.7 0.0 copy-start
  32.7 0.6 copy-done
  33.4 8.6 %forward.1 = (bf16[5,8,128,640]{3,2,1,0:T(8,128)(2,1)}, f32[16,320]{1,0:T(8,128)S(1)}) custom-call(s32[1,64]{1,0:T(1,128)S(1)} %copy-done, bf16[128,768]{1,0:T(8,128)(2,1)S(1)} %collective-permute-done.up_ref, bf16[128,768]{1,0:T(8,128)(2,1)S(1)} %bitcast.16, bf16[128,768]{1,0:T(8,128)(2,1)S(1)} %collective-permute-done.1.down_ref, ...), custom_call_target="tpu_custom_call" | custom-call | tf_op jit(solution)/shard_map/forward/pallas_call | solution.py:280
  42.0 15.1 %all_to_all.31 = f32[16,16,320]{2,1,0:T(8,128)S(1)} all-to-all(f32[16,16,320]{2,1,0:T(8,128)S(1)} %broadcast_in_dim.4), channel_id=1, replica_groups=mesh['bin'=16,'sky'=16] {'sky'}, dimensions={0} | all-to-all | bytes 655360 | tf_op jit(solution)/shard_map/all_to_all | solution.py:246
  57.1 0.8 broadcast_in_dim.5
  57.9 4.8 %all-to-all-start.2 = ((f32[16,16,320]{2,1,0:T(8,128)}), f32[16,16,320]{2,1,0:T(8,128)S(1)}, u32[]{:S(2)}, u32[]{:S(2)}) async-start(f32[16,16,320]{2,1,0:T(8,128)} %broadcast_in_dim.5), calls=%async_computation.2 | async-start | bytes 786432 | tf_op jit(solution)/shard_map/all_to_all | solution.py:246
  62.7 0.7 reshape.24
  63.5 0.1 copy.17.refs_3_
  63.6 0.7 reshape.25
  64.3 0.1 copy.18.refs_4_
  64.4 0.8 copy.16.refs_2_
  65.2 11.0 %all-to-all-done.2 = f32[16,16,320]{2,1,0:T(8,128)S(1)} async-done(((f32[16,16,320]{2,1,0:T(8,128)}), f32[16,16,320]{2,1,0:T(8,128)S(1)}, u32[]{:S(2)}, u32[]{:S(2)}) %all-to-all-start.2) | async-done | bytes 327712 | tf_op jit(solution)/shard_map/all_to_all | solution.py:246
  76.2 0.0 copy-done.1
  76.2 8.7 %backward.1 = (f32[136,20]{1,0:T(8,128)S(1)}, f32[128,512]{1,0:T(8,128)S(1)}, f32[128,512]{1,0:T(8,128)S(1)}, f32[128,512]{1,0:T(8,128)S(1)}) custom-call(s32[1,64]{1,0:T(1,128)S(1)} %copy-done.1, f32[16,320]{1,0:T(8,128)S(1)} %reduce_sum.19.refs_1_, s32[136,2]{1,0:T(8,128)S(1)} %copy.16.refs_2_, f32[136,20]{1,0:T(8,128)S(1)} %copy.17.refs_3_, ...), custom_call_target="tpu_custom_call" | custom-call | tf_op jit(solution)/shard_map/backward/pallas_call | solution.py:301
  84.9 1.9 %collective-permute-start.2 = (f32[128,512]{1,0:T(8,128)S(1)}, f32[128,512]{1,0:T(8,128)S(1)}, u32[]{:S(2)}, u32[]{:S(2)}) collective-permute-start(f32[128,512]{1,0:T(8,128)S(1)} %get-tuple-element.20), channel_id=1, source_target_pairs={{1,0},{2,1},{3,2},{4,3},{5,4},{6,5},{7,6},{8,7},{9,8},{10,9},{11,1... | collective-permute-start | bytes 786440 | tf_op jit(solution)/shard_map/ppermute | solution.py:333
  86.8 2.4 %collective-permute-start.3 = (f32[128,512]{1,0:T(8,128)S(1)}, f32[128,512]{1,0:T(8,128)S(1)}, u32[]{:S(2)}, u32[]{:S(2)}) collective-permute-start(f32[128,512]{1,0:T(8,128)S(1)} %get-tuple-element.21), channel_id=1, source_target_pairs={{0,1},{1,2},{2,3},{3,4},{4,5},{5,6},{6,7},{7,8},{8,9},{9,10},{10,1... | collective-permute-start | bytes 786440 | tf_op jit(solution)/shard_map/ppermute | solution.py:334
  89.3 1.5 %collective-permute-done.2 = f32[128,512]{1,0:T(8,128)S(1)} collective-permute-done((f32[128,512]{1,0:T(8,128)S(1)}, f32[128,512]{1,0:T(8,128)S(1)}, u32[]{:S(2)}, u32[]{:S(2)}) %collective-permute-start.2) | collective-permute-done | bytes 262176 | tf_op jit(solution)/shard_map/ppermute | solution.py:333
  90.7 5.3 %collective-permute-done.3 = f32[128,512]{1,0:T(8,128)S(1)} collective-permute-done((f32[128,512]{1,0:T(8,128)S(1)}, f32[128,512]{1,0:T(8,128)S(1)}, u32[]{:S(2)}, u32[]{:S(2)}) %collective-permute-start.3) | collective-permute-done | bytes 262176 | tf_op jit(solution)/shard_map/ppermute | solution.py:334
  96.0 0.8 add_bitcast_fusion
  96.8 6.1 %all-to-all-start.3 = ((f32[16,8,512]{2,1,0:T(8,128)}), f32[16,8,512]{2,1,0:T(8,128)S(1)}, u32[]{:S(2)}, u32[]{:S(2)}) async-start(f32[16,8,512]{2,1,0:T(8,128)} %add_bitcast_fusion), calls=%async_computation.3 | async-start | bytes 524288 | tf_op jit(solution)/shard_map/all_to_all | solution.py:336
  102.9 0.1 copy.19
  103.0 0.6 reshape.26
  103.6 8.5 %all-to-all-done.3 = f32[16,8,512]{2,1,0:T(8,128)S(1)} async-done(((f32[16,8,512]{2,1,0:T(8,128)}), f32[16,8,512]{2,1,0:T(8,128)S(1)}, u32[]{:S(2)}, u32[]{:S(2)}) %all-to-all-start.3) | async-done | bytes 262176 | tf_op jit(solution)/shard_map/all_to_all | solution.py:336
  112.1 0.7 copy.21
  (3 shorter events, 0.1 us)
Async XLA Ops:
  0.6 75.6 %copy-start.1 = (s32[1,64]{1,0:T(1,128)S(1)}, s32[1,64]{1,0:T(1,128)}, u32[]{:S(2)}) copy-start(s32[1,64]{1,0:T(1,128)} %refs_0_.1) | copy-start | bytes 772
  20.6 12.1 %collective-permute-start = (bf16[128,768]{1,0:T(8,128)(2,1)S(1)}, bf16[128,768]{1,0:T(8,128)(2,1)S(1)}, u32[]{:S(2)}, u32[]{:S(2)}) collective-permute-start(bf16[128,768]{1,0:T(8,128)(2,1)S(1)} %bitcast.14), channel_id=1, source_target_pairs={{0,1},{1,2},{2,3},{3,4},{4,5},{5,6},{6,7},{7,8},{8,9},{9,10},{10,1... | collective-permute-start | bytes 589832 | tf_op jit(solution)/shard_map/ppermute | solution.py:277
  22.5 10.2 %collective-permute-start.1 = (bf16[128,768]{1,0:T(8,128)(2,1)S(1)}, bf16[128,768]{1,0:T(8,128)(2,1)S(1)}, u32[]{:S(2)}, u32[]{:S(2)}) collective-permute-start(bf16[128,768]{1,0:T(8,128)(2,1)S(1)} %bitcast.15), channel_id=1, source_target_pairs={{1,0},{2,1},{3,2},{4,3},{5,4},{6,5},{7,6},{8,7},{9,8},{10,9},{11,1... | collective-permute-start | bytes 589832 | tf_op jit(solution)/shard_map/ppermute | solution.py:278
  27.7 0.7 copy-start.2
  32.7 0.7 copy-start
  57.9 18.2 %all-to-all-start.2 = ((f32[16,16,320]{2,1,0:T(8,128)}), f32[16,16,320]{2,1,0:T(8,128)S(1)}, u32[]{:S(2)}, u32[]{:S(2)}) async-start(f32[16,16,320]{2,1,0:T(8,128)} %broadcast_in_dim.5), calls=%async_computation.2 | async-start | bytes 786432 | tf_op jit(solution)/shard_map/all_to_all | solution.py:246
  84.9 5.8 %collective-permute-start.2 = (f32[128,512]{1,0:T(8,128)S(1)}, f32[128,512]{1,0:T(8,128)S(1)}, u32[]{:S(2)}, u32[]{:S(2)}) collective-permute-start(f32[128,512]{1,0:T(8,128)S(1)} %get-tuple-element.20), channel_id=1, source_target_pairs={{1,0},{2,1},{3,2},{4,3},{5,4},{6,5},{7,6},{8,7},{9,8},{10,9},{11,1... | collective-permute-start | bytes 786440 | tf_op jit(solution)/shard_map/ppermute | solution.py:333
  86.8 9.2 %collective-permute-start.3 = (f32[128,512]{1,0:T(8,128)S(1)}, f32[128,512]{1,0:T(8,128)S(1)}, u32[]{:S(2)}, u32[]{:S(2)}) collective-permute-start(f32[128,512]{1,0:T(8,128)S(1)} %get-tuple-element.21), channel_id=1, source_target_pairs={{0,1},{1,2},{2,3},{3,4},{4,5},{5,6},{6,7},{7,8},{8,9},{9,10},{10,1... | collective-permute-start | bytes 786440 | tf_op jit(solution)/shard_map/ppermute | solution.py:334
  96.8 15.3 %all-to-all-start.3 = ((f32[16,8,512]{2,1,0:T(8,128)}), f32[16,8,512]{2,1,0:T(8,128)S(1)}, u32[]{:S(2)}, u32[]{:S(2)}) async-start(f32[16,8,512]{2,1,0:T(8,128)} %add_bitcast_fusion), calls=%async_computation.3 | async-start | bytes 524288 | tf_op jit(solution)/shard_map/all_to_all | solution.py:336

commit v2 on v1

v2 whole, which is shorter than its diff:
```python
import jax
import jax.numpy as jnp
from jax import lax
from jax.experimental import pallas as pl
from jax.experimental.pallas import tpu as pltpu
from jax.sharding import PartitionSpec as P

F32 = jnp.float32
BF16 = jnp.bfloat16
HIGH = lax.Precision.HIGHEST

BINS = 16
SCALES = 5
TAPS = 17
LAGS = 4
ROWS = 8
OWN = 512
LANE = 128
EDGE = 64
WIN = OWN + 2 * EDGE
RAW = OWN + 4 * EDGE
XB = ROWS * BINS
WIDE = LAGS * BINS
TABLE = SCALES * WIDE
ENTRIES = SCALES * LAGS
PAIRS = 144
GROUPS = PAIRS // 8
PACK = 384


def full(shape):
    return pl.BlockSpec(shape, lambda *_: (0,) * len(shape))


def per_scale(shape):
    return pl.BlockSpec((1,) + shape, lambda s: (s,) + (0,) * len(shape))


SMEM = pl.BlockSpec(memory_space=pltpu.SMEM)


def split2(v):
    hi = v.astype(BF16)
    return hi, (v - hi.astype(F32)).astype(BF16)


def iota(shape, dim):
    return lax.broadcasted_iota(jnp.int32, shape, dim)


def windows_kernel(x_ref, out_ref):
    x = x_ref[...].astype(F32)
    count = x.shape[1] // OWN
    blank = jnp.zeros((ROWS, LANE), F32)

    def window(b):
        parts = []
        if b == 0:
            parts.append(blank)
        low = max(b * OWN - LANE, 0)
        high = min((b + 1) * OWN + LANE, x.shape[1])
        parts.append(x[:, low:high])
        if b == count - 1:
            parts.append(blank)
        return jnp.concatenate(parts, axis=1) if len(parts) > 1 else parts[0]

    for p in range(count // 2):
        pair = jnp.concatenate([window(2 * p), window(2 * p + 1)], axis=0)
        out_ref[2 * ROWS * p : 2 * ROWS * (p + 1), :] = pair.astype(BF16)


def matrices_kernel(
    taps_ref, mask_ref, pairs_ref, r_ref, w_ref, wa_ref, ra_ref, window_ref, left_ref, right_ref
):
    window_ref[...] = jnp.broadcast_to(window_mask(mask_ref), window_ref.shape)
    for c, out_ref in enumerate((left_ref, right_ref)):
        bins = iota(out_ref.shape, 1) % BINS
        out_ref[...] = (pairs_ref[:, c : c + 1] == bins).astype(F32).astype(BF16)
    q = iota((XB, 3 * XB), 0)
    n = iota((XB, 3 * XB), 1)
    row_tap = jnp.where(q % BINS == (n % XB) // ROWS, n % ROWS - q // BINS + ROWS * (n // XB), -1)
    n = iota((2 * LANE, LANE), 0)
    o = iota((2 * LANE, LANE), 1)
    col_tap = n - o - 56
    col_adj_tap = o + 72 - n
    q = iota((3 * XB, XB), 0)
    n = iota((3 * XB, XB), 1)
    row_adj_tap = jnp.where(
        (q % XB) // ROWS == n % BINS, q % ROWS - n // BINS + ROWS * (q // XB), -1
    )

    def spread(index, s):
        value = jnp.zeros(index.shape, F32)
        for a in range(TAPS):
            value = jnp.where(index == a, taps_ref[s, a], value)
        return split2(value)

    def one(s, carry):
        hi, lo = spread(row_tap, s)
        at = pl.ds(pl.multiple_of(s * XB, XB), XB)
        r_ref[at, 0 : 3 * XB] = hi
        r_ref[at, 3 * XB : 6 * XB] = lo
        hi, lo = spread(col_tap, s)
        w_ref[s, :, 0:LANE] = hi
        w_ref[s, :, LANE : 2 * LANE] = lo
        hi, lo = spread(col_adj_tap, s)
        wa_ref[s, :, 0:LANE] = hi
        wa_ref[s, :, LANE : 2 * LANE] = lo
        hi, lo = spread(row_adj_tap, s)
        ra_ref[0, :, at] = hi
        ra_ref[1, :, at] = lo
        return carry

    lax.fori_loop(0, SCALES, one, 0)


def window_mask(mask_ref):
    b = lax.axis_index("bin")
    tiles = mask_ref.shape[1]
    lane = iota((1, LANE), 1)

    def tile(t):
        value = mask_ref[0, jnp.clip(t, 0, tiles - 1)]
        return jnp.where((t >= 0) & (t < tiles), value, 0)

    first = b * (OWN // LANE)
    parts = [
        jnp.where(lane < EDGE, tile(first + f - 1), tile(first + f)) for f in range(WIN // LANE)
    ]
    return jnp.concatenate(parts, axis=1)


def banded(v, w, tiles):
    parts = split2(v)
    stacked = jnp.concatenate(
        [p[:, LANE * f : LANE * (f + 2)] for p in parts for f in range(tiles)], axis=0
    )
    d = jnp.dot(stacked, w, preferred_element_type=F32)
    d = d[:, :LANE] + d[:, LANE:]
    return [d[XB * f : XB * (f + 1)] + d[XB * (tiles + f) : XB * (tiles + f + 1)] for f in range(tiles)]


def spread_matrix():
    return (iota((ENTRIES, TABLE), 1) // BINS == iota((ENTRIES, TABLE), 0)).astype(F32).astype(BF16)


def forward_kernel(
    window_ref, up_ref, own_ref, down_ref, r_ref, w_ref, left_ref, right_ref,
    g_ref, out_ref, raw_ref, pass_ref,
):
    for i, ref in enumerate((up_ref, own_ref, down_ref) * 2):
        raw_ref[XB * i : XB * (i + 1), :] = ref[...]
    pass_ref[...] = jnp.dot(r_ref[...], raw_ref[...], preferred_element_type=F32)
    mask = window_ref[0:1, :] != 0
    lane = iota((XB, WIN), 1)
    inner = (lane >= EDGE) & (lane < EDGE + OWN)
    slab = iota((BINS, ROWS * WIDE), 1) // WIDE
    parts = []
    for s in range(SCALES):
        tiles = banded(pass_ref[XB * s : XB * (s + 1), :], w_ref[s], WIN // LANE)
        filtered = jnp.concatenate(tiles, axis=1).astype(BF16).astype(F32)
        g = jnp.where(mask, filtered, 0.0)
        g_ref[s] = g.astype(BF16)
        left = jnp.where(inner, g, 0.0).astype(BF16)
        right = jnp.concatenate(
            [
                (pltpu.roll(g, WIN - l, 1) if l else g).astype(BF16).reshape(ROWS, BINS, WIN)
                for l in range(LAGS)
            ],
            axis=1,
        ).reshape(ROWS * WIDE, WIN)
        cross = lax.dot_general(left, right, (((1,), (1,)), ((), ())), preferred_element_type=F32)
        total = jnp.zeros((BINS, ROWS * WIDE), F32)
        for x in range(ROWS):
            total = jnp.where(slab == x, cross[BINS * x : BINS * (x + 1)], total)
        total = sum(total[:, LANE * i : LANE * (i + 1)] for i in range(ROWS * WIDE // LANE))
        parts.append(total[:, :WIDE] + total[:, WIDE:])
    table = jnp.concatenate(parts, axis=1)
    pieces = []
    for _ in range(3):
        piece = table.astype(BF16)
        table = table - piece.astype(F32)
        chosen = jnp.dot(left_ref[:, 0:BINS], piece, preferred_element_type=F32)
        pieces.append(chosen.astype(BF16) * right_ref[...])
    entries = lax.dot_general(
        jnp.concatenate(pieces, axis=0), spread_matrix(), (((1,), (1,)), ((), ())),
        preferred_element_type=F32,
    )
    entries = entries[0:PAIRS] + (entries[PAIRS : 2 * PAIRS] + entries[2 * PAIRS :])
    packed = jnp.concatenate(
        [entries[8 * a : 8 * (a + 1)] for a in range(GROUPS)]
        + [jnp.zeros((8, PACK - GROUPS * ENTRIES), F32)],
        axis=1,
    )
    out_ref[...] = jnp.broadcast_to(packed[None], out_ref.shape)


def shifts_kernel(g_ref, out_ref):
    g = g_ref[0].astype(F32)
    for l in range(LAGS):
        for side in range(2):
            steps = (WIN - l) % WIN if side == 0 else l
            moved = pltpu.roll(g, steps, 1) if steps else g
            at = (side * LAGS + l) * BINS
            out_ref[0, :, at : at + BINS, :] = moved.astype(BF16).reshape(ROWS, BINS, WIN)


def backward_kernel(
    inverse_area,
    window_ref, sums_ref, target_ref, weight_ref, left_ref, right_ref, g_ref, wa_ref, ra_ref,
    corr_ref, up_ref, own_ref, down_ref, hi_ref, lo_ref,
):
    packed = sums_ref[0]
    for i in range(1, sums_ref.shape[0]):
        packed = packed + sums_ref[i]
    corr = inverse_area * jnp.concatenate(
        [packed[:, ENTRIES * a : ENTRIES * (a + 1)] for a in range(GROUPS)], axis=0
    )
    corr_ref[...] = corr
    grad = weight_ref[...] * (corr - target_ref[...])
    spread = spread_matrix()
    halves = []
    for piece in split2(grad):
        wide = jnp.dot(piece, spread, preferred_element_type=F32).astype(BF16)
        both = []
        for one, other in ((left_ref, right_ref), (right_ref, left_ref)):
            both.append(
                lax.dot_general(
                    one[:, 0:BINS], wide * other[...], (((0,), (0,)), ((), ())),
                    preferred_element_type=F32,
                )
            )
        halves.append(both)

    mask = window_ref[0:1, :] != 0
    for s in range(SCALES):
        at = slice(WIDE * s, WIDE * (s + 1))
        mix = jnp.concatenate(
            [jnp.concatenate([ahead[:, at], behind[:, at]], axis=1) for ahead, behind in halves],
            axis=0,
        )
        zero = jnp.zeros_like(mix)
        mix = jnp.concatenate(
            [jnp.concatenate([mix, zero], axis=1), jnp.concatenate([zero, mix], axis=1)], axis=0
        ).astype(BF16)
        rows = []
        for x in range(0, ROWS, 2):
            maps = g_ref[s, x : x + 2].reshape(2 * 2 * WIDE, WIN)
            d = jnp.dot(mix, maps, preferred_element_type=F32)
            for i in (0, 2 * BINS):
                rows.append(jnp.where(mask, d[i : i + BINS] + d[i + BINS : i + 2 * BINS], 0.0))
        tiles = banded(jnp.concatenate(rows, axis=0), wa_ref[s], OWN // LANE)
        for c, tile in enumerate(tiles):
            hi, lo = split2(tile)
            hi_ref[XB * s : XB * (s + 1), LANE * c : LANE * (c + 1)] = hi
            lo_ref[XB * s : XB * (s + 1), LANE * c : LANE * (c + 1)] = lo
    for i, ref in enumerate((up_ref, own_ref, down_ref)):
        at = slice(XB * i, XB * (i + 1))
        ref[...] = (
            jnp.dot(ra_ref[0, at, :], hi_ref[...], preferred_element_type=F32)
            + jnp.dot(ra_ref[0, at, :], lo_ref[...], preferred_element_type=F32)
            + jnp.dot(ra_ref[1, at, :], hi_ref[...], preferred_element_type=F32)
        )


def struct(shape, dtype):
    return jax.ShapeDtypeStruct(shape, dtype)


LIMIT = pltpu.CompilerParams(vmem_limit_bytes=48 * 1024 * 1024)


def cost(flops, moved):
    return pl.CostEstimate(flops=flops, bytes_accessed=moved, transcendentals=0)


def matrices(filter_taps, survey_mask, bin_pairs):
    pairs = jnp.pad(bin_pairs, ((0, PAIRS - bin_pairs.shape[0]), (0, 0)), constant_values=-1)
    return pl.pallas_call(
        matrices_kernel,
        in_specs=[SMEM, SMEM, pl.BlockSpec(memory_space=pltpu.VMEM)],
        out_shape=(
            struct((SCALES * XB, 6 * XB), BF16),
            struct((SCALES, 2 * LANE, 2 * LANE), BF16),
            struct((SCALES, 2 * LANE, 2 * LANE), BF16),
            struct((2, 3 * XB, SCALES * XB), BF16),
            struct((8, WIN), jnp.int32),
            struct((PAIRS, TABLE), BF16),
            struct((PAIRS, TABLE), BF16),
        ),
        compiler_params=LIMIT,
        cost_estimate=cost(20_000_000, 4_000_000),
        name="matrices",
    )(filter_taps, survey_mask, pairs)


def forward(window, above, own, below, r, w, left, right, copies):
    return pl.pallas_call(
        forward_kernel,
        out_shape=(struct((SCALES, XB, WIN), BF16), struct((copies, 8, PACK), F32)),
        scratch_shapes=[pltpu.VMEM((6 * XB, RAW), BF16), pltpu.VMEM((SCALES * XB, RAW), F32)],
        compiler_params=LIMIT,
        name="forward",
    )(window, above, own, below, r, w, left, right)


def shifts(g):
    return pl.pallas_call(
        shifts_kernel,
        grid=(SCALES,),
        in_specs=[per_scale((XB, WIN))],
        out_specs=per_scale((ROWS, 2 * WIDE, WIN)),
        out_shape=struct((SCALES, ROWS, 2 * WIDE, WIN), BF16),
        compiler_params=LIMIT,
        cost_estimate=cost(10_000_000, 7_000_000),
        name="shifts",
    )(g)


def backward(inverse_area, window, sums, target, weight, left, right, g, wa, ra):
    return pl.pallas_call(
        lambda *refs: backward_kernel(inverse_area, *refs),
        out_shape=(struct((PAIRS, ENTRIES), F32),) + (struct((XB, OWN), F32),) * 3,
        scratch_shapes=[pltpu.VMEM((SCALES * XB, OWN), BF16), pltpu.VMEM((SCALES * XB, OWN), BF16)],
        compiler_params=LIMIT,
        name="backward",
    )(window, sums, target, weight, left, right, g, wa, ra)


def per_device(lensing_maps, filter_taps, survey_mask, bin_pairs, target_corr, pair_weight):
    strip = lensing_maps[0]
    rows, cols = strip.shape
    bins = lax.axis_size("bin")
    sky = lax.axis_size("sky")
    pairs = bin_pairs.shape[0]
    inverse_area = 1.0 / (rows * sky * cols)
    down_perm = [(i, i + 1) for i in range(sky - 1)]
    up_perm = [(i + 1, i) for i in range(sky - 1)]

    def padded(v):
        return jnp.pad(v.reshape(pairs, ENTRIES), ((0, PAIRS - pairs), (0, 0)))

    windows = pl.pallas_call(
        windows_kernel,
        out_shape=struct((XB, RAW), BF16),
        name="windows",
    )(strip)
    own = lax.all_to_all(windows, "bin", 0, 0, tiled=True)
    r, w, wa, ra, window, left, right = matrices(filter_taps, survey_mask, bin_pairs)
    above = lax.ppermute(own, "sky", down_perm)
    below = lax.ppermute(own, "sky", up_perm)
    g, partial = forward(window, above, own, below, r, w, left, right, sky)
    moved = shifts(g)
    partial = lax.all_to_all(partial, "sky", 0, 0, tiled=True)
    partial = jnp.broadcast_to(jnp.sum(partial, axis=0)[None], (bins,) + partial.shape[1:])
    partial = lax.all_to_all(partial, "bin", 0, 0, tiled=True)
    corr, up, mid, down = backward(
        inverse_area, window, partial, padded(target_corr), padded(pair_weight),
        left, right, moved, wa, ra,
    )
    from_below = lax.ppermute(up, "sky", up_perm)
    from_above = lax.ppermute(down, "sky", down_perm)
    tile_grad = mid + from_below + from_above
    back = lax.all_to_all(tile_grad, "bin", 0, 0, tiled=True)
    map_grad = jnp.transpose(back.reshape(bins, rows, OWN), (1, 0, 2)).reshape(1, rows, cols)
    return (corr[:pairs].reshape(target_corr.shape), map_grad)


def solution(mesh):
    placed = (P("bin", "sky", None), P(), P("sky", None), P(), P(), P())
    return jax.shard_map(
        per_device,
        mesh=mesh,
        in_specs=placed,
        out_specs=(P(), P("bin", "sky", None)),
        check_vma=False,
    )
```

time: 115 us -> 103 us (0.90)
  waiting for transfers between devices: 26.3 us -> 18.6 us
  starting transfers between devices: 22.3 us -> 20.8 us
    all_to_all x1, waiting for transfers between devices: 11 us -> 3.08 us  [per_device(): partial = lax.all_to_all(partial, 'bin', 0, 0, tiled=True)]
    ppermute x1, starting transfers between devices: 5.15 us -> 1.91 us  [per_device(): below = lax.ppermute(own, 'sky', up_perm)]
    pallas_call x3 -> x4, Pallas kernels: 21.6 us -> 20.6 us  [the longest x1 6.97 us: backward(): pl.pallas_call(lambda *refs: backward_kernel(inverse_area, *refs), out_sh...]
    unnamed x8 -> x6, local copies, waits for them, and re-layouts: 2.82 us -> 2.82 us
  transfers between devices with their start and end apart: 6 -> 6, of which waited for: 4 -> 4; matrix products, arithmetic and copies ran while one was open for 3% -> 3% of each run, Pallas kernels for 4% -> 9%
where the time goes in v2:
time: 103 us; the launch traced here: 102 us
  blocking collectives  32.5 us (32%)
  Pallas kernels  22.2 us (22%)
  starting transfers between devices  20.8 us (20%)
  waiting for transfers between devices  18.6 us (18%)
  local copies, waits for them, and re-layouts  5.96 us (6%)
    all_to_all x1, blocking collectives, per_device(): own = lax.all_to_all(windows, 'bin', 0, 0, tiled=True)  18.3 us
    all_to_all x1, blocking collectives, per_device(): partial = lax.all_to_all(partial, 'sky', 0, 0, tiled=True)  14.1 us
    all_to_all x1, waiting for transfers between devices, per_device(): back = lax.all_to_all(tile_grad, 'bin', 0, 0, tiled=True)  8.36 us
    pallas_call x1, Pallas kernels, backward(): pl.pallas_call(lambda *refs: backward_kernel(inverse_area, *refs), out_sh...  6.97 us
    all_to_all x1, starting transfers between devices, per_device(): back = lax.all_to_all(tile_grad, 'bin', 0, 0, tiled=True)  6.69 us
    ppermute x1, waiting for transfers between devices, per_device(): from_above = lax.ppermute(down, 'sky', down_perm)  5.69 us
    all_to_all x1, starting transfers between devices, per_device(): partial = lax.all_to_all(partial, 'bin', 0, 0, tiled=True)  5.48 us
    pallas_call x1, Pallas kernels, forward(): pl.pallas_call(forward_kernel, out_shape=(struct((SCALES, XB, WIN), BF16)...  4.84 us
  transfers between devices with their start and end apart: 6, of which 4 were waited for; matrix products, arithmetic and copies ran while one was open for 3% of the time, Pallas kernels for 9%

profile of v2, /device:TPU:16, one launch (start us, length us, event | category | flops | bytes accessed | tf_op | source)
XLA Modules:
  0.0 101.6 jit_solution(9969081092400650112)
XLA Ops:
  0.6 1.6 %windows.1 = bf16[128,768]{1,0:T(8,128)(2,1)} custom-call(bf16[8,8192]{1,0:T(8,128)(2,1)} %bitcast.19), custom_call_target="tpu_custom_call" | custom-call | tf_op jit(solution)/shard_map/windows/pallas_call | solution.py:343
  2.2 18.3 %all_to_all.30 = bf16[16,8,768]{2,1,0:T(8,128)(2,1)S(1)} all-to-all(bf16[16,8,768]{2,1,0:T(8,128)(2,1)} %bitcast.18), channel_id=1, replica_groups=mesh['bin'=16,'sky'=16] {'bin'}, dimensions={0} | all-to-all | bytes 393216 | tf_op jit(solution)/shard_map/all_to_all | solution.py:348
  20.6 1.9 %collective-permute-start.1 = (bf16[128,768]{1,0:T(8,128)(2,1)S(1)}, bf16[128,768]{1,0:T(8,128)(2,1)S(1)}, u32[]{:S(2)}, u32[]{:S(2)}) collective-permute-start(bf16[128,768]{1,0:T(8,128)(2,1)S(1)} %bitcast.14), channel_id=1, source_target_pairs={{1,0},{2,1},{3,2},{4,3},{5,4},{6,5},{7,6},{8,7},{9,8},{10,9},{11,1... | collective-permute-start | bytes 589832 | tf_op jit(solution)/shard_map/ppermute | solution.py:351
  22.5 2.4 %collective-permute-start = (bf16[128,768]{1,0:T(8,128)(2,1)S(1)}, bf16[128,768]{1,0:T(8,128)(2,1)S(1)}, u32[]{:S(2)}, u32[]{:S(2)}) collective-permute-start(bf16[128,768]{1,0:T(8,128)(2,1)S(1)} %bitcast.15), channel_id=1, source_target_pairs={{0,1},{1,2},{2,3},{3,4},{4,5},{5,6},{6,7},{7,8},{8,9},{9,10},{10,1... | collective-permute-start | bytes 589832 | tf_op jit(solution)/shard_map/ppermute | solution.py:350
  24.9 0.8 copy.12
  25.7 0.0 copy-start
  25.7 0.7 copy-done
  26.4 0.0 copy-start.1
  26.4 0.7 copy-done.1
  27.1 4.4 %matrices.1 = (bf16[640,768]{1,0:T(8,128)(2,1)S(1)}, bf16[5,256,256]{2,1,0:T(8,128)(2,1)S(1)}, bf16[5,256,256]{2,1,0:T(8,128)(2,1)S(1)}, bf16[2,384,640]{2,1,0:T...) custom-call(f32[5,17]{1,0:T(8,128)S(1)} %copy-done, ...), custom_call_target="tpu_custom_call" | custom-call | flops 20000000 | bytes 4000000 | tf_op jit(solution)/shard_map/matrices/pallas_call | solution.py:279
  31.4 0.0 collective-permute-done.1.down_ref
  31.5 0.0 collective-permute-done.up_ref
  31.5 4.8 %forward.1 = (bf16[5,128,640]{2,1,0:T(8,128)(2,1)S(1)}, f32[16,8,384]{2,1,0:T(8,128)S(1)}) custom-call(s32[8,640]{1,0:T(8,128)S(1)} %get-tuple-element.15.window_ref.refs_0_, bf16[128,768]{1,0:T(8,128)(2,1)S(1)} %collective-permute-done.up_ref, bf16[128,768]{1,0:T(8,128)(2,1)S(1)} %bitcast.16, bf16[128,768]{1,0:T(8,128)(2,1)S(1)} %collective-permute-done.1.down_ref, ...), custom_call_target="tpu_custom_call" | custom-call | tf_op jit(solution)/shard_map/forward/pallas_call | solution.py:298
  36.3 14.1 %all_to_all.31 = f32[16,8,384]{2,1,0:T(8,128)S(1)} all-to-all(f32[16,8,384]{2,1,0:T(8,128)S(1)} %get-tuple-element.20), channel_id=1, replica_groups=mesh['bin'=16,'sky'=16] {'sky'}, dimensions={0} | all-to-all | bytes 393216 | tf_op jit(solution)/shard_map/all_to_all | solution.py:354
  50.5 0.7 broadcast_in_dim.2
  51.2 5.5 %all-to-all-start.2 = ((f32[16,8,384]{2,1,0:T(8,128)}), f32[16,8,384]{2,1,0:T(8,128)S(1)}, u32[]{:S(2)}, u32[]{:S(2)}) async-start(f32[16,8,384]{2,1,0:T(8,128)} %broadcast_in_dim.2), calls=%async_computation.2 | async-start | bytes 393216 | tf_op jit(solution)/shard_map/all_to_all | solution.py:356
  56.7 0.7 reshape.23
  57.4 0.7 reshape.24
  58.1 0.1 copy.14
  58.3 0.1 copy.13
  58.4 4.4 %shifts.1.refs_6_ = bf16[5,8,128,640]{3,2,1,0:T(8,128)(2,1)} custom-call(bf16[5,128,640]{2,1,0:T(8,128)(2,1)S(1)} %get-tuple-element.21.g_ref), custom_call_target="tpu_custom_call" | custom-call | flops 10000000 | bytes 7000000 | tf_op jit(solution)/shard_map/shifts/pallas_call | solution.py:308
  62.8 3.1 %all-to-all-done.2.refs_1_ = f32[16,8,384]{2,1,0:T(8,128)S(1)} async-done(((f32[16,8,384]{2,1,0:T(8,128)}), f32[16,8,384]{2,1,0:T(8,128)S(1)}, u32[]{:S(2)}, u32[]{:S(2)}) %all-to-all-start.2) | async-done | bytes 196640 | tf_op jit(solution)/shard_map/all_to_all | solution.py:356
  65.8 7.0 %backward.1 = (f32[144,20]{1,0:T(8,128)S(1)}, f32[128,512]{1,0:T(8,128)S(1)}, f32[128,512]{1,0:T(8,128)S(1)}, f32[128,512]{1,0:T(8,128)S(1)}) custom-call(s32[8,640]{1,0:T(8,128)S(1)} %get-tuple-element.15.window_ref.refs_0_, f32[16,8,384]{2,1,0:T(8,128)S(1)} %all-to-all-done.2.refs_1_, f32[144,20]{1,0:T(8,128)S(1)} %pad.12.refs_2_, ...), custom_call_target="tpu_custom_call" | custom-call | tf_op jit(solution)/shard_map/backward/pallas_call | solution.py:321
  72.8 1.9 %collective-permute-start.2 = (f32[128,512]{1,0:T(8,128)S(1)}, f32[128,512]{1,0:T(8,128)S(1)}, u32[]{:S(2)}, u32[]{:S(2)}) collective-permute-start(f32[128,512]{1,0:T(8,128)S(1)} %get-tuple-element.26), channel_id=1, source_target_pairs={{1,0},{2,1},{3,2},{4,3},{5,4},{6,5},{7,6},{8,7},{9,8},{10,9},{11,1... | collective-permute-start | bytes 786440 | tf_op jit(solution)/shard_map/ppermute | solution.py:361
  74.8 2.4 %collective-permute-start.3 = (f32[128,512]{1,0:T(8,128)S(1)}, f32[128,512]{1,0:T(8,128)S(1)}, u32[]{:S(2)}, u32[]{:S(2)}) collective-permute-start(f32[128,512]{1,0:T(8,128)S(1)} %get-tuple-element.27), channel_id=1, source_target_pairs={{0,1},{1,2},{2,3},{3,4},{4,5},{5,6},{6,7},{7,8},{8,9},{9,10},{10,1... | collective-permute-start | bytes 786440 | tf_op jit(solution)/shard_map/ppermute | solution.py:362
  77.2 1.5 %collective-permute-done.2 = f32[128,512]{1,0:T(8,128)S(1)} collective-permute-done((f32[128,512]{1,0:T(8,128)S(1)}, f32[128,512]{1,0:T(8,128)S(1)}, u32[]{:S(2)}, u32[]{:S(2)}) %collective-permute-start.2) | collective-permute-done | bytes 262176 | tf_op jit(solution)/shard_map/ppermute | solution.py:361
  78.6 5.7 %collective-permute-done.3 = f32[128,512]{1,0:T(8,128)S(1)} collective-permute-done((f32[128,512]{1,0:T(8,128)S(1)}, f32[128,512]{1,0:T(8,128)S(1)}, u32[]{:S(2)}, u32[]{:S(2)}) %collective-permute-start.3) | collective-permute-done | bytes 262176 | tf_op jit(solution)/shard_map/ppermute | solution.py:362
  84.3 0.8 add_bitcast_fusion
  85.1 6.7 %all-to-all-start.3 = ((f32[16,8,512]{2,1,0:T(8,128)}), f32[16,8,512]{2,1,0:T(8,128)S(1)}, u32[]{:S(2)}, u32[]{:S(2)}) async-start(f32[16,8,512]{2,1,0:T(8,128)} %add_bitcast_fusion), calls=%async_computation.3 | async-start | bytes 524288 | tf_op jit(solution)/shard_map/all_to_all | solution.py:364
  91.8 0.1 copy.15
  91.9 0.6 reshape.25
  92.5 8.4 %all-to-all-done.3 = f32[16,8,512]{2,1,0:T(8,128)S(1)} async-done(((f32[16,8,512]{2,1,0:T(8,128)}), f32[16,8,512]{2,1,0:T(8,128)S(1)}, u32[]{:S(2)}, u32[]{:S(2)}) %all-to-all-start.3) | async-done | bytes 262176 | tf_op jit(solution)/shard_map/all_to_all | solution.py:364
  100.9 0.7 copy.17
  (5 shorter events, 0.1 us)
Async XLA Ops:
  20.6 10.9 %collective-permute-start.1 = (bf16[128,768]{1,0:T(8,128)(2,1)S(1)}, bf16[128,768]{1,0:T(8,128)(2,1)S(1)}, u32[]{:S(2)}, u32[]{:S(2)}) collective-permute-start(bf16[128,768]{1,0:T(8,128)(2,1)S(1)} %bitcast.14), channel_id=1, source_target_pairs={{1,0},{2,1},{3,2},{4,3},{5,4},{6,5},{7,6},{8,7},{9,8},{10,9},{11,1... | collective-permute-start | bytes 589832 | tf_op jit(solution)/shard_map/ppermute | solution.py:351
  22.5 9.0 %collective-permute-start = (bf16[128,768]{1,0:T(8,128)(2,1)S(1)}, bf16[128,768]{1,0:T(8,128)(2,1)S(1)}, u32[]{:S(2)}, u32[]{:S(2)}) collective-permute-start(bf16[128,768]{1,0:T(8,128)(2,1)S(1)} %bitcast.15), channel_id=1, source_target_pairs={{0,1},{1,2},{2,3},{3,4},{4,5},{5,6},{6,7},{7,8},{8,9},{9,10},{10,1... | collective-permute-start | bytes 589832 | tf_op jit(solution)/shard_map/ppermute | solution.py:350
  25.7 0.7 copy-start
  26.4 0.7 copy-start.1
  51.2 14.7 %all-to-all-start.2 = ((f32[16,8,384]{2,1,0:T(8,128)}), f32[16,8,384]{2,1,0:T(8,128)S(1)}, u32[]{:S(2)}, u32[]{:S(2)}) async-start(f32[16,8,384]{2,1,0:T(8,128)} %broadcast_in_dim.2), calls=%async_computation.2 | async-start | bytes 393216 | tf_op jit(solution)/shard_map/all_to_all | solution.py:356
  72.8 5.8 %collective-permute-start.2 = (f32[128,512]{1,0:T(8,128)S(1)}, f32[128,512]{1,0:T(8,128)S(1)}, u32[]{:S(2)}, u32[]{:S(2)}) collective-permute-start(f32[128,512]{1,0:T(8,128)S(1)} %get-tuple-element.26), channel_id=1, source_target_pairs={{1,0},{2,1},{3,2},{4,3},{5,4},{6,5},{7,6},{8,7},{9,8},{10,9},{11,1... | collective-permute-start | bytes 786440 | tf_op jit(solution)/shard_map/ppermute | solution.py:361
  74.8 9.6 %collective-permute-start.3 = (f32[128,512]{1,0:T(8,128)S(1)}, f32[128,512]{1,0:T(8,128)S(1)}, u32[]{:S(2)}, u32[]{:S(2)}) collective-permute-start(f32[128,512]{1,0:T(8,128)S(1)} %get-tuple-element.27), channel_id=1, source_target_pairs={{0,1},{1,2},{2,3},{3,4},{4,5},{5,6},{6,7},{7,8},{8,9},{9,10},{10,1... | collective-permute-start | bytes 786440 | tf_op jit(solution)/shard_map/ppermute | solution.py:362
  85.1 15.8 %all-to-all-start.3 = ((f32[16,8,512]{2,1,0:T(8,128)}), f32[16,8,512]{2,1,0:T(8,128)S(1)}, u32[]{:S(2)}, u32[]{:S(2)}) async-start(f32[16,8,512]{2,1,0:T(8,128)} %add_bitcast_fusion), calls=%async_computation.3 | async-start | bytes 524288 | tf_op jit(solution)/shard_map/all_to_all | solution.py:364

commit v3 on v2

v3 whole, which is shorter than its diff:
```python
import jax
import jax.numpy as jnp
from jax import lax
from jax.experimental import pallas as pl
from jax.experimental.pallas import tpu as pltpu
from jax.sharding import PartitionSpec as P

F32 = jnp.float32
BF16 = jnp.bfloat16
HIGH = lax.Precision.HIGHEST

BINS = 16
SCALES = 5
TAPS = 17
LAGS = 4
ROWS = 8
OWN = 512
LANE = 128
EDGE = 64
WIN = OWN + 2 * EDGE
XB = ROWS * BINS
WIDE = LAGS * BINS
TABLE = SCALES * WIDE
ENTRIES = SCALES * LAGS
PAIRS = 144
GROUPS = PAIRS // 8
PACK = 384


def full(shape):
    return pl.BlockSpec(shape, lambda *_: (0,) * len(shape))


def per_scale(shape):
    return pl.BlockSpec((1,) + shape, lambda s: (s,) + (0,) * len(shape))


SMEM = pl.BlockSpec(memory_space=pltpu.SMEM)


def split2(v):
    hi = v.astype(BF16)
    return hi, (v - hi.astype(F32)).astype(BF16)


def iota(shape, dim):
    return lax.broadcasted_iota(jnp.int32, shape, dim)


def windows_kernel(x_ref, out_ref):
    x = pltpu.roll(x_ref[...].astype(F32), EDGE, 1)
    count = x.shape[1] // OWN
    left = iota((ROWS, LANE), 1) < EDGE
    head = jnp.where(left, 0.0, x[:, :LANE])
    tail = jnp.where(left, x[:, :LANE], 0.0)

    def window(b):
        if b == 0:
            return jnp.concatenate([head, x[:, LANE:WIN]], axis=1)
        if b == count - 1:
            return jnp.concatenate([x[:, b * OWN :], tail], axis=1)
        return x[:, b * OWN : b * OWN + WIN]

    for p in range(count // 2):
        pair = jnp.concatenate([window(2 * p), window(2 * p + 1)], axis=0)
        out_ref[2 * ROWS * p : 2 * ROWS * (p + 1), :] = pair.astype(BF16)


def matrices_kernel(
    taps_ref, mask_ref, pairs_ref,
    row_ref, w_ref, wh_ref, wa_ref, row_adj_ref, window_ref, left_ref, right_ref,
):
    mask = jnp.broadcast_to(window_mask(mask_ref), (8, WIN))
    window_ref[0:8, :] = mask
    window_ref[8:16, :] = pltpu.roll(mask, WIN - EDGE, 1)
    for c, out_ref in enumerate((left_ref, right_ref)):
        bins = iota(out_ref.shape, 1) % BINS
        out_ref[...] = (pairs_ref[:, c : c + 1] == bins).astype(F32).astype(BF16)

    lane = iota((8, LANE), 1)
    n = iota((2 * LANE, LANE), 0)
    o = iota((2 * LANE, LANE), 1)
    k = o + 72 - n
    middle = (k >= 0) & (k < TAPS)
    k = jnp.where((o < EDGE) == (n >= LANE), jnp.where(o < EDGE, o + 200, o - 56) - n, -1)
    ends = (k >= 0) & (k < TAPS)

    def toeplitz(base, shift, valid):
        wide = jnp.broadcast_to(base[0:1], (2 * LANE, LANE))
        return jnp.where(valid, pltpu.roll(wide, shift, 1, stride=1, stride_axis=0), 0.0).astype(BF16)

    q = iota((ROWS, 3 * XB), 0)
    m = iota((ROWS, 3 * XB), 1)
    row_tap = m % ROWS - q + ROWS * (m // XB)
    q = iota((3 * ROWS, XB), 0)
    m = iota((3 * ROWS, XB), 1)
    row_adj_tap = q - m // BINS

    def one(s, carry):
        base = jnp.zeros((8, LANE), F32)
        flipped = jnp.zeros((8, LANE), F32)
        rows = jnp.zeros(row_tap.shape, F32)
        rows_adj = jnp.zeros(row_adj_tap.shape, F32)
        for a in range(TAPS):
            tap = taps_ref[s, a]
            base = jnp.where(lane == a, tap, base)
            flipped = jnp.where(lane == TAPS - 1 - a, tap, flipped)
            rows = jnp.where(row_tap == a, tap, rows)
            rows_adj = jnp.where(row_adj_tap == a, tap, rows_adj)
        for i in range(2):
            if i:
                base, flipped, rows, rows_adj = (
                    v - v.astype(BF16).astype(F32) for v in (base, flipped, rows, rows_adj)
                )
            base_i, flipped_i, rows_i, rows_adj_i = (
                v.astype(BF16).astype(F32) for v in (base, flipped, rows, rows_adj)
            )
            at = slice(LANE * i, LANE * (i + 1))
            w_ref[s, :, at] = toeplitz(flipped_i, LANE - 72, middle)
            wh_ref[s, :, at] = toeplitz(flipped_i, 56, ends)
            wa_ref[s, :, at] = toeplitz(base_i, LANE - 72, middle)
            row_ref[i, s] = rows_i
            row_adj_ref[i, s] = rows_adj_i
        return carry

    lax.fori_loop(0, SCALES, one, 0)


def window_mask(mask_ref):
    b = lax.axis_index("bin")
    tiles = mask_ref.shape[1]
    lane = iota((1, LANE), 1)

    def tile(t):
        value = mask_ref[0, jnp.clip(t, 0, tiles - 1)]
        return jnp.where((t >= 0) & (t < tiles), value, 0)

    first = b * (OWN // LANE)
    parts = [
        jnp.where(lane < EDGE, tile(first + f - 1), tile(first + f)) for f in range(WIN // LANE)
    ]
    return jnp.concatenate(parts, axis=1)


def banded(slabs, w):
    count = len(slabs)
    halves = [split2(slab) for slab in slabs]
    stacked = jnp.concatenate([h[i] for i in range(2) for h in halves], axis=0)
    d = jnp.dot(stacked, w, preferred_element_type=F32)
    d = d[:, :LANE] + d[:, LANE:]
    return [d[XB * f : XB * (f + 1)] + d[XB * (count + f) : XB * (count + f + 1)] for f in range(count)]


def spread_matrix():
    return (iota((ENTRIES, TABLE), 1) // BINS == iota((ENTRIES, TABLE), 0)).astype(F32).astype(BF16)


def forward_kernel(
    window_ref, up_ref, own_ref, down_ref, row_ref, w_ref, wh_ref, left_ref, right_ref,
    g_ref, out_ref, raw_ref, r_ref, pass_ref,
):

    for i, ref in enumerate((up_ref, own_ref, down_ref) * 2):
        raw_ref[XB * i : XB * (i + 1), :] = ref[...]
    own_bin = iota((BINS, 3 * XB), 0) == (iota((BINS, 3 * XB), 1) % XB) // ROWS
    for s in range(SCALES):
        for x in range(ROWS):
            for i in range(2):
                block = jnp.where(own_bin, row_ref[i, s, x : x + 1, :], 0.0).astype(BF16)
                at = XB * s + BINS * x
                r_ref[at : at + BINS, 3 * XB * i : 3 * XB * (i + 1)] = block
    pass_ref[...] = jnp.dot(r_ref[...], raw_ref[...], preferred_element_type=F32)
    mask = window_ref[8:9, :] != 0
    slab = iota((BINS, ROWS * WIDE), 1) // WIDE
    parts = []
    for s in range(SCALES):
        rows = pass_ref[XB * s : XB * (s + 1), :]
        tiles = banded([rows[:, LANE * f : LANE * (f + 2)] for f in range(OWN // LANE)], w_ref[s])
        tiles += banded([jnp.concatenate([rows[:, :LANE], rows[:, OWN:]], axis=1)], wh_ref[s])
        filtered = jnp.concatenate(tiles, axis=1).astype(BF16).astype(F32)
        g = jnp.where(mask, filtered, 0.0).astype(BF16)
        g_ref[s] = g
        left = g[:, :OWN]
        right = jnp.concatenate(
            [
                (pltpu.roll(g, WIN - l, 1) if l else g)[:, :OWN].reshape(ROWS, BINS, OWN)
                for l in range(LAGS)
            ],
            axis=1,
        ).reshape(ROWS * WIDE, OWN)
        cross = lax.dot_general(left, right, (((1,), (1,)), ((), ())), preferred_element_type=F32)
        total = jnp.zeros((BINS, ROWS * WIDE), F32)
        for x in range(ROWS):
            total = jnp.where(slab == x, cross[BINS * x : BINS * (x + 1)], total)
        total = sum(total[:, LANE * i : LANE * (i + 1)] for i in range(ROWS * WIDE // LANE))
        parts.append(total[:, :WIDE] + total[:, WIDE:])
    table = jnp.concatenate(parts, axis=1)
    pieces = []
    for _ in range(3):
        piece = table.astype(BF16)
        table = table - piece.astype(F32)
        chosen = jnp.dot(left_ref[:, 0:BINS], piece, preferred_element_type=F32)
        pieces.append(chosen.astype(BF16) * right_ref[...])
    entries = lax.dot_general(
        jnp.concatenate(pieces, axis=0), spread_matrix(), (((1,), (1,)), ((), ())),
        preferred_element_type=F32,
    )
    entries = entries[0:PAIRS] + (entries[PAIRS : 2 * PAIRS] + entries[2 * PAIRS :])
    packed = jnp.concatenate(
        [entries[8 * a : 8 * (a + 1)] for a in range(GROUPS)]
        + [jnp.zeros((8, PACK - GROUPS * ENTRIES), F32)],
        axis=1,
    )
    out_ref[...] = jnp.broadcast_to(packed[None], out_ref.shape)


def backward_kernel(
    inverse_area,
    window_ref, sums_ref, target_ref, weight_ref, left_ref, right_ref, wa_ref, row_adj_ref, g_ref,
    corr_ref, up_ref, own_ref, down_ref, hi_ref, lo_ref, ra_ref,
):
    same = iota((ROWS, XB), 1) % BINS
    for i in range(2):
        for s in range(SCALES):
            for d in range(3):
                part = row_adj_ref[i, s, ROWS * d : ROWS * (d + 1), :]
                for b in range(0, BINS, 2):
                    pair = [jnp.where(same == b + e, part, 0.0) for e in range(2)]
                    at = XB * d + ROWS * b
                    ra_ref[i, at : at + 2 * ROWS, XB * s : XB * (s + 1)] = jnp.concatenate(
                        pair, axis=0
                    ).astype(BF16)
    packed = sums_ref[0]
    for i in range(1, sums_ref.shape[0]):
        packed = packed + sums_ref[i]
    corr = inverse_area * jnp.concatenate(
        [packed[:, ENTRIES * a : ENTRIES * (a + 1)] for a in range(GROUPS)], axis=0
    )
    corr_ref[...] = corr
    grad = weight_ref[...] * (corr - target_ref[...])
    spread = spread_matrix()
    halves = []
    for piece in split2(grad):
        wide = jnp.dot(piece, spread, preferred_element_type=F32).astype(BF16)
        both = []
        for one, other in ((left_ref, right_ref), (right_ref, left_ref)):
            both.append(
                lax.dot_general(
                    one[:, 0:BINS], wide * other[...], (((0,), (0,)), ((), ())),
                    preferred_element_type=F32,
                )
            )
        halves.append(both)

    mask = window_ref[0:1, :] != 0
    for s in range(SCALES):
        at = slice(WIDE * s, WIDE * (s + 1))
        mix = jnp.concatenate(
            [jnp.concatenate([ahead[:, at], behind[:, at]], axis=1) for ahead, behind in halves],
            axis=0,
        )
        zero = jnp.zeros_like(mix)
        mix = jnp.concatenate(
            [jnp.concatenate([mix, zero], axis=1), jnp.concatenate([zero, mix], axis=1)], axis=0
        ).astype(BF16)
        rows = []
        g = g_ref[s]
        ahead = [pltpu.roll(g, EDGE - l, 1) for l in range(LAGS)]
        behind = ahead[:1] + [pltpu.roll(g, EDGE + l, 1) for l in range(1, LAGS)]
        for x in range(0, ROWS, 2):
            maps = jnp.concatenate(
                [v[BINS * y : BINS * (y + 1)] for y in (x, x + 1) for v in ahead + behind], axis=0
            )
            d = jnp.dot(mix, maps, preferred_element_type=F32)
            for i in (0, 2 * BINS):
                rows.append(jnp.where(mask, d[i : i + BINS] + d[i + BINS : i + 2 * BINS], 0.0))
        rows = jnp.concatenate(rows, axis=0)
        tiles = banded([rows[:, LANE * c : LANE * (c + 2)] for c in range(OWN // LANE)], wa_ref[s])
        for c, tile in enumerate(tiles):
            hi, lo = split2(tile)
            hi_ref[XB * s : XB * (s + 1), LANE * c : LANE * (c + 1)] = hi
            lo_ref[XB * s : XB * (s + 1), LANE * c : LANE * (c + 1)] = lo
    for i, ref in enumerate((up_ref, own_ref, down_ref)):
        at = slice(XB * i, XB * (i + 1))
        ref[...] = (
            jnp.dot(ra_ref[0, at, :], hi_ref[...], preferred_element_type=F32)
            + jnp.dot(ra_ref[0, at, :], lo_ref[...], preferred_element_type=F32)
            + jnp.dot(ra_ref[1, at, :], hi_ref[...], preferred_element_type=F32)
        )


def struct(shape, dtype):
    return jax.ShapeDtypeStruct(shape, dtype)


def limit(mib):
    return pltpu.CompilerParams(vmem_limit_bytes=mib * 1024 * 1024)


def cost(flops, moved):
    return pl.CostEstimate(flops=flops, bytes_accessed=moved, transcendentals=0)


def matrices(filter_taps, survey_mask, bin_pairs):
    pairs = jnp.pad(bin_pairs, ((0, PAIRS - bin_pairs.shape[0]), (0, 0)), constant_values=-1)
    column = struct((SCALES, 2 * LANE, 2 * LANE), BF16)
    return pl.pallas_call(
        matrices_kernel,
        in_specs=[SMEM, SMEM, VMEM],
        out_shape=(
            struct((2, SCALES, ROWS, 3 * XB), F32),
            column,
            column,
            column,
            struct((2, SCALES, 3 * ROWS, XB), F32),
            struct((16, WIN), jnp.int32),
            struct((PAIRS, TABLE), BF16),
            struct((PAIRS, TABLE), BF16),
        ),
        compiler_params=limit(32),
        cost_estimate=cost(20_000_000, 4_000_000),
        name="matrices",
    )(filter_taps, survey_mask, pairs)


VMEM = pl.BlockSpec(memory_space=pltpu.VMEM)


def forward(window, above, own, below, row, w, wh, left, right, copies):
    return pl.pallas_call(
        forward_kernel,
        out_shape=(struct((SCALES, XB, WIN), BF16), struct((copies, 8, PACK), F32)),
        scratch_shapes=[
            pltpu.VMEM((6 * XB, WIN), BF16),
            pltpu.VMEM((SCALES * XB, 6 * XB), BF16),
            pltpu.VMEM((SCALES * XB, WIN), F32),
        ],
        compiler_params=limit(32),
        name="forward",
    )(window, above, own, below, row, w, wh, left, right)


def backward(inverse_area, window, sums, target, weight, left, right, wa, row_adj, g):
    return pl.pallas_call(
        lambda *refs: backward_kernel(inverse_area, *refs),
        out_shape=(struct((PAIRS, ENTRIES), F32),) + (struct((XB, OWN), F32),) * 3,
        scratch_shapes=[
            pltpu.VMEM((SCALES * XB, OWN), BF16),
            pltpu.VMEM((SCALES * XB, OWN), BF16),
            pltpu.VMEM((2, 3 * XB, SCALES * XB), BF16),
        ],
        compiler_params=limit(32),
        name="backward",
    )(window, sums, target, weight, left, right, wa, row_adj, g)


def per_device(lensing_maps, filter_taps, survey_mask, bin_pairs, target_corr, pair_weight):
    strip = lensing_maps[0]
    rows, cols = strip.shape
    bins = lax.axis_size("bin")
    sky = lax.axis_size("sky")
    pairs = bin_pairs.shape[0]
    inverse_area = 1.0 / (rows * sky * cols)
    down_perm = [(i, i + 1) for i in range(sky - 1)]
    up_perm = [(i + 1, i) for i in range(sky - 1)]

    def padded(v):
        return jnp.pad(v.reshape(pairs, ENTRIES), ((0, PAIRS - pairs), (0, 0)))

    windows = pl.pallas_call(
        windows_kernel,
        out_shape=struct((XB, WIN), BF16),
        compiler_params=limit(8),
        name="windows",
    )(strip)
    own = lax.all_to_all(windows, "bin", 0, 0, tiled=True)
    made = matrices(filter_taps, survey_mask, bin_pairs)
    own, (row, w, wh, wa, row_adj, window, left, right) = lax.optimization_barrier((own, made))
    above = lax.ppermute(own, "sky", down_perm)
    below = lax.ppermute(own, "sky", up_perm)
    g, partial = forward(window, above, own, below, row, w, wh, left, right, sky)
    partial = lax.all_to_all(partial, "sky", 0, 0, tiled=True)
    partial = jnp.broadcast_to(jnp.sum(partial, axis=0)[None], (bins,) + partial.shape[1:])
    partial = lax.all_to_all(partial, "bin", 0, 0, tiled=True)
    corr, up, mid, down = backward(
        inverse_area, window, partial, padded(target_corr), padded(pair_weight),
        left, right, wa, row_adj, g,
    )
    from_below = lax.ppermute(up, "sky", up_perm)
    from_above = lax.ppermute(down, "sky", down_perm)
    tile_grad = mid + from_below + from_above
    back = lax.all_to_all(tile_grad, "bin", 0, 0, tiled=True)
    map_grad = jnp.transpose(back.reshape(bins, rows, OWN), (1, 0, 2)).reshape(1, rows, cols)
    return (corr[:pairs].reshape(target_corr.shape), map_grad)


def solution(mesh):
    placed = (P("bin", "sky", None), P(), P("sky", None), P(), P(), P())
    return jax.shard_map(
        per_device,
        mesh=mesh,
        in_specs=placed,
        out_specs=(P(), P("bin", "sky", None)),
        check_vma=False,
    )
```

time: 103 us -> 97.9 us (0.950)
  blocking collectives: 32.5 us -> 14.9 us
  waiting for transfers between devices: 18.6 us -> 32.9 us
  Pallas kernels: 22.2 us -> 11 us
  starting transfers between devices: 20.8 us -> 31.3 us
  local copies, waits for them, and re-layouts: 5.96 us -> 4.76 us
    all_to_all x1 -> x0, blocking collectives: 18.3 us -> none  [per_device(): own = lax.all_to_all(windows, 'bin', 0, 0, tiled=True)]
    all_to_all x0 -> x1, starting transfers between devices: none -> 9.42 us  [per_device(): own = lax.all_to_all(windows, 'bin', 0, 0, tiled=True)]
    pallas_call x3 -> x2, Pallas kernels: 10.3 us -> 2.34 us  [the longest x1 1.57 us: matrices(): pl.pallas_call(matrices_kernel, in_specs=[SMEM, SMEM, VMEM], out_shape=(s...]
    all_to_all x0 -> x1, waiting for transfers between devices: none -> 6.45 us  [per_device(): own = lax.all_to_all(windows, 'bin', 0, 0, tiled=True)]
    all_to_all x1, waiting for transfers between devices: 3.08 us -> 8.16 us  [per_device(): partial = lax.all_to_all(partial, 'bin', 0, 0, tiled=True)]
    ppermute x1, starting transfers between devices: 1.91 us -> 5.15 us  [per_device(): below = lax.ppermute(own, 'sky', up_perm)]
    pallas_call x1, Pallas kernels: 6.97 us -> 4.14 us  [backward(): pl.pallas_call(lambda *refs: backward_kernel(inverse_area, *refs), out_sh...]
    ppermute x1, waiting for transfers between devices: 0.01 us -> 1.76 us  [per_device(): below = lax.ppermute(own, 'sky', up_perm)]
  transfers between devices with their start and end apart: 6 -> 7, of which waited for: 4 -> 7; matrix products, arithmetic and copies ran while one was open for 3% -> 1% of each run, Pallas kernels for 9% -> 2%
where the time goes in v3:
time: 97.9 us; the launch traced here: 96.5 us
  waiting for transfers between devices  32.9 us (34%)
  starting transfers between devices  31.3 us (32%)
  blocking collectives  14.9 us (15%)
  Pallas kernels  11 us (11%)
  local copies, waits for them, and re-layouts  4.76 us (5%)
    all_to_all x1, blocking collectives, per_device(): partial = lax.all_to_all(partial, 'sky', 0, 0, tiled=True)  14.9 us
    all_to_all x1, starting transfers between devices, per_device(): own = lax.all_to_all(windows, 'bin', 0, 0, tiled=True)  9.42 us
    all_to_all x1, waiting for transfers between devices, per_device(): back = lax.all_to_all(tile_grad, 'bin', 0, 0, tiled=True)  8.36 us
    all_to_all x1, waiting for transfers between devices, per_device(): partial = lax.all_to_all(partial, 'bin', 0, 0, tiled=True)  8.16 us
    all_to_all x1, waiting for transfers between devices, per_device(): own = lax.all_to_all(windows, 'bin', 0, 0, tiled=True)  6.45 us
    all_to_all x1, starting transfers between devices, per_device(): back = lax.all_to_all(tile_grad, 'bin', 0, 0, tiled=True)  6.07 us
    ppermute x1, waiting for transfers between devices, per_device(): from_above = lax.ppermute(down, 'sky', down_perm)  5.62 us
    ppermute x1, starting transfers between devices, per_device(): below = lax.ppermute(own, 'sky', up_perm)  5.15 us
  transfers between devices with their start and end apart: 7, of which 7 were waited for; matrix products, arithmetic and copies ran while one was open for 1% of the time, Pallas kernels for 2%

profile of v3, /device:TPU:16, one launch (start us, length us, event | category | flops | bytes accessed | tf_op | source)
XLA Modules:
  0.0 96.5 jit_solution(8998408707862432866)
XLA Ops:
  0.6 0.0 copy-start
  0.6 0.9 copy-done
  1.5 0.8 windows.1
  2.3 0.0 copy-start.5
  2.3 9.4 %all-to-all-start = ((bf16[16,8,640]{2,1,0:T(8,128)(2,1)}), bf16[16,8,640]{2,1,0:T(8,128)(2,1)S(1)}, u32[]{:S(2)}, u32[]{:S(2)}) async-start(bf16[16,8,640]{2,1,0:T(8,128)(2,1)} %bitcast.1), calls=%async_computation | async-start | bytes 327680 | tf_op jit(solution)/shard_map/all_to_all | solution.py:376
  11.7 0.0 copy-done.5
  11.7 0.1 copy.12
  11.9 0.0 copy-start.1
  11.9 0.0 copy-start.2
  11.9 0.7 copy-done.1
  12.5 0.0 copy-done.2
  12.6 1.6 %matrices.1 = (f32[2,5,8,384]{3,2,1,0:T(8,128)S(1)}, bf16[5,256,256]{2,1,0:T(8,128)(2,1)S(1)}, bf16[5,256,256]{2,1,0:T(8,128)(2,1)S(1)}, bf16[5,256,256]{2,1,0:T...) custom-call(f32[5,17]{1,0:T(8,128)S(1)} %copy-done.1, ...), custom_call_target="tpu_custom_call" | custom-call | flops 20000000 | bytes 4000000 | tf_op jit(solution)/shard_map/matrices/pallas_call | solution.py:307
  14.1 6.4 %all-to-all-done = bf16[16,8,640]{2,1,0:T(8,128)(2,1)S(1)} async-done(((bf16[16,8,640]{2,1,0:T(8,128)(2,1)}), bf16[16,8,640]{2,1,0:T(8,128)(2,1)S(1)}, u32[]{:S(2)}, u32[]{:S(2)}) %all-to-all-start) | async-done | bytes 163872 | tf_op jit(solution)/shard_map/all_to_all | solution.py:376
  20.6 1.9 %collective-permute-start = (bf16[128,640]{1,0:T(8,128)(2,1)S(1)}, bf16[128,640]{1,0:T(8,128)(2,1)S(1)}, u32[]{:S(2)}, u32[]{:S(2)}) collective-permute-start(bf16[128,640]{1,0:T(8,128)(2,1)S(1)} %bitcast.14), channel_id=1, source_target_pairs={{0,1},{1,2},{2,3},{3,4},{4,5},{5,6},{6,7},{7,8},{8,9},{9,10},{10,1... | collective-permute-start | bytes 491528 | tf_op jit(solution)/shard_map/ppermute | solution.py:379
  22.5 5.1 %collective-permute-start.1 = (bf16[128,640]{1,0:T(8,128)(2,1)S(1)}, bf16[128,640]{1,0:T(8,128)(2,1)S(1)}, u32[]{:S(2)}, u32[]{:S(2)}) collective-permute-start(bf16[128,640]{1,0:T(8,128)(2,1)S(1)} %bitcast.15), channel_id=1, source_target_pairs={{1,0},{2,1},{3,2},{4,3},{5,4},{6,5},{7,6},{8,7},{9,8},{10,9},{11,1... | collective-permute-start | bytes 491528 | tf_op jit(solution)/shard_map/ppermute | solution.py:380
  27.6 1.1 %collective-permute-done.up_ref = bf16[128,640]{1,0:T(8,128)(2,1)S(1)} collective-permute-done((bf16[128,640]{1,0:T(8,128)(2,1)S(1)}, bf16[128,640]{1,0:T(8,128)(2,1)S(1)}, u32[]{:S(2)}, u32[]{:S(2)}) %collective-permute-start) | collective-permute-done | bytes 163872 | tf_op jit(solution)/shard_map/ppermute | solution.py:379
  28.7 1.8 %collective-permute-done.1.down_ref = bf16[128,640]{1,0:T(8,128)(2,1)S(1)} collective-permute-done((bf16[128,640]{1,0:T(8,128)(2,1)S(1)}, bf16[128,640]{1,0:T(8,128)(2,1)S(1)}, u32[]{:S(2)}, u32[]{:S(2)}) %collective-permute-start.1) | collective-permute-done | bytes 163872 | tf_op jit(solution)/shard_map/ppermute | solution.py:380
  30.5 4.5 %forward.1 = (bf16[5,128,640]{2,1,0:T(8,128)(2,1)S(1)}, f32[16,8,384]{2,1,0:T(8,128)S(1)}) custom-call(s32[16,640]{1,0:T(8,128)S(1)} %get-tuple-element.33.window_ref.refs_0_, bf16[128,640]{1,0:T(8,128)(2,1)S(1)} %collective-permute-done.up_ref, bf16[128,640]{1,0:T(8,128)(2,1)S(1)} %bitcast.16, bf16[128,640]{1,0:T(8,128)(2,1)S(1)} %collective-permute-done.1.down_ref, ...), custom_call_target="tpu_custom_call" | custom-call | tf_op jit(solution)/shard_map/forward/pallas_call | solution.py:330
  35.0 14.9 %all_to_all.31 = f32[16,8,384]{2,1,0:T(8,128)S(1)} all-to-all(f32[16,8,384]{2,1,0:T(8,128)S(1)} %get-tuple-element.40), channel_id=1, replica_groups=mesh['bin'=16,'sky'=16] {'sky'}, dimensions={0} | all-to-all | bytes 393216 | tf_op jit(solution)/shard_map/all_to_all | solution.py:382
  49.9 0.7 broadcast_in_dim.2
  50.6 0.0 copy-start.3
  50.6 4.4 %all-to-all-start.2 = ((f32[16,8,384]{2,1,0:T(8,128)}), f32[16,8,384]{2,1,0:T(8,128)S(1)}, u32[]{:S(2)}, u32[]{:S(2)}) async-start(f32[16,8,384]{2,1,0:T(8,128)} %broadcast_in_dim.2), calls=%async_computation.2 | async-start | bytes 393216 | tf_op jit(solution)/shard_map/all_to_all | solution.py:384
  55.1 0.0 copy-done.3
  55.1 0.1 copy.13
  55.2 0.0 copy-start.4
  55.2 0.7 copy-done.4
  55.9 0.1 copy.14
  56.1 8.2 %all-to-all-done.2.refs_1_ = f32[16,8,384]{2,1,0:T(8,128)S(1)} async-done(((f32[16,8,384]{2,1,0:T(8,128)}), f32[16,8,384]{2,1,0:T(8,128)S(1)}, u32[]{:S(2)}, u32[]{:S(2)}) %all-to-all-start.2) | async-done | bytes 196640 | tf_op jit(solution)/shard_map/all_to_all | solution.py:384
  64.2 4.1 %backward.1 = (f32[144,20]{1,0:T(8,128)S(1)}, f32[128,512]{1,0:T(8,128)S(1)}, f32[128,512]{1,0:T(8,128)S(1)}, f32[128,512]{1,0:T(8,128)S(1)}) custom-call(s32[16,640]{1,0:T(8,128)S(1)} %get-tuple-element.33.window_ref.refs_0_, f32[16,8,384]{2,1,0:T(8,128)S(1)} %all-to-all-done.2.refs_1_, f32[144,20]{1,0:T(8,128)S(1)} %pad.12.refs_2_, ...), custom_call_target="tpu_custom_call" | custom-call | tf_op jit(solution)/shard_map/backward/pallas_call | solution.py:344
  68.4 2.0 %collective-permute-start.2 = (f32[128,512]{1,0:T(8,128)S(1)}, f32[128,512]{1,0:T(8,128)S(1)}, u32[]{:S(2)}, u32[]{:S(2)}) collective-permute-start(f32[128,512]{1,0:T(8,128)S(1)} %get-tuple-element.46), channel_id=1, source_target_pairs={{1,0},{2,1},{3,2},{4,3},{5,4},{6,5},{7,6},{8,7},{9,8},{10,9},{11,1... | collective-permute-start | bytes 786440 | tf_op jit(solution)/shard_map/ppermute | solution.py:389
  70.4 2.3 %collective-permute-start.3 = (f32[128,512]{1,0:T(8,128)S(1)}, f32[128,512]{1,0:T(8,128)S(1)}, u32[]{:S(2)}, u32[]{:S(2)}) collective-permute-start(f32[128,512]{1,0:T(8,128)S(1)} %get-tuple-element.47), channel_id=1, source_target_pairs={{0,1},{1,2},{2,3},{3,4},{4,5},{5,6},{6,7},{7,8},{8,9},{9,10},{10,1... | collective-permute-start | bytes 786440 | tf_op jit(solution)/shard_map/ppermute | solution.py:390
  72.7 1.5 %collective-permute-done.2 = f32[128,512]{1,0:T(8,128)S(1)} collective-permute-done((f32[128,512]{1,0:T(8,128)S(1)}, f32[128,512]{1,0:T(8,128)S(1)}, u32[]{:S(2)}, u32[]{:S(2)}) %collective-permute-start.2) | collective-permute-done | bytes 262176 | tf_op jit(solution)/shard_map/ppermute | solution.py:389
  74.3 5.6 %collective-permute-done.3 = f32[128,512]{1,0:T(8,128)S(1)} collective-permute-done((f32[128,512]{1,0:T(8,128)S(1)}, f32[128,512]{1,0:T(8,128)S(1)}, u32[]{:S(2)}, u32[]{:S(2)}) %collective-permute-start.3) | collective-permute-done | bytes 262176 | tf_op jit(solution)/shard_map/ppermute | solution.py:390
  79.9 0.8 add_bitcast_fusion
  80.6 6.1 %all-to-all-start.3 = ((f32[16,8,512]{2,1,0:T(8,128)}), f32[16,8,512]{2,1,0:T(8,128)S(1)}, u32[]{:S(2)}, u32[]{:S(2)}) async-start(f32[16,8,512]{2,1,0:T(8,128)} %add_bitcast_fusion), calls=%async_computation.3 | async-start | bytes 524288 | tf_op jit(solution)/shard_map/all_to_all | solution.py:392
  86.7 0.1 copy.15
  86.8 0.6 reshape.25
  87.4 8.4 %all-to-all-done.3 = f32[16,8,512]{2,1,0:T(8,128)S(1)} async-done(((f32[16,8,512]{2,1,0:T(8,128)}), f32[16,8,512]{2,1,0:T(8,128)S(1)}, u32[]{:S(2)}, u32[]{:S(2)}) %all-to-all-start.3) | async-done | bytes 262176 | tf_op jit(solution)/shard_map/all_to_all | solution.py:392
  95.8 0.7 copy.17
  (7 shorter events, 0.1 us)
Async XLA Ops:
  0.6 0.9 copy-start
  2.3 9.4 %copy-start.5 = (s32[136,2]{0,1:T(2,128)S(1)}, s32[136,2]{0,1:T(2,128)}, u32[]{:S(2)}) copy-start(s32[136,2]{0,1:T(2,128)} %param.9) | copy-start | bytes 3268
  2.3 18.3 %all-to-all-start = ((bf16[16,8,640]{2,1,0:T(8,128)(2,1)}), bf16[16,8,640]{2,1,0:T(8,128)(2,1)S(1)}, u32[]{:S(2)}, u32[]{:S(2)}) async-start(bf16[16,8,640]{2,1,0:T(8,128)(2,1)} %bitcast.1), calls=%async_computation | async-start | bytes 327680 | tf_op jit(solution)/shard_map/all_to_all | solution.py:376
  11.9 0.7 copy-start.1
  11.9 0.7 copy-start.2
  20.6 8.1 %collective-permute-start = (bf16[128,640]{1,0:T(8,128)(2,1)S(1)}, bf16[128,640]{1,0:T(8,128)(2,1)S(1)}, u32[]{:S(2)}, u32[]{:S(2)}) collective-permute-start(bf16[128,640]{1,0:T(8,128)(2,1)S(1)} %bitcast.14), channel_id=1, source_target_pairs={{0,1},{1,2},{2,3},{3,4},{4,5},{5,6},{6,7},{7,8},{8,9},{9,10},{10,1... | collective-permute-start | bytes 491528 | tf_op jit(solution)/shard_map/ppermute | solution.py:379
  22.5 8.0 %collective-permute-start.1 = (bf16[128,640]{1,0:T(8,128)(2,1)S(1)}, bf16[128,640]{1,0:T(8,128)(2,1)S(1)}, u32[]{:S(2)}, u32[]{:S(2)}) collective-permute-start(bf16[128,640]{1,0:T(8,128)(2,1)S(1)} %bitcast.15), channel_id=1, source_target_pairs={{1,0},{2,1},{3,2},{4,3},{5,4},{6,5},{7,6},{8,7},{9,8},{10,9},{11,1... | collective-permute-start | bytes 491528 | tf_op jit(solution)/shard_map/ppermute | solution.py:380
  50.6 4.4 %copy-start.3 = (f32[136,5,4]{0,2,1:T(4,128)S(1)}, f32[136,5,4]{0,2,1:T(4,128)}, u32[]{:S(2)}) copy-start(f32[136,5,4]{0,2,1:T(4,128)} %param.10) | copy-start | bytes 32644
  50.6 13.6 %all-to-all-start.2 = ((f32[16,8,384]{2,1,0:T(8,128)}), f32[16,8,384]{2,1,0:T(8,128)S(1)}, u32[]{:S(2)}, u32[]{:S(2)}) async-start(f32[16,8,384]{2,1,0:T(8,128)} %broadcast_in_dim.2), calls=%async_computation.2 | async-start | bytes 393216 | tf_op jit(solution)/shard_map/all_to_all | solution.py:384
  55.2 0.7 copy-start.4
  68.4 5.9 %collective-permute-start.2 = (f32[128,512]{1,0:T(8,128)S(1)}, f32[128,512]{1,0:T(8,128)S(1)}, u32[]{:S(2)}, u32[]{:S(2)}) collective-permute-start(f32[128,512]{1,0:T(8,128)S(1)} %get-tuple-element.46), channel_id=1, source_target_pairs={{1,0},{2,1},{3,2},{4,3},{5,4},{6,5},{7,6},{8,7},{9,8},{10,9},{11,1... | collective-permute-start | bytes 786440 | tf_op jit(solution)/shard_map/ppermute | solution.py:389
  70.4 9.5 %collective-permute-start.3 = (f32[128,512]{1,0:T(8,128)S(1)}, f32[128,512]{1,0:T(8,128)S(1)}, u32[]{:S(2)}, u32[]{:S(2)}) collective-permute-start(f32[128,512]{1,0:T(8,128)S(1)} %get-tuple-element.47), channel_id=1, source_target_pairs={{0,1},{1,2},{2,3},{3,4},{4,5},{5,6},{6,7},{7,8},{8,9},{9,10},{10,1... | collective-permute-start | bytes 786440 | tf_op jit(solution)/shard_map/ppermute | solution.py:390
  80.6 15.2 %all-to-all-start.3 = ((f32[16,8,512]{2,1,0:T(8,128)}), f32[16,8,512]{2,1,0:T(8,128)S(1)}, u32[]{:S(2)}, u32[]{:S(2)}) async-start(f32[16,8,512]{2,1,0:T(8,128)} %add_bitcast_fusion), calls=%async_computation.3 | async-start | bytes 524288 | tf_op jit(solution)/shard_map/all_to_all | solution.py:392

commit v4 on v3

v4 whole, which is shorter than its diff:
```python
import jax
import jax.numpy as jnp
from jax import lax
from jax.experimental import pallas as pl
from jax.experimental.pallas import tpu as pltpu
from jax.sharding import PartitionSpec as P

F32 = jnp.float32
BF16 = jnp.bfloat16
HIGH = lax.Precision.HIGHEST

BINS = 16
SCALES = 5
TAPS = 17
LAGS = 4
ROWS = 8
OWN = 512
LANE = 128
EDGE = 64
WIN = OWN + 2 * EDGE
XB = ROWS * BINS
WIDE = LAGS * BINS
TABLE = SCALES * WIDE
ENTRIES = SCALES * LAGS
PAIRS = 144
GROUPS = PAIRS // 8
PACK = 384


def full(shape):
    return pl.BlockSpec(shape, lambda *_: (0,) * len(shape))


def per_scale(shape):
    return pl.BlockSpec((1,) + shape, lambda s: (s,) + (0,) * len(shape))


SMEM = pl.BlockSpec(memory_space=pltpu.SMEM)


def split2(v):
    hi = v.astype(BF16)
    return hi, (v - hi.astype(F32)).astype(BF16)


def iota(shape, dim):
    return lax.broadcasted_iota(jnp.int32, shape, dim)


def windows_kernel(x_ref, mask_ref, out_ref):
    tiles = mask_ref.shape[1]
    tiles = jnp.concatenate([mask_ref[...].astype(F32), jnp.zeros((1, LANE - tiles), F32)], axis=1)
    tiles = jnp.broadcast_to(tiles, (ROWS, LANE))
    corner = (iota((ROWS, LANE), 0) == 0) & (iota((ROWS, LANE), 1) <= WIN // LANE)
    x = pltpu.roll(x_ref[...].astype(F32), EDGE, 1)
    count = x.shape[1] // OWN
    left = iota((ROWS, LANE), 1) < EDGE
    head = jnp.where(left, 0.0, x[:, :LANE])
    tail = jnp.where(left, x[:, :LANE], 0.0)

    def window(b):
        first = head if b == 0 else x[:, b * OWN : b * OWN + LANE]
        first = jnp.where(corner, pltpu.roll(tiles, (1 - b * (OWN // LANE)) % LANE, 1), first)
        if b == count - 1:
            return jnp.concatenate([first, x[:, b * OWN + LANE :], tail], axis=1)
        return jnp.concatenate([first, x[:, b * OWN + LANE : b * OWN + WIN]], axis=1)

    for p in range(count // 2):
        pair = jnp.concatenate([window(2 * p), window(2 * p + 1)], axis=0)
        out_ref[2 * ROWS * p : 2 * ROWS * (p + 1), :] = pair.astype(BF16)


def matrices_kernel(
    taps_ref, pairs_ref, row_ref, w_ref, wh_ref, wa_ref, left_ref, right_ref, w_far, wh_far, sem,
):
    for c, out_ref in enumerate((left_ref, right_ref)):
        bins = iota(out_ref.shape, 1) % BINS
        out_ref[...] = (pairs_ref[:, c : c + 1] == bins).astype(F32).astype(BF16)

    lane = iota((8, LANE), 1)
    n = iota((2 * LANE, LANE), 0)
    o = iota((2 * LANE, LANE), 1)
    k = o + 72 - n
    middle = (k >= 0) & (k < TAPS)
    k = jnp.where((o < EDGE) == (n >= LANE), jnp.where(o < EDGE, o + 200, o - 56) - n, -1)
    ends = (k >= 0) & (k < TAPS)

    def toeplitz(base, shift, valid):
        wide = jnp.broadcast_to(base[0:1], (2 * LANE, LANE))
        return jnp.where(valid, pltpu.roll(wide, shift, 1, stride=1, stride_axis=0), 0.0).astype(BF16)

    q = iota((ROWS, 3 * XB), 0)
    m = iota((ROWS, 3 * XB), 1)
    row_tap = m % ROWS - q + ROWS * (m // XB)
    def one(s, carry):
        base = jnp.zeros((8, LANE), F32)
        flipped = jnp.zeros((8, LANE), F32)
        rows = jnp.zeros(row_tap.shape, F32)
        for a in range(TAPS):
            tap = taps_ref[s, a]
            base = jnp.where(lane == a, tap, base)
            flipped = jnp.where(lane == TAPS - 1 - a, tap, flipped)
            rows = jnp.where(row_tap == a, tap, rows)
        for i in range(2):
            if i:
                base, flipped, rows = (
                    v - v.astype(BF16).astype(F32) for v in (base, flipped, rows)
                )
            base_i, flipped_i, rows_i = (v.astype(BF16).astype(F32) for v in (base, flipped, rows))
            at = slice(LANE * i, LANE * (i + 1))
            w_ref[s, :, at] = toeplitz(flipped_i, LANE - 72, middle)
            wh_ref[s, :, at] = toeplitz(flipped_i, 56, ends)
            wa_ref[s, :, at] = toeplitz(base_i, LANE - 72, middle)
            row_ref[i, s] = rows_i
        return carry

    lax.fori_loop(0, SCALES, one, 0)
    copies = [
        pltpu.make_async_copy(near, far, sem.at[i])
        for i, (near, far) in enumerate(((w_ref, w_far), (wh_ref, wh_far)))
    ]
    for copy in copies:
        copy.start()
    for copy in copies:
        copy.wait()


def banded(slabs, w):
    count = len(slabs)
    halves = [split2(slab) for slab in slabs]
    stacked = jnp.concatenate([h[i] for i in range(2) for h in halves], axis=0)
    d = jnp.dot(stacked, w, preferred_element_type=F32)
    d = d[:, :LANE] + d[:, LANE:]
    return [d[XB * f : XB * (f + 1)] + d[XB * (count + f) : XB * (count + f + 1)] for f in range(count)]


def spread_matrix():
    return (iota((ENTRIES, TABLE), 1) // BINS == iota((ENTRIES, TABLE), 0)).astype(F32).astype(BF16)


def strip_mask(raw_ref):
    tiles = raw_ref[0:BINS, 0:LANE].astype(F32)[0:1]
    left = iota((1, LANE), 1) < EDGE
    return jnp.concatenate(
        [jnp.where(left, tiles[:, f : f + 1], tiles[:, f + 1 : f + 2]) for f in range(WIN // LANE)],
        axis=1,
    )


def filter_strip(strips, row_ref, w_ref, wh_ref, g_ref, raw_ref, r_ref, pass_ref, arrive=()):
    for copy in arrive:
        copy.start()
    for i, ref in enumerate(strips * 2):
        raw_ref[XB * i : XB * (i + 1), :] = ref[...]
    own_bin = iota((BINS, 3 * XB), 0) == (iota((BINS, 3 * XB), 1) % XB) // ROWS
    for s in range(SCALES):
        for x in range(ROWS):
            for i in range(2):
                block = jnp.where(own_bin, row_ref[i, s, x : x + 1, :], 0.0).astype(BF16)
                at = XB * s + BINS * x
                r_ref[at : at + BINS, 3 * XB * i : 3 * XB * (i + 1)] = block
    pass_ref[...] = jnp.dot(r_ref[...], raw_ref[...], preferred_element_type=F32)
    mask = jnp.broadcast_to(strip_mask(strips[1]), (BINS, WIN))
    g_ref[SCALES * XB :, :] = mask.astype(BF16)
    mask = pltpu.roll(mask, WIN - EDGE, 1)[0:1] != 0
    for copy in arrive:
        copy.wait()
    for s in range(SCALES):
        rows = pass_ref[XB * s : XB * (s + 1), :]
        tiles = banded([rows[:, LANE * f : LANE * (f + 2)] for f in range(OWN // LANE)], w_ref[s])
        tiles += banded([jnp.concatenate([rows[:, :LANE], rows[:, OWN:]], axis=1)], wh_ref[s])
        filtered = jnp.concatenate(tiles, axis=1).astype(BF16).astype(F32)
        g = jnp.where(mask, filtered, 0.0).astype(BF16)
        g_ref[XB * s : XB * (s + 1), :] = g
        yield g


def beside_kernel(
    first_ref, second_ref, third_ref, row_ref, w_far, wh_far, g_far,
    raw_ref, r_ref, pass_ref, w_ref, wh_ref, g_ref, sem,
):
    strips = (first_ref, second_ref, third_ref)
    arrive = [
        pltpu.make_async_copy(w_far, w_ref, sem.at[0]),
        pltpu.make_async_copy(wh_far, wh_ref, sem.at[1]),
    ]
    for _ in filter_strip(strips, row_ref, w_ref, wh_ref, g_ref, raw_ref, r_ref, pass_ref, arrive):
        pass
    leave = pltpu.make_async_copy(g_ref, g_far, sem.at[2])
    leave.start()
    leave.wait()


def forward_kernel(
    up_ref, own_ref, down_ref, row_ref, w_ref, wh_ref, left_ref, right_ref,
    g_ref, out_ref, raw_ref, r_ref, pass_ref,
):
    slab = iota((BINS, ROWS * WIDE), 1) // WIDE
    parts = []
    strips = (up_ref, own_ref, down_ref)
    for g in filter_strip(strips, row_ref, w_ref, wh_ref, g_ref, raw_ref, r_ref, pass_ref):
        left = g[:, :OWN]
        right = jnp.concatenate(
            [
                (pltpu.roll(g, WIN - l, 1) if l else g)[:, :OWN].reshape(ROWS, BINS, OWN)
                for l in range(LAGS)
            ],
            axis=1,
        ).reshape(ROWS * WIDE, OWN)
        cross = lax.dot_general(left, right, (((1,), (1,)), ((), ())), preferred_element_type=F32)
        total = jnp.zeros((BINS, ROWS * WIDE), F32)
        for x in range(ROWS):
            total = jnp.where(slab == x, cross[BINS * x : BINS * (x + 1)], total)
        total = sum(total[:, LANE * i : LANE * (i + 1)] for i in range(ROWS * WIDE // LANE))
        parts.append(total[:, :WIDE] + total[:, WIDE:])
    table = jnp.concatenate(parts, axis=1)
    pieces = []
    for _ in range(3):
        piece = table.astype(BF16)
        table = table - piece.astype(F32)
        chosen = jnp.dot(left_ref[:, 0:BINS], piece, preferred_element_type=F32)
        pieces.append(chosen.astype(BF16) * right_ref[...])
    entries = lax.dot_general(
        jnp.concatenate(pieces, axis=0), spread_matrix(), (((1,), (1,)), ((), ())),
        preferred_element_type=F32,
    )
    entries = entries[0:PAIRS] + (entries[PAIRS : 2 * PAIRS] + entries[2 * PAIRS :])
    packed = jnp.concatenate(
        [entries[8 * a : 8 * (a + 1)] for a in range(GROUPS)]
        + [jnp.zeros((8, PACK - GROUPS * ENTRIES), F32)],
        axis=1,
    )
    out_ref[...] = jnp.broadcast_to(packed[None], out_ref.shape)


def backward_kernel(
    inverse_area,
    taps_ref, sums_ref, target_ref, weight_ref, left_ref, right_ref, wa_ref, own_ref, up_far, down_far,
    corr_ref, out_ref, grad_ref, up_ref, down_ref, sem,
):
    copies = [
        pltpu.make_async_copy(up_far, up_ref, sem.at[0]),
        pltpu.make_async_copy(down_far, down_ref, sem.at[1]),
    ]
    for copy in copies:
        copy.start()
    packed = sums_ref[0]
    for i in range(1, sums_ref.shape[0]):
        packed = packed + sums_ref[i]
    corr = inverse_area * jnp.concatenate(
        [packed[:, ENTRIES * a : ENTRIES * (a + 1)] for a in range(GROUPS)], axis=0
    )
    corr_ref[...] = corr
    grad = weight_ref[...] * (corr - target_ref[...])
    spread = spread_matrix()
    halves = []
    for piece in split2(grad):
        wide = jnp.dot(piece, spread, preferred_element_type=F32).astype(BF16)
        both = []
        for one, other in ((left_ref, right_ref), (right_ref, left_ref)):
            both.append(
                lax.dot_general(
                    one[:, 0:BINS], wide * other[...], (((0,), (0,)), ((), ())),
                    preferred_element_type=F32,
                )
            )
        halves.append(both)

    def mask_of(ref):
        return ref[SCALES * XB :, :].astype(F32) != 0

    masks = [mask_of(own_ref)]
    totals = [jnp.zeros((XB, LANE), F32)] * (OWN // LANE)
    for s in range(SCALES):
        at = slice(WIDE * s, WIDE * (s + 1))
        mix = jnp.concatenate(
            [jnp.concatenate([ahead[:, at], behind[:, at]], axis=1) for ahead, behind in halves],
            axis=0,
        )
        zero = jnp.zeros_like(mix)
        mix = jnp.concatenate(
            [jnp.concatenate([mix, zero], axis=1), jnp.concatenate([zero, mix], axis=1)], axis=0
        ).astype(BF16)
        for n, (k, ref) in enumerate(((1, own_ref), (0, up_ref), (2, down_ref))):
            if s == 0 and n == 1:
                for copy in copies:
                    copy.wait()
                masks += [mask_of(up_ref), mask_of(down_ref)]
            mask = masks[n]
            g = ref[XB * s : XB * (s + 1), :]
            ahead = [pltpu.roll(g, EDGE - l, 1) for l in range(LAGS)]
            behind = ahead[:1] + [pltpu.roll(g, EDGE + l, 1) for l in range(1, LAGS)]
            for x in range(0, ROWS, 2):
                maps = jnp.concatenate(
                    [v[BINS * y : BINS * (y + 1)] for y in (x, x + 1) for v in ahead + behind], axis=0
                )
                d = jnp.dot(mix, maps, preferred_element_type=F32)
                for i in range(2):
                    v = d[2 * BINS * i : 2 * BINS * (i + 1)]
                    grad_ref[s % 2, ROWS * k + x + i] = jnp.where(mask, v[:BINS] + v[BINS:], 0.0)
        rows = []
        for x in range(ROWS):
            acc = taps_ref[s, TAPS - 1] * grad_ref[s % 2, x]
            for a in range(1, TAPS):
                acc = acc + taps_ref[s, TAPS - 1 - a] * grad_ref[s % 2, x + a]
            rows.append(acc)
        rows = jnp.concatenate(rows, axis=0)
        tiles = banded([rows[:, LANE * c : LANE * (c + 2)] for c in range(OWN // LANE)], wa_ref[s])
        totals = [total + tile for total, tile in zip(totals, tiles)]
    for c, total in enumerate(totals):
        for x in range(ROWS):
            at = pl.ds(ROWS * c + x, BINS, stride=ROWS * OWN // LANE)
            out_ref[at, :] = total[BINS * x : BINS * (x + 1)]


def struct(shape, dtype):
    return jax.ShapeDtypeStruct(shape, dtype)


VMEM = pl.BlockSpec(memory_space=pltpu.VMEM)
HBM = pl.BlockSpec(memory_space=pltpu.HBM)
COLUMN = (SCALES, 2 * LANE, 2 * LANE)
MAPS = (SCALES * XB + BINS, WIN)


def far(v):
    return pltpu.with_memory_space_constraint(v, pltpu.HBM)


def limit(mib):
    return pltpu.CompilerParams(vmem_limit_bytes=mib * 1024 * 1024)


def cost(flops, moved):
    return pl.CostEstimate(flops=flops, bytes_accessed=moved, transcendentals=0)


def matrices(filter_taps, bin_pairs):
    pairs = jnp.pad(bin_pairs, ((0, PAIRS - bin_pairs.shape[0]), (0, 0)), constant_values=-1)
    column = struct(COLUMN, BF16)
    return pl.pallas_call(
        matrices_kernel,
        in_specs=[SMEM, VMEM],
        out_shape=(
            struct((2, SCALES, ROWS, 3 * XB), F32),
            column,
            column,
            column,
            struct((PAIRS, TABLE), BF16),
            struct((PAIRS, TABLE), BF16),
            pltpu.HBM(COLUMN, BF16),
            pltpu.HBM(COLUMN, BF16),
        ),
        out_specs=[VMEM] * 6 + [HBM] * 2,
        scratch_shapes=[pltpu.SemaphoreType.DMA((2,))],
        compiler_params=limit(32),
        cost_estimate=cost(20_000_000, 4_000_000),
        name="matrices",
    )(filter_taps, pairs)


def scratch():
    return [
        pltpu.VMEM((6 * XB, WIN), BF16),
        pltpu.VMEM((SCALES * XB, 6 * XB), BF16),
        pltpu.VMEM((SCALES * XB, WIN), F32),
    ]


def forward(strips, row, w, wh, left, right, copies):
    return pl.pallas_call(
        forward_kernel,
        out_shape=(struct(MAPS, BF16), struct((copies, 8, PACK), F32)),
        scratch_shapes=scratch(),
        compiler_params=limit(32),
        name="forward",
    )(*strips, row, w, wh, left, right)


def beside(strips, row, w, wh):
    return pl.pallas_call(
        beside_kernel,
        in_specs=[VMEM] * 4 + [HBM] * 2,
        out_specs=HBM,
        out_shape=pltpu.HBM(MAPS, BF16),
        scratch_shapes=scratch()
        + [
            pltpu.VMEM(COLUMN, BF16),
            pltpu.VMEM(COLUMN, BF16),
            pltpu.VMEM(MAPS, BF16),
            pltpu.SemaphoreType.DMA((3,)),
        ],
        compiler_params=limit(32),
        cost_estimate=cost(2_000_000_000, 8_000_000),
        name="beside",
    )(*strips, row, far(w), far(wh))


def backward(inverse_area, taps, sums, target, weight, left, right, wa, above, own, below):
    return pl.pallas_call(
        lambda *refs: backward_kernel(inverse_area, *refs),
        in_specs=[SMEM] + [VMEM] * 7 + [HBM] * 2,
        out_shape=(struct((PAIRS, ENTRIES), F32), struct((XB * OWN // LANE, LANE), F32)),
        scratch_shapes=[
            pltpu.VMEM((2, 3 * ROWS, BINS, WIN), F32),
            pltpu.VMEM(MAPS, BF16),
            pltpu.VMEM(MAPS, BF16),
            pltpu.SemaphoreType.DMA((2,)),
        ],
        compiler_params=limit(32),
        name="backward",
    )(taps, sums, target, weight, left, right, wa, own, far(above), far(below))


def per_device(lensing_maps, filter_taps, survey_mask, bin_pairs, target_corr, pair_weight):
    strip = lensing_maps[0]
    rows, cols = strip.shape
    bins = lax.axis_size("bin")
    sky = lax.axis_size("sky")
    pairs = bin_pairs.shape[0]
    inverse_area = 1.0 / (rows * sky * cols)
    down_perm = [(i, i + 1) for i in range(sky - 1)]
    up_perm = [(i + 1, i) for i in range(sky - 1)]

    def padded(v):
        return jnp.pad(v.reshape(pairs, ENTRIES), ((0, PAIRS - pairs), (0, 0)))

    windows = pl.pallas_call(
        windows_kernel,
        out_shape=struct((XB, WIN), BF16),
        compiler_params=limit(8),
        name="windows",
    )(strip, survey_mask)
    own = lax.all_to_all(windows, "bin", 0, 0, tiled=True)
    made = matrices(filter_taps, bin_pairs)
    own, (row, w, wh, wa, left, right, w_far, wh_far) = lax.optimization_barrier((own, made))
    above = lax.ppermute(own, "sky", down_perm)
    below = lax.ppermute(own, "sky", up_perm)
    above2 = lax.ppermute(own, "sky", [(i, i + 2) for i in range(sky - 2)])
    below2 = lax.ppermute(own, "sky", [(i + 2, i) for i in range(sky - 2)])
    g, partial = forward((above, own, below), row, w, wh, left, right, sky)
    g_above = beside((above2, above, own), row, w_far, wh_far)
    g_below = beside((own, below, below2), row, w_far, wh_far)
    partial = lax.all_to_all(partial, "sky", 0, 0, tiled=True)
    partial = jnp.broadcast_to(jnp.sum(partial, axis=0)[None], (bins,) + partial.shape[1:])
    partial = lax.all_to_all(partial, "bin", 0, 0, tiled=True)
    corr, tile_grad = backward(
        inverse_area, filter_taps, partial, padded(target_corr), padded(pair_weight),
        left, right, wa, g_above, g, g_below,
    )
    back = lax.all_to_all(tile_grad, "bin", 0, 0, tiled=True)
    map_grad = jnp.transpose(back.reshape(cols // LANE, rows, LANE), (1, 0, 2)).reshape(1, rows, cols)
    return (corr[:pairs].reshape(target_corr.shape), map_grad)


def solution(mesh):
    placed = (P("bin", "sky", None), P(), P("sky", None), P(), P(), P())
    return jax.shard_map(
        per_device,
        mesh=mesh,
        in_specs=placed,
        out_specs=(P(), P("bin", "sky", None)),
        check_vma=False,
    )
```

time: 97.9 us -> 93.2 us (0.952)
  blocking collectives: 14.9 us -> 0 us
  Pallas kernels: 11 us -> 24.1 us
  waiting for transfers between devices: 32.9 us -> 21.5 us
  starting transfers between devices: 31.3 us -> 39.6 us
  local copies, waits for them, and re-layouts: 4.76 us -> 6.27 us
    all_to_all x1 -> x0, blocking collectives: 14.9 us -> none  [per_device(): partial = lax.all_to_all(partial, 'sky', 0, 0, tiled=True)]
    pallas_call x3 -> x5, Pallas kernels: 10.2 us -> 23.3 us  [the longest x1 8.76 us: backward(): pl.pallas_call(lambda *refs: backward_kernel(inverse_area, *refs), in_spe...]
    all_to_all x0 -> x1, starting transfers between devices: none -> 7.41 us  [per_device(): partial = lax.all_to_all(partial, 'sky', 0, 0, tiled=True)]
    ppermute x2, waiting for transfers between devices: 7.17 us -> 0.01 us  [the longest x1 0.01 us: per_device(): below2 = lax.ppermute(own, 'sky', [(i + 2, i) for i in range(sky - 2)])]
    all_to_all x1, waiting for transfers between devices: 8.16 us -> 2.1 us  [per_device(): partial = lax.all_to_all(partial, 'bin', 0, 0, tiled=True)]
    ppermute x1, waiting for transfers between devices: 1.06 us -> 5.32 us  [per_device(): above = lax.ppermute(own, 'sky', down_perm)]
    ppermute x2, starting transfers between devices: 4.33 us -> 8.25 us  [the longest x1 6.23 us: per_device(): above2 = lax.ppermute(own, 'sky', [(i, i + 2) for i in range(sky - 2)])]
    ppermute x1, starting transfers between devices: 5.15 us -> 1.91 us  [per_device(): below = lax.ppermute(own, 'sky', up_perm)]
  transfers between devices with their start and end apart: 7 -> 8, of which waited for: 7 -> 5; matrix products, arithmetic and copies ran while one was open for 1% -> 2% of each run, Pallas kernels for 2% -> 10%
where the time goes in v4:
time: 93.2 us; the launch traced here: 92.3 us
  starting transfers between devices  39.6 us (42%)
  Pallas kernels  24.1 us (26%)
  waiting for transfers between devices  21.5 us (23%)
  local copies, waits for them, and re-layouts  6.27 us (7%)
    all_to_all x1, starting transfers between devices, per_device(): own = lax.all_to_all(windows, 'bin', 0, 0, tiled=True)  9.42 us
    all_to_all x1, waiting for transfers between devices, per_device(): back = lax.all_to_all(tile_grad, 'bin', 0, 0, tiled=True)  8.85 us
    pallas_call x1, Pallas kernels, backward(): pl.pallas_call(lambda *refs: backward_kernel(inverse_area, *refs), in_spe...  8.76 us
    all_to_all x1, starting transfers between devices, per_device(): partial = lax.all_to_all(partial, 'sky', 0, 0, tiled=True)  7.41 us
    pallas_call x2, Pallas kernels, beside(): pl.pallas_call(beside_kernel, in_specs=[VMEM] * 4 + [HBM] * 2, out_specs=...  6.77 us
    ppermute x1, starting transfers between devices, per_device(): above2 = lax.ppermute(own, 'sky', [(i, i + 2) for i in range(sky - 2)])  6.23 us
    all_to_all x1, starting transfers between devices, per_device(): back = lax.all_to_all(tile_grad, 'bin', 0, 0, tiled=True)  6.03 us
    ppermute x1, waiting for transfers between devices, per_device(): above = lax.ppermute(own, 'sky', down_perm)  5.32 us
  transfers between devices with their start and end apart: 8, of which 5 were waited for; matrix products, arithmetic and copies ran while one was open for 2% of the time, Pallas kernels for 10%

profile of v4, /device:TPU:16, one launch (start us, length us, event | category | flops | bytes accessed | tf_op | source)
XLA Modules:
  0.0 92.3 jit_solution(7141599741437965778)
XLA Ops:
  0.6 0.0 copy-start.7
  0.6 0.6 copy-done.7
  1.3 0.0 copy-start.2
  1.3 0.9 copy-done.2
  2.2 0.8 windows.1
  3.0 0.0 copy-start.10
  3.0 9.4 %all-to-all-start = ((bf16[16,8,640]{2,1,0:T(8,128)(2,1)}), bf16[16,8,640]{2,1,0:T(8,128)(2,1)S(1)}, u32[]{:S(2)}, u32[]{:S(2)}) async-start(bf16[16,8,640]{2,1,0:T(8,128)(2,1)} %bitcast.1), calls=%async_computation | async-start | bytes 327680 | tf_op jit(solution)/shard_map/all_to_all | solution.py:434
  12.4 0.0 copy-done.10
  12.4 0.1 copy.12
  12.5 0.0 copy-start.6
  12.6 0.7 copy-done.6
  13.2 2.6 %matrices.1 = (f32[2,5,8,384]{3,2,1,0:T(8,128)S(1)}, bf16[5,256,256]{2,1,0:T(8,128)(2,1)S(1)}, bf16[5,256,256]{2,1,0:T(8,128)(2,1)S(1)}, bf16[5,256,256]{2,1,0:T...) custom-call(f32[5,17]{1,0:T(8,128)S(1)} %copy-done.6, ...), custom_call_target="tpu_custom_call" | custom-call | flops 20000000 | bytes 4000000 | tf_op jit(solution)/shard_map/matrices/pallas_call | solution.py:341
  15.8 0.0 copy-start.3
  15.8 0.6 copy-done.3
  16.4 4.8 %all-to-all-done = bf16[16,8,640]{2,1,0:T(8,128)(2,1)S(1)} async-done(((bf16[16,8,640]{2,1,0:T(8,128)(2,1)}), bf16[16,8,640]{2,1,0:T(8,128)(2,1)S(1)}, u32[]{:S(2)}, u32[]{:S(2)}) %all-to-all-start) | async-done | bytes 163872 | tf_op jit(solution)/shard_map/all_to_all | solution.py:434
  21.2 1.9 %collective-permute-start.1 = (bf16[128,640]{1,0:T(8,128)(2,1)S(1)}, bf16[128,640]{1,0:T(8,128)(2,1)S(1)}, u32[]{:S(2)}, u32[]{:S(2)}) collective-permute-start(bf16[128,640]{1,0:T(8,128)(2,1)S(1)} %bitcast.15), channel_id=1, source_target_pairs={{1,0},{2,1},{3,2},{4,3},{5,4},{6,5},{7,6},{8,7},{9,8},{10,9},{11,1... | collective-permute-start | bytes 491528 | tf_op jit(solution)/shard_map/ppermute | solution.py:438
  23.2 2.4 %collective-permute-start = (bf16[128,640]{1,0:T(8,128)(2,1)S(1)}, bf16[128,640]{1,0:T(8,128)(2,1)S(1)}, u32[]{:S(2)}, u32[]{:S(2)}) collective-permute-start(bf16[128,640]{1,0:T(8,128)(2,1)S(1)} %bitcast.16), channel_id=1, source_target_pairs={{0,1},{1,2},{2,3},{3,4},{4,5},{5,6},{6,7},{7,8},{8,9},{9,10},{10,1... | collective-permute-start | bytes 491528 | tf_op jit(solution)/shard_map/ppermute | solution.py:437
  25.6 0.4 collective-permute-done.1.down_ref.second_ref
  26.0 0.0 copy-start
  26.0 5.3 %collective-permute-done.up_ref.second_ref = bf16[128,640]{1,0:T(8,128)(2,1)S(1)} collective-permute-done((bf16[128,640]{1,0:T(8,128)(2,1)S(1)}, bf16[128,640]{1,0:T(8,128)(2,1)S(1)}, u32[]{:S(2)}, u32[]{:S(2)}) %collective-permute-start) | collective-permute-done | bytes 163872 | tf_op jit(solution)/shard_map/ppermute | solution.py:437
  31.3 0.0 copy-start.4
  31.3 0.9 copy-done.4
  32.2 5.2 %forward.1 = (bf16[656,640]{1,0:T(8,128)(2,1)S(1)}, f32[16,8,384]{2,1,0:T(8,128)}) custom-call(bf16[128,640]{1,0:T(8,128)(2,1)S(1)} %collective-permute-done.up_ref.second_ref, bf16[128,640]{1,0:T(8,128)(2,1)S(1)} %bitcast.17, bf16[128,640]{1,0:T(8,128)(2,1)S(1)} %collective-permute-done.1.down_ref.second_ref, f32[2,5,8,384]{3,2,1,0:T(8,128)S(1)} %copy-done.4, ...), custom_call_target="tpu_custom_call" | custom-call | tf_op jit(solution)/shard_map/forward/pallas_call | solution.py:371
  37.4 0.0 copy-done
  37.4 0.0 copy-start.8
  37.4 7.4 %all-to-all-start.1 = ((f32[16,8,384]{2,1,0:T(8,128)}), f32[16,8,384]{2,1,0:T(8,128)S(1)}, u32[]{:S(2)}, u32[]{:S(2)}) async-start(f32[16,8,384]{2,1,0:T(8,128)} %get-tuple-element.37), calls=%async_computation.1 | async-start | bytes 393216 | tf_op jit(solution)/shard_map/all_to_all | solution.py:444
  44.8 0.0 copy-start.9
  44.8 2.0 %collective-permute-start.3 = (bf16[128,640]{1,0:T(8,128)(2,1)S(1)}, bf16[128,640]{1,0:T(8,128)(2,1)S(1)}, u32[]{:S(2)}, u32[]{:S(2)}) collective-permute-start(bf16[128,640]{1,0:T(8,128)(2,1)S(1)} %bitcast.18), channel_id=1, source_target_pairs={{2,0},{3,1},{4,2},{5,3},{6,4},{7,5},{8,6},{9,7},{10,8},{11,9},{12,... | collective-permute-start | bytes 491528 | tf_op jit(solution)/shard_map/ppermute | solution.py:440
  46.9 0.0 copy-done.8
  46.9 0.0 copy-done.9
  46.9 0.1 copy.14
  47.0 0.1 copy.13
  47.2 6.2 %collective-permute-start.2 = (bf16[128,640]{1,0:T(8,128)(2,1)S(1)}, bf16[128,640]{1,0:T(8,128)(2,1)S(1)}, u32[]{:S(2)}, u32[]{:S(2)}) collective-permute-start(bf16[128,640]{1,0:T(8,128)(2,1)S(1)} %bitcast.19), channel_id=1, source_target_pairs={{0,2},{1,3},{2,4},{3,5},{4,6},{5,7},{6,8},{7,9},{8,10},{9,11},{10,... | collective-permute-start | bytes 491528 | tf_op jit(solution)/shard_map/ppermute | solution.py:439
  53.4 0.0 all-to-all-done.1
  53.5 0.7 broadcast_in_dim.2
  54.1 0.0 copy-start.1
  54.2 0.0 copy-start.5
  54.2 4.2 %all-to-all-start.2 = ((f32[16,8,384]{2,1,0:T(8,128)}), f32[16,8,384]{2,1,0:T(8,128)S(1)}, u32[]{:S(2)}, u32[]{:S(2)}) async-start(f32[16,8,384]{2,1,0:T(8,128)} %broadcast_in_dim.2), calls=%async_computation.2 | async-start | bytes 393216 | tf_op jit(solution)/shard_map/all_to_all | solution.py:446
  58.3 0.0 collective-permute-done.3.third_ref
  58.3 0.0 copy-done.1
  58.4 0.0 copy-done.5
  58.4 3.4 %beside.3.refs_9_ = bf16[656,640]{1,0:T(8,128)(2,1)} custom-call(bf16[128,640]{1,0:T(8,128)(2,1)S(1)} %bitcast.20, bf16[128,640]{1,0:T(8,128)(2,1)S(1)} %copy-done.1, bf16[128,640]{1,0:T(8,128)(2,1)S(1)} %collective-permute-done.3.third_ref, f32[2,5,8,384]{3,2,1,0:T(8,128)S(1)} %copy-done.5, bf16[5,256,256]{2,1,0:T(8,128)(2,1)} %get-tuple-element.40.w_far, ...), custom_call_target="tpu_custom_call" | custom-call | flops 2000000000 | bytes 8000000 | tf_op jit(solution)/shard_map/beside/pallas_call | solution.py:381
  61.8 0.0 collective-permute-done.2.first_ref
  61.8 3.4 %beside.2.refs_8_ = bf16[656,640]{1,0:T(8,128)(2,1)} custom-call(bf16[128,640]{1,0:T(8,128)(2,1)S(1)} %collective-permute-done.2.first_ref, bf16[128,640]{1,0:T(8,128)(2,1)S(1)} %collective-permute-done.up_ref.second_ref, bf16[128,640]{1,0:T(8,128)(2,1)S(1)} %bitcast.21, f32[2,5,8,384]{3,2,1,0:T(8,128)S(1)} %copy-done.5, ...), custom_call_target="tpu_custom_call" | custom-call | flops 2000000000 | bytes 8000000 | tf_op jit(solution)/shard_map/beside/pallas_call | solution.py:381
  65.2 2.1 %all-to-all-done.2.refs_1_ = f32[16,8,384]{2,1,0:T(8,128)S(1)} async-done(((f32[16,8,384]{2,1,0:T(8,128)}), f32[16,8,384]{2,1,0:T(8,128)S(1)}, u32[]{:S(2)}, u32[]{:S(2)}) %all-to-all-start.2) | async-done | bytes 196640 | tf_op jit(solution)/shard_map/all_to_all | solution.py:446
  67.3 8.8 %backward.1 = (f32[144,20]{1,0:T(8,128)S(1)}, f32[512,128]{1,0:T(8,128)}) custom-call(f32[5,17]{1,0:T(8,128)S(1)} %copy-done.6, f32[16,8,384]{2,1,0:T(8,128)S(1)} %all-to-all-done.2.refs_1_, f32[144,20]{1,0:T(8,128)S(1)} %pad.12.refs_2_, f32[144,20]{1,0:T(8,128)S(1)} %pad.13.refs_3_, bf16[144,320]{1,0:T(8,128)(2,1)S(1)} %get-tuple-element.35.left_ref.refs_4_, ...), custom_call_target="tpu_custom_call" | custom-call | tf_op jit(solution)/shard_map/backward/pallas_call | solution.py:400
  76.0 6.0 %all-to-all-start.3 = ((f32[16,32,128]{2,1,0:T(8,128)}), f32[16,32,128]{2,1,0:T(8,128)S(1)}, u32[]{:S(2)}, u32[]{:S(2)}) async-start(f32[16,32,128]{2,1,0:T(8,128)} %bitcast.3), calls=%async_computation.3 | async-start | bytes 524288 | tf_op jit(solution)/shard_map/all_to_all | solution.py:451
  82.1 0.1 copy.15
  82.2 0.6 reshape.27
  82.8 8.9 %all-to-all-done.3 = f32[16,32,128]{2,1,0:T(8,128)S(1)} async-done(((f32[16,32,128]{2,1,0:T(8,128)}), f32[16,32,128]{2,1,0:T(8,128)S(1)}, u32[]{:S(2)}, u32[]{:S(2)}) %all-to-all-start.3) | async-done | bytes 262176 | tf_op jit(solution)/shard_map/all_to_all | solution.py:451
  91.6 0.7 copy.17
  (7 shorter events, 0.1 us)
Async XLA Ops:
  0.6 0.7 copy-start.7
  1.3 0.9 copy-start.2
  3.0 9.4 %copy-start.10 = (s32[136,2]{0,1:T(2,128)S(1)}, s32[136,2]{0,1:T(2,128)}, u32[]{:S(2)}) copy-start(s32[136,2]{0,1:T(2,128)} %param.9) | copy-start | bytes 3268
  3.0 18.3 %all-to-all-start = ((bf16[16,8,640]{2,1,0:T(8,128)(2,1)}), bf16[16,8,640]{2,1,0:T(8,128)(2,1)S(1)}, u32[]{:S(2)}, u32[]{:S(2)}) async-start(bf16[16,8,640]{2,1,0:T(8,128)(2,1)} %bitcast.1), calls=%async_computation | async-start | bytes 327680 | tf_op jit(solution)/shard_map/all_to_all | solution.py:434
  12.5 0.7 copy-start.6
  15.8 0.7 copy-start.3
  21.2 4.7 %collective-permute-start.1 = (bf16[128,640]{1,0:T(8,128)(2,1)S(1)}, bf16[128,640]{1,0:T(8,128)(2,1)S(1)}, u32[]{:S(2)}, u32[]{:S(2)}) collective-permute-start(bf16[128,640]{1,0:T(8,128)(2,1)S(1)} %bitcast.15), channel_id=1, source_target_pairs={{1,0},{2,1},{3,2},{4,3},{5,4},{6,5},{7,6},{8,7},{9,8},{10,9},{11,1... | collective-permute-start | bytes 491528 | tf_op jit(solution)/shard_map/ppermute | solution.py:438
  23.2 8.1 %collective-permute-start = (bf16[128,640]{1,0:T(8,128)(2,1)S(1)}, bf16[128,640]{1,0:T(8,128)(2,1)S(1)}, u32[]{:S(2)}, u32[]{:S(2)}) collective-permute-start(bf16[128,640]{1,0:T(8,128)(2,1)S(1)} %bitcast.16), channel_id=1, source_target_pairs={{0,1},{1,2},{2,3},{3,4},{4,5},{5,6},{6,7},{7,8},{8,9},{9,10},{10,1... | collective-permute-start | bytes 491528 | tf_op jit(solution)/shard_map/ppermute | solution.py:437
  26.0 11.4 %copy-start = (bf16[128,640]{1,0:T(8,128)(2,1)}, bf16[128,640]{1,0:T(8,128)(2,1)S(1)}, u32[]{:S(2)}) copy-start(bf16[128,640]{1,0:T(8,128)(2,1)S(1)} %collective-permute-done.1.down_ref.second_ref) | copy-start | bytes 491524
  31.3 0.9 copy-start.4
  37.4 9.4 %copy-start.8 = (f32[136,5,4]{0,2,1:T(4,128)S(1)}, f32[136,5,4]{0,2,1:T(4,128)}, u32[]{:S(2)}) copy-start(f32[136,5,4]{0,2,1:T(4,128)} %param.10) | copy-start | bytes 32644
  37.4 16.0 %all-to-all-start.1 = ((f32[16,8,384]{2,1,0:T(8,128)}), f32[16,8,384]{2,1,0:T(8,128)S(1)}, u32[]{:S(2)}, u32[]{:S(2)}) async-start(f32[16,8,384]{2,1,0:T(8,128)} %get-tuple-element.37), calls=%async_computation.1 | async-start | bytes 393216 | tf_op jit(solution)/shard_map/all_to_all | solution.py:444
  44.8 2.1 %copy-start.9 = (f32[136,5,4]{0,2,1:T(4,128)S(1)}, f32[136,5,4]{0,2,1:T(4,128)}, u32[]{:S(2)}) copy-start(f32[136,5,4]{0,2,1:T(4,128)} %param.11) | copy-start | bytes 32644
  44.8 13.5 %collective-permute-start.3 = (bf16[128,640]{1,0:T(8,128)(2,1)S(1)}, bf16[128,640]{1,0:T(8,128)(2,1)S(1)}, u32[]{:S(2)}, u32[]{:S(2)}) collective-permute-start(bf16[128,640]{1,0:T(8,128)(2,1)S(1)} %bitcast.18), channel_id=1, source_target_pairs={{2,0},{3,1},{4,2},{5,3},{6,4},{7,5},{8,6},{9,7},{10,8},{11,9},{12,... | collective-permute-start | bytes 491528 | tf_op jit(solution)/shard_map/ppermute | solution.py:440
  47.2 14.6 %collective-permute-start.2 = (bf16[128,640]{1,0:T(8,128)(2,1)S(1)}, bf16[128,640]{1,0:T(8,128)(2,1)S(1)}, u32[]{:S(2)}, u32[]{:S(2)}) collective-permute-start(bf16[128,640]{1,0:T(8,128)(2,1)S(1)} %bitcast.19), channel_id=1, source_target_pairs={{0,2},{1,3},{2,4},{3,5},{4,6},{5,7},{6,8},{7,9},{8,10},{9,11},{10,... | collective-permute-start | bytes 491528 | tf_op jit(solution)/shard_map/ppermute | solution.py:439
  54.1 4.2 %copy-start.1 = (bf16[128,640]{1,0:T(8,128)(2,1)S(1)}, bf16[128,640]{1,0:T(8,128)(2,1)}, u32[]{:S(2)}) copy-start(bf16[128,640]{1,0:T(8,128)(2,1)} %copy-done) | copy-start | bytes 491524
  54.2 4.2 %copy-start.5 = (f32[2,5,8,384]{3,2,1,0:T(8,128)S(1)}, f32[2,5,8,384]{3,2,1,0:T(8,128)}, u32[]{:S(2)}) copy-start(f32[2,5,8,384]{3,2,1,0:T(8,128)} %copy-done.3) | copy-start | bytes 368644
  54.2 13.1 %all-to-all-start.2 = ((f32[16,8,384]{2,1,0:T(8,128)}), f32[16,8,384]{2,1,0:T(8,128)S(1)}, u32[]{:S(2)}, u32[]{:S(2)}) async-start(f32[16,8,384]{2,1,0:T(8,128)} %broadcast_in_dim.2), calls=%async_computation.2 | async-start | bytes 393216 | tf_op jit(solution)/shard_map/all_to_all | solution.py:446
  76.0 15.6 %all-to-all-start.3 = ((f32[16,32,128]{2,1,0:T(8,128)}), f32[16,32,128]{2,1,0:T(8,128)S(1)}, u32[]{:S(2)}, u32[]{:S(2)}) async-start(f32[16,32,128]{2,1,0:T(8,128)} %bitcast.3), calls=%async_computation.3 | async-start | bytes 524288 | tf_op jit(solution)/shard_map/all_to_all | solution.py:451

commit v5 on v4

--- a/solution.py
+++ b/solution.py
@@ -71,7 +71,8 @@
 
 
 def matrices_kernel(
-    taps_ref, pairs_ref, row_ref, w_ref, wh_ref, wa_ref, left_ref, right_ref, w_far, wh_far, sem,
+    taps_ref, pairs_ref, row_ref, w_ref, wh_ref, left_ref, right_ref,
+    w_far, wh_far, wa_far, wa_ref, sem,
 ):
     for c, out_ref in enumerate((left_ref, right_ref)):
         bins = iota(out_ref.shape, 1) % BINS
@@ -117,7 +118,7 @@
     lax.fori_loop(0, SCALES, one, 0)
     copies = [
         pltpu.make_async_copy(near, far, sem.at[i])
-        for i, (near, far) in enumerate(((w_ref, w_far), (wh_ref, wh_far)))
+        for i, (near, far) in enumerate(((w_ref, w_far), (wh_ref, wh_far), (wa_ref, wa_far)))
     ]
     for copy in copies:
         copy.start()
@@ -235,12 +236,13 @@
 
 def backward_kernel(
     inverse_area,
-    taps_ref, sums_ref, target_ref, weight_ref, left_ref, right_ref, wa_ref, own_ref, up_far, down_far,
-    corr_ref, out_ref, grad_ref, up_ref, down_ref, sem,
+    taps_ref, sums_ref, target_ref, weight_ref, left_ref, right_ref, own_ref, up_far, down_far, wa_far,
+    corr_ref, out_ref, grad_ref, up_ref, down_ref, wa_ref, sem,
 ):
     copies = [
         pltpu.make_async_copy(up_far, up_ref, sem.at[0]),
         pltpu.make_async_copy(down_far, down_ref, sem.at[1]),
+        pltpu.make_async_copy(wa_far, wa_ref, sem.at[2]),
     ]
     for copy in copies:
         copy.start()
@@ -345,14 +347,14 @@
             struct((2, SCALES, ROWS, 3 * XB), F32),
             column,
             column,
-            column,
             struct((PAIRS, TABLE), BF16),
             struct((PAIRS, TABLE), BF16),
             pltpu.HBM(COLUMN, BF16),
             pltpu.HBM(COLUMN, BF16),
+            pltpu.HBM(COLUMN, BF16),
         ),
-        out_specs=[VMEM] * 6 + [HBM] * 2,
-        scratch_shapes=[pltpu.SemaphoreType.DMA((2,))],
+        out_specs=[VMEM] * 5 + [HBM] * 3,
+        scratch_shapes=[pltpu.VMEM(COLUMN, BF16), pltpu.SemaphoreType.DMA((3,))],
         compiler_params=limit(32),
         cost_estimate=cost(20_000_000, 4_000_000),
         name="matrices",
@@ -399,17 +401,18 @@
 def backward(inverse_area, taps, sums, target, weight, left, right, wa, above, own, below):
     return pl.pallas_call(
         lambda *refs: backward_kernel(inverse_area, *refs),
-        in_specs=[SMEM] + [VMEM] * 7 + [HBM] * 2,
+        in_specs=[SMEM] + [VMEM] * 6 + [HBM] * 3,
         out_shape=(struct((PAIRS, ENTRIES), F32), struct((XB * OWN // LANE, LANE), F32)),
         scratch_shapes=[
             pltpu.VMEM((2, 3 * ROWS, BINS, WIN), F32),
             pltpu.VMEM(MAPS, BF16),
             pltpu.VMEM(MAPS, BF16),
-            pltpu.SemaphoreType.DMA((2,)),
+            pltpu.VMEM(COLUMN, BF16),
+            pltpu.SemaphoreType.DMA((3,)),
         ],
         compiler_params=limit(32),
         name="backward",
-    )(taps, sums, target, weight, left, right, wa, own, far(above), far(below))
+    )(taps, sums, target, weight, left, right, own, far(above), far(below), far(wa))
 
 
 def per_device(lensing_maps, filter_taps, survey_mask, bin_pairs, target_corr, pair_weight):
@@ -428,12 +431,12 @@
     windows = pl.pallas_call(
         windows_kernel,
         out_shape=struct((XB, WIN), BF16),
-        compiler_params=limit(8),
+        compiler_params=limit(60),
         name="windows",
     )(strip, survey_mask)
     own = lax.all_to_all(windows, "bin", 0, 0, tiled=True)
     made = matrices(filter_taps, bin_pairs)
-    own, (row, w, wh, wa, left, right, w_far, wh_far) = lax.optimization_barrier((own, made))
+    own, (row, w, wh, left, right, w_far, wh_far, wa) = lax.optimization_barrier((own, made))
     above = lax.ppermute(own, "sky", down_perm)
     below = lax.ppermute(own, "sky", up_perm)
     above2 = lax.ppermute(own, "sky", [(i, i + 2) for i in range(sky - 2)])

time: 93.2 us -> 91.7 us (0.984)
  local copies, waits for them, and re-layouts: 6.27 us -> 3.16 us
  Pallas kernels: 24.1 us -> 25.5 us
    unnamed x24 -> x10, local copies, waits for them, and re-layouts: 4.59 us -> 1.48 us
  transfers between devices with their start and end apart: 8 -> 8, of which waited for: 5 -> 5; matrix products, arithmetic and copies ran while one was open for 2% -> 2% of each run, Pallas kernels for 10% -> 11%
where the time goes in v5:
time: 91.7 us; the launch traced here: 90.9 us
  starting transfers between devices  39.5 us (43%)
  Pallas kernels  25.5 us (28%)
  waiting for transfers between devices  21.9 us (24%)
  local copies, waits for them, and re-layouts  3.16 us (3%)
    all_to_all x1, starting transfers between devices, per_device(): own = lax.all_to_all(windows, 'bin', 0, 0, tiled=True)  9.42 us
    pallas_call x1, Pallas kernels, backward(): pl.pallas_call(lambda *refs: backward_kernel(inverse_area, *refs), in_spe...  9.01 us
    all_to_all x1, waiting for transfers between devices, per_device(): back = lax.all_to_all(tile_grad, 'bin', 0, 0, tiled=True)  8.85 us
    all_to_all x1, starting transfers between devices, per_device(): partial = lax.all_to_all(partial, 'sky', 0, 0, tiled=True)  7.41 us
    pallas_call x2, Pallas kernels, beside(): pl.pallas_call(beside_kernel, in_specs=[VMEM] * 4 + [HBM] * 2, out_specs=...  6.82 us
    ppermute x1, starting transfers between devices, per_device(): above2 = lax.ppermute(own, 'sky', [(i, i + 2) for i in range(sky - 2)])  6.23 us
    all_to_all x1, starting transfers between devices, per_device(): back = lax.all_to_all(tile_grad, 'bin', 0, 0, tiled=True)  6.06 us
    ppermute x1, waiting for transfers between devices, per_device(): above = lax.ppermute(own, 'sky', down_perm)  5.33 us
  transfers between devices with their start and end apart: 8, of which 5 were waited for; matrix products, arithmetic and copies ran while one was open for 2% of the time, Pallas kernels for 11%

profile of v5, /device:TPU:16, one launch (start us, length us, event | category | flops | bytes accessed | tf_op | source)
XLA Modules:
  0.0 90.9 jit_solution(1097094564874010465)
XLA Ops:
  0.6 1.7 %windows.1 = bf16[128,640]{1,0:T(8,128)(2,1)} custom-call(bf16[8,8192]{1,0:T(8,128)(2,1)} %bitcast.24, s32[1,64]{1,0:T(1,128)} %mask_ref.1), custom_call_target="tpu_custom_call" | custom-call | tf_op jit(solution)/shard_map/windows/pallas_call | solution.py:431
  2.3 0.0 copy-start.3
  2.3 9.4 %all-to-all-start = ((bf16[16,8,640]{2,1,0:T(8,128)(2,1)}), bf16[16,8,640]{2,1,0:T(8,128)(2,1)S(1)}, u32[]{:S(2)}, u32[]{:S(2)}) async-start(bf16[16,8,640]{2,1,0:T(8,128)(2,1)} %bitcast.23), calls=%async_computation | async-start | bytes 327680 | tf_op jit(solution)/shard_map/all_to_all | solution.py:437
  11.8 0.0 copy-done.3
  11.8 0.1 copy.12
  11.9 0.0 copy-start
  11.9 0.7 copy-done
  12.6 2.8 %matrices.1 = (f32[2,5,8,384]{3,2,1,0:T(8,128)S(1)}, bf16[5,256,256]{2,1,0:T(8,128)(2,1)S(1)}, bf16[5,256,256]{2,1,0:T(8,128)(2,1)S(1)}, bf16[144,320]{1,0:T(8,1...) custom-call(f32[5,17]{1,0:T(8,128)S(1)} %copy-done, ...), custom_call_target="tpu_custom_call" | custom-call | flops 20000000 | bytes 4000000 | tf_op jit(solution)/shard_map/matrices/pallas_call | solution.py:343
  15.3 5.3 %all-to-all-done = bf16[16,8,640]{2,1,0:T(8,128)(2,1)S(1)} async-done(((bf16[16,8,640]{2,1,0:T(8,128)(2,1)}), bf16[16,8,640]{2,1,0:T(8,128)(2,1)S(1)}, u32[]{:S(2)}, u32[]{:S(2)}) %all-to-all-start) | async-done | bytes 163872 | tf_op jit(solution)/shard_map/all_to_all | solution.py:437
  20.6 1.9 %collective-permute-start.1 = (bf16[128,640]{1,0:T(8,128)(2,1)S(1)}, bf16[128,640]{1,0:T(8,128)(2,1)S(1)}, u32[]{:S(2)}, u32[]{:S(2)}) collective-permute-start(bf16[128,640]{1,0:T(8,128)(2,1)S(1)} %bitcast.15), channel_id=1, source_target_pairs={{1,0},{2,1},{3,2},{4,3},{5,4},{6,5},{7,6},{8,7},{9,8},{10,9},{11,1... | collective-permute-start | bytes 491528 | tf_op jit(solution)/shard_map/ppermute | solution.py:441
  22.5 2.4 %collective-permute-start = (bf16[128,640]{1,0:T(8,128)(2,1)S(1)}, bf16[128,640]{1,0:T(8,128)(2,1)S(1)}, u32[]{:S(2)}, u32[]{:S(2)}) collective-permute-start(bf16[128,640]{1,0:T(8,128)(2,1)S(1)} %bitcast.16), channel_id=1, source_target_pairs={{0,1},{1,2},{2,3},{3,4},{4,5},{5,6},{6,7},{7,8},{8,9},{9,10},{10,1... | collective-permute-start | bytes 491528 | tf_op jit(solution)/shard_map/ppermute | solution.py:440
  24.9 0.4 collective-permute-done.1.down_ref.second_ref
  25.3 5.3 %collective-permute-done.up_ref.second_ref = bf16[128,640]{1,0:T(8,128)(2,1)S(1)} collective-permute-done((bf16[128,640]{1,0:T(8,128)(2,1)S(1)}, bf16[128,640]{1,0:T(8,128)(2,1)S(1)}, u32[]{:S(2)}, u32[]{:S(2)}) %collective-permute-start) | collective-permute-done | bytes 163872 | tf_op jit(solution)/shard_map/ppermute | solution.py:440
  30.7 5.2 %forward.1 = (bf16[656,640]{1,0:T(8,128)(2,1)S(1)}, f32[16,8,384]{2,1,0:T(8,128)}) custom-call(bf16[128,640]{1,0:T(8,128)(2,1)S(1)} %collective-permute-done.up_ref.second_ref, bf16[128,640]{1,0:T(8,128)(2,1)S(1)} %bitcast.17, bf16[128,640]{1,0:T(8,128)(2,1)S(1)} %collective-permute-done.1.down_ref.second_ref, ...), custom_call_target="tpu_custom_call" | custom-call | tf_op jit(solution)/shard_map/forward/pallas_call | solution.py:373
  35.9 0.0 copy-start.1
  35.9 7.4 %all-to-all-start.1 = ((f32[16,8,384]{2,1,0:T(8,128)}), f32[16,8,384]{2,1,0:T(8,128)S(1)}, u32[]{:S(2)}, u32[]{:S(2)}) async-start(f32[16,8,384]{2,1,0:T(8,128)} %get-tuple-element.37), calls=%async_computation.1 | async-start | bytes 393216 | tf_op jit(solution)/shard_map/all_to_all | solution.py:447
  43.3 0.0 copy-start.2
  43.3 2.0 %collective-permute-start.3 = (bf16[128,640]{1,0:T(8,128)(2,1)S(1)}, bf16[128,640]{1,0:T(8,128)(2,1)S(1)}, u32[]{:S(2)}, u32[]{:S(2)}) collective-permute-start(bf16[128,640]{1,0:T(8,128)(2,1)S(1)} %bitcast.18), channel_id=1, source_target_pairs={{2,0},{3,1},{4,2},{5,3},{6,4},{7,5},{8,6},{9,7},{10,8},{11,9},{12,... | collective-permute-start | bytes 491528 | tf_op jit(solution)/shard_map/ppermute | solution.py:443
  45.3 0.0 copy-done.1
  45.3 0.0 copy-done.2
  45.4 0.1 copy.14
  45.5 0.1 copy.13
  45.6 6.2 %collective-permute-start.2 = (bf16[128,640]{1,0:T(8,128)(2,1)S(1)}, bf16[128,640]{1,0:T(8,128)(2,1)S(1)}, u32[]{:S(2)}, u32[]{:S(2)}) collective-permute-start(bf16[128,640]{1,0:T(8,128)(2,1)S(1)} %bitcast.19), channel_id=1, source_target_pairs={{0,2},{1,3},{2,4},{3,5},{4,6},{5,7},{6,8},{7,9},{8,10},{9,11},{10,... | collective-permute-start | bytes 491528 | tf_op jit(solution)/shard_map/ppermute | solution.py:442
  51.9 0.0 all-to-all-done.1
  51.9 0.7 broadcast_in_dim.2
  52.6 4.0 %all-to-all-start.2 = ((f32[16,8,384]{2,1,0:T(8,128)}), f32[16,8,384]{2,1,0:T(8,128)S(1)}, u32[]{:S(2)}, u32[]{:S(2)}) async-start(f32[16,8,384]{2,1,0:T(8,128)} %broadcast_in_dim.2), calls=%async_computation.2 | async-start | bytes 393216 | tf_op jit(solution)/shard_map/all_to_all | solution.py:449
  56.6 0.0 collective-permute-done.3.third_ref
  56.7 3.4 %beside.3.refs_8_ = bf16[656,640]{1,0:T(8,128)(2,1)} custom-call(bf16[128,640]{1,0:T(8,128)(2,1)S(1)} %bitcast.20, bf16[128,640]{1,0:T(8,128)(2,1)S(1)} %collective-permute-done.1.down_ref.second_ref, bf16[128,640]{1,0:T(8,128)(2,1)S(1)} %collective-permute-done.3.third_ref, f32[2,5,8,384]{3,2,1,0:T(8,128)S(1)} %get-tuple-element.32.row_ref, ...), custom_call_target="tpu_custom_call" | custom-call | flops 2000000000 | bytes 8000000 | tf_op jit(solution)/shard_map/beside/pallas_call | solution.py:383
  60.1 0.0 collective-permute-done.2.first_ref
  60.1 3.4 %beside.2.refs_7_ = bf16[656,640]{1,0:T(8,128)(2,1)} custom-call(bf16[128,640]{1,0:T(8,128)(2,1)S(1)} %collective-permute-done.2.first_ref, bf16[128,640]{1,0:T(8,128)(2,1)S(1)} %collective-permute-done.up_ref.second_ref, bf16[128,640]{1,0:T(8,128)(2,1)S(1)} %bitcast.21, f32[2,5,8,384]{3,2,1,0:T(8,128)S(1)} %get-tuple-element.32.row_ref, ...), custom_call_target="tpu_custom_call" | custom-call | flops 2000000000 | bytes 8000000 | tf_op jit(solution)/shard_map/beside/pallas_call | solution.py:383
  63.5 2.1 %all-to-all-done.2.refs_1_ = f32[16,8,384]{2,1,0:T(8,128)S(1)} async-done(((f32[16,8,384]{2,1,0:T(8,128)}), f32[16,8,384]{2,1,0:T(8,128)S(1)}, u32[]{:S(2)}, u32[]{:S(2)}) %all-to-all-start.2) | async-done | bytes 196640 | tf_op jit(solution)/shard_map/all_to_all | solution.py:449
  65.6 9.0 %backward.1 = (f32[144,20]{1,0:T(8,128)S(1)}, f32[512,128]{1,0:T(8,128)}) custom-call(f32[5,17]{1,0:T(8,128)S(1)} %copy-done, f32[16,8,384]{2,1,0:T(8,128)S(1)} %all-to-all-done.2.refs_1_, f32[144,20]{1,0:T(8,128)S(1)} %pad.12.refs_2_, f32[144,20]{1,0:T(8,128)S(1)} %pad.13.refs_3_, bf16[144,320]{1,0:T(8,128)(2,1)S(1)} %get-tuple-element.35.left_ref.refs_4_, ...), custom_call_target="tpu_custom_call" | custom-call | tf_op jit(solution)/shard_map/backward/pallas_call | solution.py:402
  74.6 6.1 %all-to-all-start.3 = ((f32[16,32,128]{2,1,0:T(8,128)}), f32[16,32,128]{2,1,0:T(8,128)S(1)}, u32[]{:S(2)}, u32[]{:S(2)}) async-start(f32[16,32,128]{2,1,0:T(8,128)} %bitcast.3), calls=%async_computation.3 | async-start | bytes 524288 | tf_op jit(solution)/shard_map/all_to_all | solution.py:454
  80.7 0.1 copy.15
  80.7 0.6 reshape.27
  81.4 8.9 %all-to-all-done.3 = f32[16,32,128]{2,1,0:T(8,128)S(1)} async-done(((f32[16,32,128]{2,1,0:T(8,128)}), f32[16,32,128]{2,1,0:T(8,128)S(1)}, u32[]{:S(2)}, u32[]{:S(2)}) %all-to-all-start.3) | async-done | bytes 262176 | tf_op jit(solution)/shard_map/all_to_all | solution.py:454
  90.2 0.7 copy.17
  (7 shorter events, 0.1 us)
Async XLA Ops:
  2.3 9.4 %copy-start.3 = (s32[136,2]{0,1:T(2,128)S(1)}, s32[136,2]{0,1:T(2,128)}, u32[]{:S(2)}) copy-start(s32[136,2]{0,1:T(2,128)} %param.9) | copy-start | bytes 3268
  2.3 18.3 %all-to-all-start = ((bf16[16,8,640]{2,1,0:T(8,128)(2,1)}), bf16[16,8,640]{2,1,0:T(8,128)(2,1)S(1)}, u32[]{:S(2)}, u32[]{:S(2)}) async-start(bf16[16,8,640]{2,1,0:T(8,128)(2,1)} %bitcast.23), calls=%async_computation | async-start | bytes 327680 | tf_op jit(solution)/shard_map/all_to_all | solution.py:437
  11.9 0.7 copy-start
  20.6 4.7 %collective-permute-start.1 = (bf16[128,640]{1,0:T(8,128)(2,1)S(1)}, bf16[128,640]{1,0:T(8,128)(2,1)S(1)}, u32[]{:S(2)}, u32[]{:S(2)}) collective-permute-start(bf16[128,640]{1,0:T(8,128)(2,1)S(1)} %bitcast.15), channel_id=1, source_target_pairs={{1,0},{2,1},{3,2},{4,3},{5,4},{6,5},{7,6},{8,7},{9,8},{10,9},{11,1... | collective-permute-start | bytes 491528 | tf_op jit(solution)/shard_map/ppermute | solution.py:441
  22.5 8.1 %collective-permute-start = (bf16[128,640]{1,0:T(8,128)(2,1)S(1)}, bf16[128,640]{1,0:T(8,128)(2,1)S(1)}, u32[]{:S(2)}, u32[]{:S(2)}) collective-permute-start(bf16[128,640]{1,0:T(8,128)(2,1)S(1)} %bitcast.16), channel_id=1, source_target_pairs={{0,1},{1,2},{2,3},{3,4},{4,5},{5,6},{6,7},{7,8},{8,9},{9,10},{10,1... | collective-permute-start | bytes 491528 | tf_op jit(solution)/shard_map/ppermute | solution.py:440
  35.9 9.4 %copy-start.1 = (f32[136,5,4]{0,2,1:T(4,128)S(1)}, f32[136,5,4]{0,2,1:T(4,128)}, u32[]{:S(2)}) copy-start(f32[136,5,4]{0,2,1:T(4,128)} %param.10) | copy-start | bytes 32644
  35.9 16.0 %all-to-all-start.1 = ((f32[16,8,384]{2,1,0:T(8,128)}), f32[16,8,384]{2,1,0:T(8,128)S(1)}, u32[]{:S(2)}, u32[]{:S(2)}) async-start(f32[16,8,384]{2,1,0:T(8,128)} %get-tuple-element.37), calls=%async_computation.1 | async-start | bytes 393216 | tf_op jit(solution)/shard_map/all_to_all | solution.py:447
  43.3 2.1 %copy-start.2 = (f32[136,5,4]{0,2,1:T(4,128)S(1)}, f32[136,5,4]{0,2,1:T(4,128)}, u32[]{:S(2)}) copy-start(f32[136,5,4]{0,2,1:T(4,128)} %param.11) | copy-start | bytes 32644
  43.3 13.4 %collective-permute-start.3 = (bf16[128,640]{1,0:T(8,128)(2,1)S(1)}, bf16[128,640]{1,0:T(8,128)(2,1)S(1)}, u32[]{:S(2)}, u32[]{:S(2)}) collective-permute-start(bf16[128,640]{1,0:T(8,128)(2,1)S(1)} %bitcast.18), channel_id=1, source_target_pairs={{2,0},{3,1},{4,2},{5,3},{6,4},{7,5},{8,6},{9,7},{10,8},{11,9},{12,... | collective-permute-start | bytes 491528 | tf_op jit(solution)/shard_map/ppermute | solution.py:443
  45.6 14.5 %collective-permute-start.2 = (bf16[128,640]{1,0:T(8,128)(2,1)S(1)}, bf16[128,640]{1,0:T(8,128)(2,1)S(1)}, u32[]{:S(2)}, u32[]{:S(2)}) collective-permute-start(bf16[128,640]{1,0:T(8,128)(2,1)S(1)} %bitcast.19), channel_id=1, source_target_pairs={{0,2},{1,3},{2,4},{3,5},{4,6},{5,7},{6,8},{7,9},{8,10},{9,11},{10,... | collective-permute-start | bytes 491528 | tf_op jit(solution)/shard_map/ppermute | solution.py:442
  52.6 13.0 %all-to-all-start.2 = ((f32[16,8,384]{2,1,0:T(8,128)}), f32[16,8,384]{2,1,0:T(8,128)S(1)}, u32[]{:S(2)}, u32[]{:S(2)}) async-start(f32[16,8,384]{2,1,0:T(8,128)} %broadcast_in_dim.2), calls=%async_computation.2 | async-start | bytes 393216 | tf_op jit(solution)/shard_map/all_to_all | solution.py:449
  74.6 15.6 %all-to-all-start.3 = ((f32[16,32,128]{2,1,0:T(8,128)}), f32[16,32,128]{2,1,0:T(8,128)S(1)}, u32[]{:S(2)}, u32[]{:S(2)}) async-start(f32[16,32,128]{2,1,0:T(8,128)} %bitcast.3), calls=%async_computation.3 | async-start | bytes 524288 | tf_op jit(solution)/shard_map/all_to_all | solution.py:454

commit v6 on v5

--- a/solution.py
+++ b/solution.py
@@ -284,10 +284,9 @@
             [jnp.concatenate([mix, zero], axis=1), jnp.concatenate([zero, mix], axis=1)], axis=0
         ).astype(BF16)
         for n, (k, ref) in enumerate(((1, own_ref), (0, up_ref), (2, down_ref))):
-            if s == 0 and n == 1:
-                for copy in copies:
-                    copy.wait()
-                masks += [mask_of(up_ref), mask_of(down_ref)]
+            if s == 0 and n:
+                copies[n - 1].wait()
+                masks.append(mask_of(ref))
             mask = masks[n]
             g = ref[XB * s : XB * (s + 1), :]
             ahead = [pltpu.roll(g, EDGE - l, 1) for l in range(LAGS)]
@@ -307,6 +306,8 @@
                 acc = acc + taps_ref[s, TAPS - 1 - a] * grad_ref[s % 2, x + a]
             rows.append(acc)
         rows = jnp.concatenate(rows, axis=0)
+        if s == 0:
+            copies[2].wait()
         tiles = banded([rows[:, LANE * c : LANE * (c + 2)] for c in range(OWN // LANE)], wa_ref[s])
         totals = [total + tile for total, tile in zip(totals, tiles)]
     for c, total in enumerate(totals):

time: 91.7 us -> 91.5 us (level)
  no operation moved by 1% of the time
where the time goes in v6:
time: 91.5 us; the launch traced here: 90.8 us
  starting transfers between devices  39.5 us (43%)
  Pallas kernels  25.3 us (28%)
  waiting for transfers between devices  21.9 us (24%)
  local copies, waits for them, and re-layouts  3.16 us (3%)
    all_to_all x1, starting transfers between devices, per_device(): own = lax.all_to_all(windows, 'bin', 0, 0, tiled=True)  9.42 us
    all_to_all x1, waiting for transfers between devices, per_device(): back = lax.all_to_all(tile_grad, 'bin', 0, 0, tiled=True)  8.85 us
    pallas_call x1, Pallas kernels, backward(): pl.pallas_call(lambda *refs: backward_kernel(inverse_area, *refs), in_spe...  8.83 us
    all_to_all x1, starting transfers between devices, per_device(): partial = lax.all_to_all(partial, 'sky', 0, 0, tiled=True)  7.41 us
    pallas_call x2, Pallas kernels, beside(): pl.pallas_call(beside_kernel, in_specs=[VMEM] * 4 + [HBM] * 2, out_specs=...  6.82 us
    ppermute x1, starting transfers between devices, per_device(): above2 = lax.ppermute(own, 'sky', [(i, i + 2) for i in range(sky - 2)])  6.23 us
    all_to_all x1, starting transfers between devices, per_device(): back = lax.all_to_all(tile_grad, 'bin', 0, 0, tiled=True)  6.06 us
    ppermute x1, waiting for transfers between devices, per_device(): above = lax.ppermute(own, 'sky', down_perm)  5.33 us
  transfers between devices with their start and end apart: 8, of which 5 were waited for; matrix products, arithmetic and copies ran while one was open for 2% of the time, Pallas kernels for 11%

profile of v6, /device:TPU:16, one launch (start us, length us, event | category | flops | bytes accessed | tf_op | source)
XLA Modules:
  0.0 90.8 jit_solution(2782998072798118998)
XLA Ops:
  0.6 1.7 %windows.1 = bf16[128,640]{1,0:T(8,128)(2,1)} custom-call(bf16[8,8192]{1,0:T(8,128)(2,1)} %bitcast.24, s32[1,64]{1,0:T(1,128)} %mask_ref.1), custom_call_target="tpu_custom_call" | custom-call | tf_op jit(solution)/shard_map/windows/pallas_call | solution.py:432
  2.3 0.0 copy-start.3
  2.3 9.4 %all-to-all-start = ((bf16[16,8,640]{2,1,0:T(8,128)(2,1)}), bf16[16,8,640]{2,1,0:T(8,128)(2,1)S(1)}, u32[]{:S(2)}, u32[]{:S(2)}) async-start(bf16[16,8,640]{2,1,0:T(8,128)(2,1)} %bitcast.23), calls=%async_computation | async-start | bytes 327680 | tf_op jit(solution)/shard_map/all_to_all | solution.py:438
  11.8 0.0 copy-done.3
  11.8 0.1 copy.12
  11.9 0.0 copy-start
  11.9 0.7 copy-done
  12.6 2.8 %matrices.1 = (f32[2,5,8,384]{3,2,1,0:T(8,128)S(1)}, bf16[5,256,256]{2,1,0:T(8,128)(2,1)S(1)}, bf16[5,256,256]{2,1,0:T(8,128)(2,1)S(1)}, bf16[144,320]{1,0:T(8,1...) custom-call(f32[5,17]{1,0:T(8,128)S(1)} %copy-done, ...), custom_call_target="tpu_custom_call" | custom-call | flops 20000000 | bytes 4000000 | tf_op jit(solution)/shard_map/matrices/pallas_call | solution.py:344
  15.3 5.3 %all-to-all-done = bf16[16,8,640]{2,1,0:T(8,128)(2,1)S(1)} async-done(((bf16[16,8,640]{2,1,0:T(8,128)(2,1)}), bf16[16,8,640]{2,1,0:T(8,128)(2,1)S(1)}, u32[]{:S(2)}, u32[]{:S(2)}) %all-to-all-start) | async-done | bytes 163872 | tf_op jit(solution)/shard_map/all_to_all | solution.py:438
  20.6 1.9 %collective-permute-start.1 = (bf16[128,640]{1,0:T(8,128)(2,1)S(1)}, bf16[128,640]{1,0:T(8,128)(2,1)S(1)}, u32[]{:S(2)}, u32[]{:S(2)}) collective-permute-start(bf16[128,640]{1,0:T(8,128)(2,1)S(1)} %bitcast.15), channel_id=1, source_target_pairs={{1,0},{2,1},{3,2},{4,3},{5,4},{6,5},{7,6},{8,7},{9,8},{10,9},{11,1... | collective-permute-start | bytes 491528 | tf_op jit(solution)/shard_map/ppermute | solution.py:442
  22.5 2.4 %collective-permute-start = (bf16[128,640]{1,0:T(8,128)(2,1)S(1)}, bf16[128,640]{1,0:T(8,128)(2,1)S(1)}, u32[]{:S(2)}, u32[]{:S(2)}) collective-permute-start(bf16[128,640]{1,0:T(8,128)(2,1)S(1)} %bitcast.16), channel_id=1, source_target_pairs={{0,1},{1,2},{2,3},{3,4},{4,5},{5,6},{6,7},{7,8},{8,9},{9,10},{10,1... | collective-permute-start | bytes 491528 | tf_op jit(solution)/shard_map/ppermute | solution.py:441
  24.9 0.4 collective-permute-done.1.down_ref.second_ref
  25.3 5.3 %collective-permute-done.up_ref.second_ref = bf16[128,640]{1,0:T(8,128)(2,1)S(1)} collective-permute-done((bf16[128,640]{1,0:T(8,128)(2,1)S(1)}, bf16[128,640]{1,0:T(8,128)(2,1)S(1)}, u32[]{:S(2)}, u32[]{:S(2)}) %collective-permute-start) | collective-permute-done | bytes 163872 | tf_op jit(solution)/shard_map/ppermute | solution.py:441
  30.7 5.2 %forward.1 = (bf16[656,640]{1,0:T(8,128)(2,1)S(1)}, f32[16,8,384]{2,1,0:T(8,128)}) custom-call(bf16[128,640]{1,0:T(8,128)(2,1)S(1)} %collective-permute-done.up_ref.second_ref, bf16[128,640]{1,0:T(8,128)(2,1)S(1)} %bitcast.17, bf16[128,640]{1,0:T(8,128)(2,1)S(1)} %collective-permute-done.1.down_ref.second_ref, ...), custom_call_target="tpu_custom_call" | custom-call | tf_op jit(solution)/shard_map/forward/pallas_call | solution.py:374
  35.9 0.0 copy-start.1
  35.9 7.4 %all-to-all-start.1 = ((f32[16,8,384]{2,1,0:T(8,128)}), f32[16,8,384]{2,1,0:T(8,128)S(1)}, u32[]{:S(2)}, u32[]{:S(2)}) async-start(f32[16,8,384]{2,1,0:T(8,128)} %get-tuple-element.37), calls=%async_computation.1 | async-start | bytes 393216 | tf_op jit(solution)/shard_map/all_to_all | solution.py:448
  43.3 0.0 copy-start.2
  43.3 2.0 %collective-permute-start.3 = (bf16[128,640]{1,0:T(8,128)(2,1)S(1)}, bf16[128,640]{1,0:T(8,128)(2,1)S(1)}, u32[]{:S(2)}, u32[]{:S(2)}) collective-permute-start(bf16[128,640]{1,0:T(8,128)(2,1)S(1)} %bitcast.18), channel_id=1, source_target_pairs={{2,0},{3,1},{4,2},{5,3},{6,4},{7,5},{8,6},{9,7},{10,8},{11,9},{12,... | collective-permute-start | bytes 491528 | tf_op jit(solution)/shard_map/ppermute | solution.py:444
  45.3 0.0 copy-done.1
  45.3 0.0 copy-done.2
  45.4 0.1 copy.14
  45.5 0.1 copy.13
  45.6 6.2 %collective-permute-start.2 = (bf16[128,640]{1,0:T(8,128)(2,1)S(1)}, bf16[128,640]{1,0:T(8,128)(2,1)S(1)}, u32[]{:S(2)}, u32[]{:S(2)}) collective-permute-start(bf16[128,640]{1,0:T(8,128)(2,1)S(1)} %bitcast.19), channel_id=1, source_target_pairs={{0,2},{1,3},{2,4},{3,5},{4,6},{5,7},{6,8},{7,9},{8,10},{9,11},{10,... | collective-permute-start | bytes 491528 | tf_op jit(solution)/shard_map/ppermute | solution.py:443
  51.9 0.0 all-to-all-done.1
  51.9 0.7 broadcast_in_dim.2
  52.6 4.0 %all-to-all-start.2 = ((f32[16,8,384]{2,1,0:T(8,128)}), f32[16,8,384]{2,1,0:T(8,128)S(1)}, u32[]{:S(2)}, u32[]{:S(2)}) async-start(f32[16,8,384]{2,1,0:T(8,128)} %broadcast_in_dim.2), calls=%async_computation.2 | async-start | bytes 393216 | tf_op jit(solution)/shard_map/all_to_all | solution.py:450
  56.6 0.0 collective-permute-done.3.third_ref
  56.7 3.4 %beside.3.refs_8_ = bf16[656,640]{1,0:T(8,128)(2,1)} custom-call(bf16[128,640]{1,0:T(8,128)(2,1)S(1)} %bitcast.20, bf16[128,640]{1,0:T(8,128)(2,1)S(1)} %collective-permute-done.1.down_ref.second_ref, bf16[128,640]{1,0:T(8,128)(2,1)S(1)} %collective-permute-done.3.third_ref, f32[2,5,8,384]{3,2,1,0:T(8,128)S(1)} %get-tuple-element.32.row_ref, ...), custom_call_target="tpu_custom_call" | custom-call | flops 2000000000 | bytes 8000000 | tf_op jit(solution)/shard_map/beside/pallas_call | solution.py:384
  60.1 0.0 collective-permute-done.2.first_ref
  60.1 3.4 %beside.2.refs_7_ = bf16[656,640]{1,0:T(8,128)(2,1)} custom-call(bf16[128,640]{1,0:T(8,128)(2,1)S(1)} %collective-permute-done.2.first_ref, bf16[128,640]{1,0:T(8,128)(2,1)S(1)} %collective-permute-done.up_ref.second_ref, bf16[128,640]{1,0:T(8,128)(2,1)S(1)} %bitcast.21, f32[2,5,8,384]{3,2,1,0:T(8,128)S(1)} %get-tuple-element.32.row_ref, ...), custom_call_target="tpu_custom_call" | custom-call | flops 2000000000 | bytes 8000000 | tf_op jit(solution)/shard_map/beside/pallas_call | solution.py:384
  63.5 2.1 %all-to-all-done.2.refs_1_ = f32[16,8,384]{2,1,0:T(8,128)S(1)} async-done(((f32[16,8,384]{2,1,0:T(8,128)}), f32[16,8,384]{2,1,0:T(8,128)S(1)}, u32[]{:S(2)}, u32[]{:S(2)}) %all-to-all-start.2) | async-done | bytes 196640 | tf_op jit(solution)/shard_map/all_to_all | solution.py:450
  65.6 8.8 %backward.1 = (f32[144,20]{1,0:T(8,128)S(1)}, f32[512,128]{1,0:T(8,128)}) custom-call(f32[5,17]{1,0:T(8,128)S(1)} %copy-done, f32[16,8,384]{2,1,0:T(8,128)S(1)} %all-to-all-done.2.refs_1_, f32[144,20]{1,0:T(8,128)S(1)} %pad.12.refs_2_, f32[144,20]{1,0:T(8,128)S(1)} %pad.13.refs_3_, bf16[144,320]{1,0:T(8,128)(2,1)S(1)} %get-tuple-element.35.left_ref.refs_4_, ...), custom_call_target="tpu_custom_call" | custom-call | tf_op jit(solution)/shard_map/backward/pallas_call | solution.py:403
  74.4 6.1 %all-to-all-start.3 = ((f32[16,32,128]{2,1,0:T(8,128)}), f32[16,32,128]{2,1,0:T(8,128)S(1)}, u32[]{:S(2)}, u32[]{:S(2)}) async-start(f32[16,32,128]{2,1,0:T(8,128)} %bitcast.3), calls=%async_computation.3 | async-start | bytes 524288 | tf_op jit(solution)/shard_map/all_to_all | solution.py:455
  80.5 0.1 copy.15
  80.6 0.6 reshape.27
  81.2 8.9 %all-to-all-done.3 = f32[16,32,128]{2,1,0:T(8,128)S(1)} async-done(((f32[16,32,128]{2,1,0:T(8,128)}), f32[16,32,128]{2,1,0:T(8,128)S(1)}, u32[]{:S(2)}, u32[]{:S(2)}) %all-to-all-start.3) | async-done | bytes 262176 | tf_op jit(solution)/shard_map/all_to_all | solution.py:455
  90.1 0.7 copy.17
  (7 shorter events, 0.1 us)
Async XLA Ops:
  2.3 9.4 %copy-start.3 = (s32[136,2]{0,1:T(2,128)S(1)}, s32[136,2]{0,1:T(2,128)}, u32[]{:S(2)}) copy-start(s32[136,2]{0,1:T(2,128)} %param.9) | copy-start | bytes 3268
  2.3 18.3 %all-to-all-start = ((bf16[16,8,640]{2,1,0:T(8,128)(2,1)}), bf16[16,8,640]{2,1,0:T(8,128)(2,1)S(1)}, u32[]{:S(2)}, u32[]{:S(2)}) async-start(bf16[16,8,640]{2,1,0:T(8,128)(2,1)} %bitcast.23), calls=%async_computation | async-start | bytes 327680 | tf_op jit(solution)/shard_map/all_to_all | solution.py:438
  11.9 0.7 copy-start
  20.6 4.7 %collective-permute-start.1 = (bf16[128,640]{1,0:T(8,128)(2,1)S(1)}, bf16[128,640]{1,0:T(8,128)(2,1)S(1)}, u32[]{:S(2)}, u32[]{:S(2)}) collective-permute-start(bf16[128,640]{1,0:T(8,128)(2,1)S(1)} %bitcast.15), channel_id=1, source_target_pairs={{1,0},{2,1},{3,2},{4,3},{5,4},{6,5},{7,6},{8,7},{9,8},{10,9},{11,1... | collective-permute-start | bytes 491528 | tf_op jit(solution)/shard_map/ppermute | solution.py:442
  22.5 8.1 %collective-permute-start = (bf16[128,640]{1,0:T(8,128)(2,1)S(1)}, bf16[128,640]{1,0:T(8,128)(2,1)S(1)}, u32[]{:S(2)}, u32[]{:S(2)}) collective-permute-start(bf16[128,640]{1,0:T(8,128)(2,1)S(1)} %bitcast.16), channel_id=1, source_target_pairs={{0,1},{1,2},{2,3},{3,4},{4,5},{5,6},{6,7},{7,8},{8,9},{9,10},{10,1... | collective-permute-start | bytes 491528 | tf_op jit(solution)/shard_map/ppermute | solution.py:441
  35.9 9.4 %copy-start.1 = (f32[136,5,4]{0,2,1:T(4,128)S(1)}, f32[136,5,4]{0,2,1:T(4,128)}, u32[]{:S(2)}) copy-start(f32[136,5,4]{0,2,1:T(4,128)} %param.10) | copy-start | bytes 32644
  35.9 16.0 %all-to-all-start.1 = ((f32[16,8,384]{2,1,0:T(8,128)}), f32[16,8,384]{2,1,0:T(8,128)S(1)}, u32[]{:S(2)}, u32[]{:S(2)}) async-start(f32[16,8,384]{2,1,0:T(8,128)} %get-tuple-element.37), calls=%async_computation.1 | async-start | bytes 393216 | tf_op jit(solution)/shard_map/all_to_all | solution.py:448
  43.3 2.1 %copy-start.2 = (f32[136,5,4]{0,2,1:T(4,128)S(1)}, f32[136,5,4]{0,2,1:T(4,128)}, u32[]{:S(2)}) copy-start(f32[136,5,4]{0,2,1:T(4,128)} %param.11) | copy-start | bytes 32644
  43.3 13.4 %collective-permute-start.3 = (bf16[128,640]{1,0:T(8,128)(2,1)S(1)}, bf16[128,640]{1,0:T(8,128)(2,1)S(1)}, u32[]{:S(2)}, u32[]{:S(2)}) collective-permute-start(bf16[128,640]{1,0:T(8,128)(2,1)S(1)} %bitcast.18), channel_id=1, source_target_pairs={{2,0},{3,1},{4,2},{5,3},{6,4},{7,5},{8,6},{9,7},{10,8},{11,9},{12,... | collective-permute-start | bytes 491528 | tf_op jit(solution)/shard_map/ppermute | solution.py:444
  45.6 14.5 %collective-permute-start.2 = (bf16[128,640]{1,0:T(8,128)(2,1)S(1)}, bf16[128,640]{1,0:T(8,128)(2,1)S(1)}, u32[]{:S(2)}, u32[]{:S(2)}) collective-permute-start(bf16[128,640]{1,0:T(8,128)(2,1)S(1)} %bitcast.19), channel_id=1, source_target_pairs={{0,2},{1,3},{2,4},{3,5},{4,6},{5,7},{6,8},{7,9},{8,10},{9,11},{10,... | collective-permute-start | bytes 491528 | tf_op jit(solution)/shard_map/ppermute | solution.py:443
  52.6 13.0 %all-to-all-start.2 = ((f32[16,8,384]{2,1,0:T(8,128)}), f32[16,8,384]{2,1,0:T(8,128)S(1)}, u32[]{:S(2)}, u32[]{:S(2)}) async-start(f32[16,8,384]{2,1,0:T(8,128)} %broadcast_in_dim.2), calls=%async_computation.2 | async-start | bytes 393216 | tf_op jit(solution)/shard_map/all_to_all | solution.py:450
  74.4 15.7 %all-to-all-start.3 = ((f32[16,32,128]{2,1,0:T(8,128)}), f32[16,32,128]{2,1,0:T(8,128)S(1)}, u32[]{:S(2)}, u32[]{:S(2)}) async-start(f32[16,32,128]{2,1,0:T(8,128)} %bitcast.3), calls=%async_computation.3 | async-start | bytes 524288 | tf_op jit(solution)/shard_map/all_to_all | solution.py:455

commit v7 on v6

--- a/solution.py
+++ b/solution.py
@@ -442,12 +442,12 @@
     below = lax.ppermute(own, "sky", up_perm)
     above2 = lax.ppermute(own, "sky", [(i, i + 2) for i in range(sky - 2)])
     below2 = lax.ppermute(own, "sky", [(i + 2, i) for i in range(sky - 2)])
-    g, partial = forward((above, own, below), row, w, wh, left, right, sky)
+    g, partial = forward((above, own, below), row, w, wh, left, right, bins)
     g_above = beside((above2, above, own), row, w_far, wh_far)
     g_below = beside((own, below, below2), row, w_far, wh_far)
+    partial = lax.all_to_all(partial, "bin", 0, 0, tiled=True)
+    partial = jnp.broadcast_to(jnp.sum(partial, axis=0)[None], (sky,) + partial.shape[1:])
     partial = lax.all_to_all(partial, "sky", 0, 0, tiled=True)
-    partial = jnp.broadcast_to(jnp.sum(partial, axis=0)[None], (bins,) + partial.shape[1:])
-    partial = lax.all_to_all(partial, "bin", 0, 0, tiled=True)
     corr, tile_grad = backward(
         inverse_area, filter_taps, partial, padded(target_corr), padded(pair_weight),
         left, right, wa, g_above, g, g_below,

time: 91.5 us -> 98.6 us (1.078)
  the two profiles are of different devices: /device:TPU:16 before, /device:TPU:32 now
where the time goes in v7:
time: 98.6 us; the launch traced here: 97.8 us
  starting transfers between devices  45.4 us (46%)
  Pallas kernels  25.3 us (26%)
  waiting for transfers between devices  23.1 us (23%)
  local copies, waits for them, and re-layouts  3.16 us (3%)
    ppermute x1, starting transfers between devices, per_device(): above2 = lax.ppermute(own, 'sky', [(i, i + 2) for i in range(sky - 2)])  10.4 us
    all_to_all x1, starting transfers between devices, per_device(): own = lax.all_to_all(windows, 'bin', 0, 0, tiled=True)  9.73 us
    all_to_all x1, waiting for transfers between devices, per_device(): back = lax.all_to_all(tile_grad, 'bin', 0, 0, tiled=True)  9.61 us
    pallas_call x1, Pallas kernels, backward(): pl.pallas_call(lambda *refs: backward_kernel(inverse_area, *refs), in_spe...  8.83 us
    all_to_all x1, starting transfers between devices, per_device(): back = lax.all_to_all(tile_grad, 'bin', 0, 0, tiled=True)  8.01 us
    all_to_all x1, starting transfers between devices, per_device(): partial = lax.all_to_all(partial, 'sky', 0, 0, tiled=True)  7.55 us
    pallas_call x2, Pallas kernels, beside(): pl.pallas_call(beside_kernel, in_specs=[VMEM] * 4 + [HBM] * 2, out_specs=...  6.81 us
    pallas_call x1, Pallas kernels, forward(): pl.pallas_call(forward_kernel, out_shape=(struct(MAPS, BF16), struct((cop...  5.22 us
  transfers between devices with their start and end apart: 8, of which 5 were waited for; matrix products, arithmetic and copies ran while one was open for 2% of the time, Pallas kernels for 10%

profile of v7, /device:TPU:32, one launch (start us, length us, event | category | flops | bytes accessed | tf_op | source)
XLA Modules:
  0.0 97.8 jit_solution(13550370126330564765)
XLA Ops:
  0.6 1.7 %windows.1 = bf16[128,640]{1,0:T(8,128)(2,1)} custom-call(bf16[8,8192]{1,0:T(8,128)(2,1)} %bitcast.24, s32[1,64]{1,0:T(1,128)} %mask_ref.1), custom_call_target="tpu_custom_call" | custom-call | tf_op jit(solution)/shard_map/windows/pallas_call | solution.py:432
  2.3 0.0 copy-start.3
  2.3 9.7 %all-to-all-start = ((bf16[16,8,640]{2,1,0:T(8,128)(2,1)}), bf16[16,8,640]{2,1,0:T(8,128)(2,1)S(1)}, u32[]{:S(2)}, u32[]{:S(2)}) async-start(bf16[16,8,640]{2,1,0:T(8,128)(2,1)} %bitcast.23), calls=%async_computation | async-start | bytes 327680 | tf_op jit(solution)/shard_map/all_to_all | solution.py:438
  12.1 0.0 copy-done.3
  12.1 0.1 copy.12
  12.2 0.0 copy-start
  12.2 0.7 copy-done
  12.9 2.8 %matrices.1 = (f32[2,5,8,384]{3,2,1,0:T(8,128)S(1)}, bf16[5,256,256]{2,1,0:T(8,128)(2,1)S(1)}, bf16[5,256,256]{2,1,0:T(8,128)(2,1)S(1)}, bf16[144,320]{1,0:T(8,1...) custom-call(f32[5,17]{1,0:T(8,128)S(1)} %copy-done, ...), custom_call_target="tpu_custom_call" | custom-call | flops 20000000 | bytes 4000000 | tf_op jit(solution)/shard_map/matrices/pallas_call | solution.py:344
  15.6 5.0 %all-to-all-done = bf16[16,8,640]{2,1,0:T(8,128)(2,1)S(1)} async-done(((bf16[16,8,640]{2,1,0:T(8,128)(2,1)}), bf16[16,8,640]{2,1,0:T(8,128)(2,1)S(1)}, u32[]{:S(2)}, u32[]{:S(2)}) %all-to-all-start) | async-done | bytes 163872 | tf_op jit(solution)/shard_map/all_to_all | solution.py:438
  20.6 1.3 %collective-permute-start.1 = (bf16[128,640]{1,0:T(8,128)(2,1)S(1)}, bf16[128,640]{1,0:T(8,128)(2,1)S(1)}, u32[]{:S(2)}, u32[]{:S(2)}) collective-permute-start(bf16[128,640]{1,0:T(8,128)(2,1)S(1)} %bitcast.15), channel_id=1, source_target_pairs={{1,0},{2,1},{3,2},{4,3},{5,4},{6,5},{7,6},{8,7},{9,8},{10,9},{11,1... | collective-permute-start | bytes 491528 | tf_op jit(solution)/shard_map/ppermute | solution.py:442
  21.9 3.0 %collective-permute-start = (bf16[128,640]{1,0:T(8,128)(2,1)S(1)}, bf16[128,640]{1,0:T(8,128)(2,1)S(1)}, u32[]{:S(2)}, u32[]{:S(2)}) collective-permute-start(bf16[128,640]{1,0:T(8,128)(2,1)S(1)} %bitcast.16), channel_id=1, source_target_pairs={{0,1},{1,2},{2,3},{3,4},{4,5},{5,6},{6,7},{7,8},{8,9},{9,10},{10,1... | collective-permute-start | bytes 491528 | tf_op jit(solution)/shard_map/ppermute | solution.py:441
  24.9 0.0 collective-permute-done.1.down_ref.second_ref
  25.0 1.0 %collective-permute-done.up_ref.second_ref = bf16[128,640]{1,0:T(8,128)(2,1)S(1)} collective-permute-done((bf16[128,640]{1,0:T(8,128)(2,1)S(1)}, bf16[128,640]{1,0:T(8,128)(2,1)S(1)}, u32[]{:S(2)}, u32[]{:S(2)}) %collective-permute-start) | collective-permute-done | bytes 163872 | tf_op jit(solution)/shard_map/ppermute | solution.py:441
  25.9 5.2 %forward.1 = (bf16[656,640]{1,0:T(8,128)(2,1)S(1)}, f32[16,8,384]{2,1,0:T(8,128)}) custom-call(bf16[128,640]{1,0:T(8,128)(2,1)S(1)} %collective-permute-done.up_ref.second_ref, bf16[128,640]{1,0:T(8,128)(2,1)S(1)} %bitcast.17, bf16[128,640]{1,0:T(8,128)(2,1)S(1)} %collective-permute-done.1.down_ref.second_ref, ...), custom_call_target="tpu_custom_call" | custom-call | tf_op jit(solution)/shard_map/forward/pallas_call | solution.py:374
  31.2 0.0 copy-start.1
  31.2 4.1 %all-to-all-start.1 = ((f32[16,8,384]{2,1,0:T(8,128)}), f32[16,8,384]{2,1,0:T(8,128)S(1)}, u32[]{:S(2)}, u32[]{:S(2)}) async-start(f32[16,8,384]{2,1,0:T(8,128)} %get-tuple-element.37), calls=%async_computation.1 | async-start | bytes 393216 | tf_op jit(solution)/shard_map/all_to_all | solution.py:448
  35.3 0.0 copy-start.2
  35.3 1.3 %collective-permute-start.3 = (bf16[128,640]{1,0:T(8,128)(2,1)S(1)}, bf16[128,640]{1,0:T(8,128)(2,1)S(1)}, u32[]{:S(2)}, u32[]{:S(2)}) collective-permute-start(bf16[128,640]{1,0:T(8,128)(2,1)S(1)} %bitcast.18), channel_id=1, source_target_pairs={{2,0},{3,1},{4,2},{5,3},{6,4},{7,5},{8,6},{9,7},{10,8},{11,9},{12,... | collective-permute-start | bytes 491528 | tf_op jit(solution)/shard_map/ppermute | solution.py:444
  36.6 0.0 copy-done.1
  36.6 0.0 copy-done.2
  36.6 0.1 copy.14
  36.7 0.1 copy.13
  36.9 10.4 %collective-permute-start.2 = (bf16[128,640]{1,0:T(8,128)(2,1)S(1)}, bf16[128,640]{1,0:T(8,128)(2,1)S(1)}, u32[]{:S(2)}, u32[]{:S(2)}) collective-permute-start(bf16[128,640]{1,0:T(8,128)(2,1)S(1)} %bitcast.19), channel_id=1, source_target_pairs={{0,2},{1,3},{2,4},{3,5},{4,6},{5,7},{6,8},{7,9},{8,10},{9,11},{10,... | collective-permute-start | bytes 491528 | tf_op jit(solution)/shard_map/ppermute | solution.py:443
  47.3 2.4 %collective-permute-done.3.third_ref = bf16[128,640]{1,0:T(8,128)(2,1)S(1)} collective-permute-done((bf16[128,640]{1,0:T(8,128)(2,1)S(1)}, bf16[128,640]{1,0:T(8,128)(2,1)S(1)}, u32[]{:S(2)}, u32[]{:S(2)}) %collective-permute-start.3) | collective-permute-done | bytes 163872 | tf_op jit(solution)/shard_map/ppermute | solution.py:444
  49.6 3.4 %beside.3.refs_8_ = bf16[656,640]{1,0:T(8,128)(2,1)} custom-call(bf16[128,640]{1,0:T(8,128)(2,1)S(1)} %bitcast.20, bf16[128,640]{1,0:T(8,128)(2,1)S(1)} %collective-permute-done.1.down_ref.second_ref, bf16[128,640]{1,0:T(8,128)(2,1)S(1)} %collective-permute-done.3.third_ref, f32[2,5,8,384]{3,2,1,0:T(8,128)S(1)} %get-tuple-element.32.row_ref, ...), custom_call_target="tpu_custom_call" | custom-call | flops 2000000000 | bytes 8000000 | tf_op jit(solution)/shard_map/beside/pallas_call | solution.py:384
  53.1 0.0 all-to-all-done.1
  53.1 0.7 broadcast_in_dim.2
  53.8 7.5 %all-to-all-start.2 = ((f32[16,8,384]{2,1,0:T(8,128)}), f32[16,8,384]{2,1,0:T(8,128)S(1)}, u32[]{:S(2)}, u32[]{:S(2)}) async-start(f32[16,8,384]{2,1,0:T(8,128)} %broadcast_in_dim.2), calls=%async_computation.2 | async-start | bytes 393216 | tf_op jit(solution)/shard_map/all_to_all | solution.py:450
  61.4 0.0 collective-permute-done.2.first_ref
  61.4 3.4 %beside.2.refs_7_ = bf16[656,640]{1,0:T(8,128)(2,1)} custom-call(bf16[128,640]{1,0:T(8,128)(2,1)S(1)} %collective-permute-done.2.first_ref, bf16[128,640]{1,0:T(8,128)(2,1)S(1)} %collective-permute-done.up_ref.second_ref, bf16[128,640]{1,0:T(8,128)(2,1)S(1)} %bitcast.21, f32[2,5,8,384]{3,2,1,0:T(8,128)S(1)} %get-tuple-element.32.row_ref, ...), custom_call_target="tpu_custom_call" | custom-call | flops 2000000000 | bytes 8000000 | tf_op jit(solution)/shard_map/beside/pallas_call | solution.py:384
  64.8 5.2 %all-to-all-done.2.refs_1_ = f32[16,8,384]{2,1,0:T(8,128)S(1)} async-done(((f32[16,8,384]{2,1,0:T(8,128)}), f32[16,8,384]{2,1,0:T(8,128)S(1)}, u32[]{:S(2)}, u32[]{:S(2)}) %all-to-all-start.2) | async-done | bytes 196640 | tf_op jit(solution)/shard_map/all_to_all | solution.py:450
  69.9 8.8 %backward.1 = (f32[144,20]{1,0:T(8,128)S(1)}, f32[512,128]{1,0:T(8,128)}) custom-call(f32[5,17]{1,0:T(8,128)S(1)} %copy-done, f32[16,8,384]{2,1,0:T(8,128)S(1)} %all-to-all-done.2.refs_1_, f32[144,20]{1,0:T(8,128)S(1)} %pad.12.refs_2_, f32[144,20]{1,0:T(8,128)S(1)} %pad.13.refs_3_, bf16[144,320]{1,0:T(8,128)(2,1)S(1)} %get-tuple-element.35.left_ref.refs_4_, ...), custom_call_target="tpu_custom_call" | custom-call | tf_op jit(solution)/shard_map/backward/pallas_call | solution.py:403
  78.8 8.0 %all-to-all-start.3 = ((f32[16,32,128]{2,1,0:T(8,128)}), f32[16,32,128]{2,1,0:T(8,128)S(1)}, u32[]{:S(2)}, u32[]{:S(2)}) async-start(f32[16,32,128]{2,1,0:T(8,128)} %bitcast.3), calls=%async_computation.3 | async-start | bytes 524288 | tf_op jit(solution)/shard_map/all_to_all | solution.py:455
  86.8 0.1 copy.15
  86.9 0.6 reshape.27
  87.5 9.6 %all-to-all-done.3 = f32[16,32,128]{2,1,0:T(8,128)S(1)} async-done(((f32[16,32,128]{2,1,0:T(8,128)}), f32[16,32,128]{2,1,0:T(8,128)S(1)}, u32[]{:S(2)}, u32[]{:S(2)}) %all-to-all-start.3) | async-done | bytes 262176 | tf_op jit(solution)/shard_map/all_to_all | solution.py:455
  97.1 0.7 copy.17
  (7 shorter events, 0.1 us)
Async XLA Ops:
  2.3 9.7 %copy-start.3 = (s32[136,2]{0,1:T(2,128)S(1)}, s32[136,2]{0,1:T(2,128)}, u32[]{:S(2)}) copy-start(s32[136,2]{0,1:T(2,128)} %param.9) | copy-start | bytes 3268
  2.3 18.3 %all-to-all-start = ((bf16[16,8,640]{2,1,0:T(8,128)(2,1)}), bf16[16,8,640]{2,1,0:T(8,128)(2,1)S(1)}, u32[]{:S(2)}, u32[]{:S(2)}) async-start(bf16[16,8,640]{2,1,0:T(8,128)(2,1)} %bitcast.23), calls=%async_computation | async-start | bytes 327680 | tf_op jit(solution)/shard_map/all_to_all | solution.py:438
  12.2 0.7 copy-start
  20.6 4.3 %collective-permute-start.1 = (bf16[128,640]{1,0:T(8,128)(2,1)S(1)}, bf16[128,640]{1,0:T(8,128)(2,1)S(1)}, u32[]{:S(2)}, u32[]{:S(2)}) collective-permute-start(bf16[128,640]{1,0:T(8,128)(2,1)S(1)} %bitcast.15), channel_id=1, source_target_pairs={{1,0},{2,1},{3,2},{4,3},{5,4},{6,5},{7,6},{8,7},{9,8},{10,9},{11,1... | collective-permute-start | bytes 491528 | tf_op jit(solution)/shard_map/ppermute | solution.py:442
  21.9 4.0 %collective-permute-start = (bf16[128,640]{1,0:T(8,128)(2,1)S(1)}, bf16[128,640]{1,0:T(8,128)(2,1)S(1)}, u32[]{:S(2)}, u32[]{:S(2)}) collective-permute-start(bf16[128,640]{1,0:T(8,128)(2,1)S(1)} %bitcast.16), channel_id=1, source_target_pairs={{0,1},{1,2},{2,3},{3,4},{4,5},{5,6},{6,7},{7,8},{8,9},{9,10},{10,1... | collective-permute-start | bytes 491528 | tf_op jit(solution)/shard_map/ppermute | solution.py:441
  31.2 5.4 %copy-start.1 = (f32[136,5,4]{0,2,1:T(4,128)S(1)}, f32[136,5,4]{0,2,1:T(4,128)}, u32[]{:S(2)}) copy-start(f32[136,5,4]{0,2,1:T(4,128)} %param.10) | copy-start | bytes 32644
  31.2 21.9 %all-to-all-start.1 = ((f32[16,8,384]{2,1,0:T(8,128)}), f32[16,8,384]{2,1,0:T(8,128)S(1)}, u32[]{:S(2)}, u32[]{:S(2)}) async-start(f32[16,8,384]{2,1,0:T(8,128)} %get-tuple-element.37), calls=%async_computation.1 | async-start | bytes 393216 | tf_op jit(solution)/shard_map/all_to_all | solution.py:448
  35.3 1.3 %copy-start.2 = (f32[136,5,4]{0,2,1:T(4,128)S(1)}, f32[136,5,4]{0,2,1:T(4,128)}, u32[]{:S(2)}) copy-start(f32[136,5,4]{0,2,1:T(4,128)} %param.11) | copy-start | bytes 32644
  35.3 14.4 %collective-permute-start.3 = (bf16[128,640]{1,0:T(8,128)(2,1)S(1)}, bf16[128,640]{1,0:T(8,128)(2,1)S(1)}, u32[]{:S(2)}, u32[]{:S(2)}) collective-permute-start(bf16[128,640]{1,0:T(8,128)(2,1)S(1)} %bitcast.18), channel_id=1, source_target_pairs={{2,0},{3,1},{4,2},{5,3},{6,4},{7,5},{8,6},{9,7},{10,8},{11,9},{12,... | collective-permute-start | bytes 491528 | tf_op jit(solution)/shard_map/ppermute | solution.py:444
  36.9 24.5 %collective-permute-start.2 = (bf16[128,640]{1,0:T(8,128)(2,1)S(1)}, bf16[128,640]{1,0:T(8,128)(2,1)S(1)}, u32[]{:S(2)}, u32[]{:S(2)}) collective-permute-start(bf16[128,640]{1,0:T(8,128)(2,1)S(1)} %bitcast.19), channel_id=1, source_target_pairs={{0,2},{1,3},{2,4},{3,5},{4,6},{5,7},{6,8},{7,9},{8,10},{9,11},{10,... | collective-permute-start | bytes 491528 | tf_op jit(solution)/shard_map/ppermute | solution.py:443
  53.8 16.1 %all-to-all-start.2 = ((f32[16,8,384]{2,1,0:T(8,128)}), f32[16,8,384]{2,1,0:T(8,128)S(1)}, u32[]{:S(2)}, u32[]{:S(2)}) async-start(f32[16,8,384]{2,1,0:T(8,128)} %broadcast_in_dim.2), calls=%async_computation.2 | async-start | bytes 393216 | tf_op jit(solution)/shard_map/all_to_all | solution.py:450
  78.8 18.3 %all-to-all-start.3 = ((f32[16,32,128]{2,1,0:T(8,128)}), f32[16,32,128]{2,1,0:T(8,128)S(1)}, u32[]{:S(2)}, u32[]{:S(2)}) async-start(f32[16,32,128]{2,1,0:T(8,128)} %bitcast.3), calls=%async_computation.3 | async-start | bytes 524288 | tf_op jit(solution)/shard_map/all_to_all | solution.py:455

commit v8 on v6

--- a/solution.py
+++ b/solution.py
@@ -299,13 +299,17 @@
                 for i in range(2):
                     v = d[2 * BINS * i : 2 * BINS * (i + 1)]
                     grad_ref[s % 2, ROWS * k + x + i] = jnp.where(mask, v[:BINS] + v[BINS:], 0.0)
-        rows = []
-        for x in range(ROWS):
-            acc = taps_ref[s, TAPS - 1] * grad_ref[s % 2, x]
-            for a in range(1, TAPS):
-                acc = acc + taps_ref[s, TAPS - 1 - a] * grad_ref[s % 2, x + a]
-            rows.append(acc)
-        rows = jnp.concatenate(rows, axis=0)
+        columns = []
+        for c in range(WIN // LANE):
+            sums = [None] * ROWS
+            for k in range(3 * ROWS):
+                v = grad_ref[s % 2, k, :, LANE * c : LANE * (c + 1)]
+                for x in range(ROWS):
+                    if 0 <= k - x < TAPS:
+                        term = taps_ref[s, TAPS - 1 - (k - x)] * v
+                        sums[x] = term if sums[x] is None else sums[x] + term
+            columns.append(jnp.concatenate(sums, axis=0))
+        rows = jnp.concatenate(columns, axis=1)
         if s == 0:
             copies[2].wait()
         tiles = banded([rows[:, LANE * c : LANE * (c + 2)] for c in range(OWN // LANE)], wa_ref[s])

time: 91.5 us -> 91.5 us (level)
  no operation moved by 1% of the time
where the time goes in v8:
time: 91.5 us; the launch traced here: 90.8 us
  starting transfers between devices  39.5 us (43%)
  Pallas kernels  25.3 us (28%)
  waiting for transfers between devices  21.9 us (24%)
  local copies, waits for them, and re-layouts  3.16 us (3%)
    all_to_all x1, starting transfers between devices, per_device(): own = lax.all_to_all(windows, 'bin', 0, 0, tiled=True)  9.42 us
    all_to_all x1, waiting for transfers between devices, per_device(): back = lax.all_to_all(tile_grad, 'bin', 0, 0, tiled=True)  8.85 us
    pallas_call x1, Pallas kernels, backward(): pl.pallas_call(lambda *refs: backward_kernel(inverse_area, *refs), in_spe...  8.83 us
    all_to_all x1, starting transfers between devices, per_device(): partial = lax.all_to_all(partial, 'sky', 0, 0, tiled=True)  7.41 us
    pallas_call x2, Pallas kernels, beside(): pl.pallas_call(beside_kernel, in_specs=[VMEM] * 4 + [HBM] * 2, out_specs=...  6.82 us
    ppermute x1, starting transfers between devices, per_device(): above2 = lax.ppermute(own, 'sky', [(i, i + 2) for i in range(sky - 2)])  6.23 us
    all_to_all x1, starting transfers between devices, per_device(): back = lax.all_to_all(tile_grad, 'bin', 0, 0, tiled=True)  6.06 us
    ppermute x1, waiting for transfers between devices, per_device(): above = lax.ppermute(own, 'sky', down_perm)  5.33 us
  transfers between devices with their start and end apart: 8, of which 5 were waited for; matrix products, arithmetic and copies ran while one was open for 2% of the time, Pallas kernels for 11%

profile of v8, /device:TPU:16, one launch (start us, length us, event | category | flops | bytes accessed | tf_op | source)
XLA Modules:
  0.0 90.8 jit_solution(4642563013348109563)
XLA Ops:
  0.6 1.7 %windows.1 = bf16[128,640]{1,0:T(8,128)(2,1)} custom-call(bf16[8,8192]{1,0:T(8,128)(2,1)} %bitcast.24, s32[1,64]{1,0:T(1,128)} %mask_ref.1), custom_call_target="tpu_custom_call" | custom-call | tf_op jit(solution)/shard_map/windows/pallas_call | solution.py:436
  2.3 0.0 copy-start.3
  2.3 9.4 %all-to-all-start = ((bf16[16,8,640]{2,1,0:T(8,128)(2,1)}), bf16[16,8,640]{2,1,0:T(8,128)(2,1)S(1)}, u32[]{:S(2)}, u32[]{:S(2)}) async-start(bf16[16,8,640]{2,1,0:T(8,128)(2,1)} %bitcast.23), calls=%async_computation | async-start | bytes 327680 | tf_op jit(solution)/shard_map/all_to_all | solution.py:442
  11.8 0.0 copy-done.3
  11.8 0.1 copy.12
  11.9 0.0 copy-start
  11.9 0.7 copy-done
  12.6 2.8 %matrices.1 = (f32[2,5,8,384]{3,2,1,0:T(8,128)S(1)}, bf16[5,256,256]{2,1,0:T(8,128)(2,1)S(1)}, bf16[5,256,256]{2,1,0:T(8,128)(2,1)S(1)}, bf16[144,320]{1,0:T(8,1...) custom-call(f32[5,17]{1,0:T(8,128)S(1)} %copy-done, ...), custom_call_target="tpu_custom_call" | custom-call | flops 20000000 | bytes 4000000 | tf_op jit(solution)/shard_map/matrices/pallas_call | solution.py:348
  15.3 5.3 %all-to-all-done = bf16[16,8,640]{2,1,0:T(8,128)(2,1)S(1)} async-done(((bf16[16,8,640]{2,1,0:T(8,128)(2,1)}), bf16[16,8,640]{2,1,0:T(8,128)(2,1)S(1)}, u32[]{:S(2)}, u32[]{:S(2)}) %all-to-all-start) | async-done | bytes 163872 | tf_op jit(solution)/shard_map/all_to_all | solution.py:442
  20.6 1.9 %collective-permute-start.1 = (bf16[128,640]{1,0:T(8,128)(2,1)S(1)}, bf16[128,640]{1,0:T(8,128)(2,1)S(1)}, u32[]{:S(2)}, u32[]{:S(2)}) collective-permute-start(bf16[128,640]{1,0:T(8,128)(2,1)S(1)} %bitcast.15), channel_id=1, source_target_pairs={{1,0},{2,1},{3,2},{4,3},{5,4},{6,5},{7,6},{8,7},{9,8},{10,9},{11,1... | collective-permute-start | bytes 491528 | tf_op jit(solution)/shard_map/ppermute | solution.py:446
  22.5 2.4 %collective-permute-start = (bf16[128,640]{1,0:T(8,128)(2,1)S(1)}, bf16[128,640]{1,0:T(8,128)(2,1)S(1)}, u32[]{:S(2)}, u32[]{:S(2)}) collective-permute-start(bf16[128,640]{1,0:T(8,128)(2,1)S(1)} %bitcast.16), channel_id=1, source_target_pairs={{0,1},{1,2},{2,3},{3,4},{4,5},{5,6},{6,7},{7,8},{8,9},{9,10},{10,1... | collective-permute-start | bytes 491528 | tf_op jit(solution)/shard_map/ppermute | solution.py:445
  24.9 0.4 collective-permute-done.1.down_ref.second_ref
  25.3 5.3 %collective-permute-done.up_ref.second_ref = bf16[128,640]{1,0:T(8,128)(2,1)S(1)} collective-permute-done((bf16[128,640]{1,0:T(8,128)(2,1)S(1)}, bf16[128,640]{1,0:T(8,128)(2,1)S(1)}, u32[]{:S(2)}, u32[]{:S(2)}) %collective-permute-start) | collective-permute-done | bytes 163872 | tf_op jit(solution)/shard_map/ppermute | solution.py:445
  30.7 5.2 %forward.1 = (bf16[656,640]{1,0:T(8,128)(2,1)S(1)}, f32[16,8,384]{2,1,0:T(8,128)}) custom-call(bf16[128,640]{1,0:T(8,128)(2,1)S(1)} %collective-permute-done.up_ref.second_ref, bf16[128,640]{1,0:T(8,128)(2,1)S(1)} %bitcast.17, bf16[128,640]{1,0:T(8,128)(2,1)S(1)} %collective-permute-done.1.down_ref.second_ref, ...), custom_call_target="tpu_custom_call" | custom-call | tf_op jit(solution)/shard_map/forward/pallas_call | solution.py:378
  35.9 0.0 copy-start.1
  35.9 7.4 %all-to-all-start.1 = ((f32[16,8,384]{2,1,0:T(8,128)}), f32[16,8,384]{2,1,0:T(8,128)S(1)}, u32[]{:S(2)}, u32[]{:S(2)}) async-start(f32[16,8,384]{2,1,0:T(8,128)} %get-tuple-element.37), calls=%async_computation.1 | async-start | bytes 393216 | tf_op jit(solution)/shard_map/all_to_all | solution.py:452
  43.3 0.0 copy-start.2
  43.3 2.0 %collective-permute-start.3 = (bf16[128,640]{1,0:T(8,128)(2,1)S(1)}, bf16[128,640]{1,0:T(8,128)(2,1)S(1)}, u32[]{:S(2)}, u32[]{:S(2)}) collective-permute-start(bf16[128,640]{1,0:T(8,128)(2,1)S(1)} %bitcast.18), channel_id=1, source_target_pairs={{2,0},{3,1},{4,2},{5,3},{6,4},{7,5},{8,6},{9,7},{10,8},{11,9},{12,... | collective-permute-start | bytes 491528 | tf_op jit(solution)/shard_map/ppermute | solution.py:448
  45.3 0.0 copy-done.1
  45.3 0.0 copy-done.2
  45.4 0.1 copy.14
  45.5 0.1 copy.13
  45.6 6.2 %collective-permute-start.2 = (bf16[128,640]{1,0:T(8,128)(2,1)S(1)}, bf16[128,640]{1,0:T(8,128)(2,1)S(1)}, u32[]{:S(2)}, u32[]{:S(2)}) collective-permute-start(bf16[128,640]{1,0:T(8,128)(2,1)S(1)} %bitcast.19), channel_id=1, source_target_pairs={{0,2},{1,3},{2,4},{3,5},{4,6},{5,7},{6,8},{7,9},{8,10},{9,11},{10,... | collective-permute-start | bytes 491528 | tf_op jit(solution)/shard_map/ppermute | solution.py:447
  51.9 0.0 all-to-all-done.1
  51.9 0.7 broadcast_in_dim.2
  52.6 4.0 %all-to-all-start.2 = ((f32[16,8,384]{2,1,0:T(8,128)}), f32[16,8,384]{2,1,0:T(8,128)S(1)}, u32[]{:S(2)}, u32[]{:S(2)}) async-start(f32[16,8,384]{2,1,0:T(8,128)} %broadcast_in_dim.2), calls=%async_computation.2 | async-start | bytes 393216 | tf_op jit(solution)/shard_map/all_to_all | solution.py:454
  56.6 0.0 collective-permute-done.3.third_ref
  56.7 3.4 %beside.3.refs_8_ = bf16[656,640]{1,0:T(8,128)(2,1)} custom-call(bf16[128,640]{1,0:T(8,128)(2,1)S(1)} %bitcast.20, bf16[128,640]{1,0:T(8,128)(2,1)S(1)} %collective-permute-done.1.down_ref.second_ref, bf16[128,640]{1,0:T(8,128)(2,1)S(1)} %collective-permute-done.3.third_ref, f32[2,5,8,384]{3,2,1,0:T(8,128)S(1)} %get-tuple-element.32.row_ref, ...), custom_call_target="tpu_custom_call" | custom-call | flops 2000000000 | bytes 8000000 | tf_op jit(solution)/shard_map/beside/pallas_call | solution.py:388
  60.1 0.0 collective-permute-done.2.first_ref
  60.1 3.4 %beside.2.refs_7_ = bf16[656,640]{1,0:T(8,128)(2,1)} custom-call(bf16[128,640]{1,0:T(8,128)(2,1)S(1)} %collective-permute-done.2.first_ref, bf16[128,640]{1,0:T(8,128)(2,1)S(1)} %collective-permute-done.up_ref.second_ref, bf16[128,640]{1,0:T(8,128)(2,1)S(1)} %bitcast.21, f32[2,5,8,384]{3,2,1,0:T(8,128)S(1)} %get-tuple-element.32.row_ref, ...), custom_call_target="tpu_custom_call" | custom-call | flops 2000000000 | bytes 8000000 | tf_op jit(solution)/shard_map/beside/pallas_call | solution.py:388
  63.5 2.1 %all-to-all-done.2.refs_1_ = f32[16,8,384]{2,1,0:T(8,128)S(1)} async-done(((f32[16,8,384]{2,1,0:T(8,128)}), f32[16,8,384]{2,1,0:T(8,128)S(1)}, u32[]{:S(2)}, u32[]{:S(2)}) %all-to-all-start.2) | async-done | bytes 196640 | tf_op jit(solution)/shard_map/all_to_all | solution.py:454
  65.6 8.8 %backward.1 = (f32[144,20]{1,0:T(8,128)S(1)}, f32[512,128]{1,0:T(8,128)}) custom-call(f32[5,17]{1,0:T(8,128)S(1)} %copy-done, f32[16,8,384]{2,1,0:T(8,128)S(1)} %all-to-all-done.2.refs_1_, f32[144,20]{1,0:T(8,128)S(1)} %pad.12.refs_2_, f32[144,20]{1,0:T(8,128)S(1)} %pad.13.refs_3_, bf16[144,320]{1,0:T(8,128)(2,1)S(1)} %get-tuple-element.35.left_ref.refs_4_, ...), custom_call_target="tpu_custom_call" | custom-call | tf_op jit(solution)/shard_map/backward/pallas_call | solution.py:407
  74.4 6.1 %all-to-all-start.3 = ((f32[16,32,128]{2,1,0:T(8,128)}), f32[16,32,128]{2,1,0:T(8,128)S(1)}, u32[]{:S(2)}, u32[]{:S(2)}) async-start(f32[16,32,128]{2,1,0:T(8,128)} %bitcast.3), calls=%async_computation.3 | async-start | bytes 524288 | tf_op jit(solution)/shard_map/all_to_all | solution.py:459
  80.5 0.1 copy.15
  80.6 0.6 reshape.27
  81.2 8.9 %all-to-all-done.3 = f32[16,32,128]{2,1,0:T(8,128)S(1)} async-done(((f32[16,32,128]{2,1,0:T(8,128)}), f32[16,32,128]{2,1,0:T(8,128)S(1)}, u32[]{:S(2)}, u32[]{:S(2)}) %all-to-all-start.3) | async-done | bytes 262176 | tf_op jit(solution)/shard_map/all_to_all | solution.py:459
  90.1 0.7 copy.17
  (7 shorter events, 0.1 us)
Async XLA Ops:
  2.3 9.4 %copy-start.3 = (s32[136,2]{0,1:T(2,128)S(1)}, s32[136,2]{0,1:T(2,128)}, u32[]{:S(2)}) copy-start(s32[136,2]{0,1:T(2,128)} %param.9) | copy-start | bytes 3268
  2.3 18.3 %all-to-all-start = ((bf16[16,8,640]{2,1,0:T(8,128)(2,1)}), bf16[16,8,640]{2,1,0:T(8,128)(2,1)S(1)}, u32[]{:S(2)}, u32[]{:S(2)}) async-start(bf16[16,8,640]{2,1,0:T(8,128)(2,1)} %bitcast.23), calls=%async_computation | async-start | bytes 327680 | tf_op jit(solution)/shard_map/all_to_all | solution.py:442
  11.9 0.7 copy-start
  20.6 4.7 %collective-permute-start.1 = (bf16[128,640]{1,0:T(8,128)(2,1)S(1)}, bf16[128,640]{1,0:T(8,128)(2,1)S(1)}, u32[]{:S(2)}, u32[]{:S(2)}) collective-permute-start(bf16[128,640]{1,0:T(8,128)(2,1)S(1)} %bitcast.15), channel_id=1, source_target_pairs={{1,0},{2,1},{3,2},{4,3},{5,4},{6,5},{7,6},{8,7},{9,8},{10,9},{11,1... | collective-permute-start | bytes 491528 | tf_op jit(solution)/shard_map/ppermute | solution.py:446
  22.5 8.1 %collective-permute-start = (bf16[128,640]{1,0:T(8,128)(2,1)S(1)}, bf16[128,640]{1,0:T(8,128)(2,1)S(1)}, u32[]{:S(2)}, u32[]{:S(2)}) collective-permute-start(bf16[128,640]{1,0:T(8,128)(2,1)S(1)} %bitcast.16), channel_id=1, source_target_pairs={{0,1},{1,2},{2,3},{3,4},{4,5},{5,6},{6,7},{7,8},{8,9},{9,10},{10,1... | collective-permute-start | bytes 491528 | tf_op jit(solution)/shard_map/ppermute | solution.py:445
  35.9 9.4 %copy-start.1 = (f32[136,5,4]{0,2,1:T(4,128)S(1)}, f32[136,5,4]{0,2,1:T(4,128)}, u32[]{:S(2)}) copy-start(f32[136,5,4]{0,2,1:T(4,128)} %param.10) | copy-start | bytes 32644
  35.9 16.0 %all-to-all-start.1 = ((f32[16,8,384]{2,1,0:T(8,128)}), f32[16,8,384]{2,1,0:T(8,128)S(1)}, u32[]{:S(2)}, u32[]{:S(2)}) async-start(f32[16,8,384]{2,1,0:T(8,128)} %get-tuple-element.37), calls=%async_computation.1 | async-start | bytes 393216 | tf_op jit(solution)/shard_map/all_to_all | solution.py:452
  43.3 2.1 %copy-start.2 = (f32[136,5,4]{0,2,1:T(4,128)S(1)}, f32[136,5,4]{0,2,1:T(4,128)}, u32[]{:S(2)}) copy-start(f32[136,5,4]{0,2,1:T(4,128)} %param.11) | copy-start | bytes 32644
  43.3 13.4 %collective-permute-start.3 = (bf16[128,640]{1,0:T(8,128)(2,1)S(1)}, bf16[128,640]{1,0:T(8,128)(2,1)S(1)}, u32[]{:S(2)}, u32[]{:S(2)}) collective-permute-start(bf16[128,640]{1,0:T(8,128)(2,1)S(1)} %bitcast.18), channel_id=1, source_target_pairs={{2,0},{3,1},{4,2},{5,3},{6,4},{7,5},{8,6},{9,7},{10,8},{11,9},{12,... | collective-permute-start | bytes 491528 | tf_op jit(solution)/shard_map/ppermute | solution.py:448
  45.6 14.5 %collective-permute-start.2 = (bf16[128,640]{1,0:T(8,128)(2,1)S(1)}, bf16[128,640]{1,0:T(8,128)(2,1)S(1)}, u32[]{:S(2)}, u32[]{:S(2)}) collective-permute-start(bf16[128,640]{1,0:T(8,128)(2,1)S(1)} %bitcast.19), channel_id=1, source_target_pairs={{0,2},{1,3},{2,4},{3,5},{4,6},{5,7},{6,8},{7,9},{8,10},{9,11},{10,... | collective-permute-start | bytes 491528 | tf_op jit(solution)/shard_map/ppermute | solution.py:447
  52.6 13.0 %all-to-all-start.2 = ((f32[16,8,384]{2,1,0:T(8,128)}), f32[16,8,384]{2,1,0:T(8,128)S(1)}, u32[]{:S(2)}, u32[]{:S(2)}) async-start(f32[16,8,384]{2,1,0:T(8,128)} %broadcast_in_dim.2), calls=%async_computation.2 | async-start | bytes 393216 | tf_op jit(solution)/shard_map/all_to_all | solution.py:454
  74.4 15.7 %all-to-all-start.3 = ((f32[16,32,128]{2,1,0:T(8,128)}), f32[16,32,128]{2,1,0:T(8,128)S(1)}, u32[]{:S(2)}, u32[]{:S(2)}) async-start(f32[16,32,128]{2,1,0:T(8,128)} %bitcast.3), calls=%async_computation.3 | async-start | bytes 524288 | tf_op jit(solution)/shard_map/all_to_all | solution.py:459
